TPU v7x, 256 devices: a whole 4x4x8 slice. The times are simulated.
256 devices in a mesh: tm: 4 (over z_hi), height: 16 (over y, z_lo, core), tensor: 4 (over x).
Axes of the slice: x: 4, y: 4, z: 8 (z_hi: 4, z_lo: 2; z = z_hi * 2 + z_lo), core: 2. Of those that a mesh axis runs over, the one named last changes fastest.
Arguments:
- tokens: bfloat16 [8, 64, 64, 1024], P('tm', 'height', None, 'tensor'), may hold values from -40 to 40
- cotangent: bfloat16 [8, 64, 64, 1024], P('tm', 'height', None, 'tensor'), may hold values from -6 to 6
- w_qkv: bfloat16 [1024, 3, 1024], P(None, None, 'tensor'), may hold values from -0.125 to 0.125
- w_out: bfloat16 [1024, 1024], P('tensor'), may hold values from -0.1875 to 0.1875
Outputs:
- mixed: bfloat16 [8, 64, 64, 1024], P('tm', 'height', None, 'tensor')
- in_grad: bfloat16 [8, 64, 64, 1024], P('tm', 'height', None, 'tensor')
All inputs are finite; a program needn't handle non-finite values.
Results may differ from a plain program's by a relative error of at most 0.011.
Values may be sent and summed in bfloat16 or wider, within the bound.
No kernel may reach another device: no remote copies, remote signals or barrier semaphores. Data moves between devices by JAX's collectives and lax.ppermute only.
A program may use at most 128 MiB of HBM per device.

v0:
```python
import math

import jax
import jax.numpy as jnp
from jax import lax
from jax.sharding import PartitionSpec as P

HEAD_SIZE = 64


NEG_FILL = -1e30


def with_halo(array, sides, width):
    for axis, dim in sides:
        size, length = (lax.axis_size(axis), array.shape[dim])
        up = [(i, (i + 1) % size) for i in range(size - 1)]
        down = [(j, i) for i, j in up]
        last = lax.slice_in_dim(array, length - width, length, axis=dim)
        initial = lax.slice_in_dim(array, 0, width, axis=dim)
        before = lax.ppermute(last, axis, up)
        after = lax.ppermute(initial, axis, down)
        array = jnp.concatenate([before, array, after], axis=dim)
    return array


def flat_coords(outer_len, middle_len, inner_len):
    shape = (outer_len, middle_len, inner_len)
    outer = jnp.broadcast_to(jnp.arange(outer_len, dtype=jnp.int32)[:, None, None], shape).reshape(
        -1
    )
    middle = jnp.broadcast_to(
        jnp.arange(middle_len, dtype=jnp.int32)[None, :, None], shape
    ).reshape(-1)
    inner = jnp.broadcast_to(jnp.arange(inner_len, dtype=jnp.int32)[None, None, :], shape).reshape(
        -1
    )
    return (outer, middle, inner)


def shards(tokens, cotangent, w_qkv, w_out):
    frames, rows, columns, local_width = tokens.shape
    width = w_qkv.shape[0]
    count = frames * rows * columns
    head_width = HEAD_SIZE
    heads_here = local_width // head_width
    scale = 1.0 / math.sqrt(head_width)
    span_frames = 2
    span_columns = 64
    key_frames = span_frames + 2
    key_rows = rows + 6
    key_columns = span_columns + 6
    full_in, full_slope = (
        lax.all_gather(tokens, "tensor", axis=3, tiled=True),
        lax.all_gather(cotangent, "tensor", axis=3, tiled=True),
    )
    flat_in = w_qkv.reshape(width, 3 * local_width)
    proj = jnp.dot(
        full_in.reshape(count, width), flat_in, preferred_element_type=jnp.float32
    ).astype(jnp.bfloat16)
    query = proj[:, :local_width].reshape(frames, rows, columns, local_width)
    keyval = proj[:, local_width:].reshape(frames, rows, columns, 2 * local_width)
    back = jnp.dot(full_slope.reshape(count, width), w_out.T, preferred_element_type=jnp.float32)
    back = back.astype(jnp.bfloat16).reshape(frames, rows, columns, local_width)
    beside_all = with_halo(keyval, (("tm", 0),), 1)
    beside_all = with_halo(beside_all, (("height", 1),), 3)
    key_lane = 0
    beside_all = jnp.pad(beside_all, ((0, 0), (0, 0), (3, 3), (0, 0)))
    frame_place = lax.axis_index("tm") * frames + jnp.arange(frames + 2, dtype=jnp.int32) - 1
    frame_valid = (frame_place >= 0) & (frame_place < frames * lax.axis_size("tm"))
    row_place = lax.axis_index("height") * rows + jnp.arange(key_rows, dtype=jnp.int32) - 3
    row_valid = (row_place >= 0) & (row_place < rows * lax.axis_size("height"))
    column_place = jnp.arange(columns + 6, dtype=jnp.int32) - 3
    column_valid = (column_place >= 0) & (column_place < columns)
    query_frame, query_row, query_column = flat_coords(span_frames, rows, span_columns)
    key_frame, key_row, key_column = flat_coords(key_frames, key_rows, key_columns)
    nearby = jnp.abs(key_frame[None, :] - query_frame[:, None] - 1) <= 1
    nearby = nearby & (jnp.abs(key_row[None, :] - query_row[:, None] - 3) <= 3)
    nearby = nearby & (jnp.abs(key_column[None, :] - query_column[:, None] - 3) <= 3)
    tiles_across = columns // span_columns
    tile_count = frames // span_frames * tiles_across * heads_here
    query_box = (span_frames, rows, span_columns, head_width)
    key_box = (key_frames, key_rows, key_columns, head_width)
    contract_last = (((1,), (1,)), ((), ()))
    contract_first = (((0,), (0,)), ((), ()))

    def wide_valid():
        fine = frame_valid[:, None, None]
        fine = fine & row_valid[None, :, None]
        fine = fine & column_valid[None, None, :]
        return fine.reshape(-1)

    def locate(step):
        head = step % heads_here
        place = step // heads_here
        frame_start = place // tiles_across * span_frames
        column_start = place % tiles_across * span_columns
        return (head, frame_start, column_start, head * head_width)

    def visit(step, carry):
        out_buf, query_grad, kv_grad = carry
        head, frame_start, column_start, lane = locate(step)
        query_start = (frame_start, 0, column_start, lane)
        query_tile = lax.dynamic_slice(query, query_start, query_box).reshape(-1, head_width)
        back_tile = lax.dynamic_slice(back, query_start, query_box).reshape(-1, head_width)
        key_tile = lax.dynamic_slice(
            beside_all, (frame_start, 0, column_start, key_lane + lane), key_box
        ).reshape(-1, head_width)
        value_tile = lax.dynamic_slice(
            beside_all, (frame_start, 0, column_start, local_width + lane), key_box
        ).reshape(-1, head_width)
        allowed = nearby & wide_valid()[None, :]
        raw = (
            lax.dot_general(query_tile, key_tile, contract_last, preferred_element_type=jnp.float32)
            * scale
        )
        raw = jnp.where(allowed, raw, NEG_FILL)
        top = jnp.max(raw, axis=1, keepdims=True)
        expo = jnp.exp(raw - top)
        total = jnp.sum(expo, axis=1, keepdims=True)
        probs = expo / total
        probs_low = probs.astype(jnp.bfloat16)
        attended = jnp.dot(probs_low, value_tile, preferred_element_type=jnp.float32).astype(
            jnp.bfloat16
        )
        slopes = lax.dot_general(
            back_tile, value_tile, contract_last, preferred_element_type=jnp.float32
        )
        centre = jnp.sum(probs * slopes, axis=1, keepdims=True)
        dscore = (probs * (slopes - centre) * scale).astype(jnp.bfloat16)
        dquery = jnp.dot(dscore, key_tile, preferred_element_type=jnp.float32).astype(jnp.bfloat16)
        out_buf = lax.dynamic_update_slice(out_buf, attended.reshape(query_box), query_start)
        query_grad = lax.dynamic_update_slice(query_grad, dquery.reshape(query_box), query_start)
        dkeys = lax.dot_general(
            dscore, query_tile, contract_first, preferred_element_type=jnp.float32
        )
        dvalues = lax.dot_general(
            probs_low, back_tile, contract_first, preferred_element_type=jnp.float32
        )
        key_start = (frame_start, 0, column_start, lane)
        value_start = (frame_start, 0, column_start, lane + local_width)
        older = lax.dynamic_slice(kv_grad, key_start, key_box)
        kv_grad = lax.dynamic_update_slice(kv_grad, older + dkeys.reshape(key_box), key_start)
        older = lax.dynamic_slice(kv_grad, value_start, key_box)
        kv_grad = lax.dynamic_update_slice(kv_grad, older + dvalues.reshape(key_box), value_start)
        return (out_buf, query_grad, kv_grad)

    start_carry = (
        jnp.zeros((frames, rows, columns, local_width), jnp.bfloat16),
        jnp.zeros((frames, rows, columns, local_width), jnp.bfloat16),
        jnp.zeros((frames + 2, key_rows, columns + 6, 2 * local_width), jnp.float32),
    )
    out_buf, query_grad, kv_grad = lax.fori_loop(0, tile_count, visit, start_carry)
    grads = kv_grad[:, :, 3 : columns + 3, :]
    near_frames = with_halo(grads, (("tm", 0),), 1)
    owned = near_frames[2 : frames + 2]
    owned = owned.at[0].add(near_frames[0])
    owned = owned.at[frames - 1].add(near_frames[frames + 3])
    near_rows = with_halo(owned, (("height", 1),), 3)
    settled = near_rows[:, 6 : rows + 6]
    settled = settled.at[:, 0:3].add(near_rows[:, 0:3])
    settled = settled.at[:, rows - 3 : rows].add(near_rows[:, rows + 9 : rows + 12])
    grad_low = settled.astype(jnp.bfloat16)
    all_grads = jnp.concatenate([query_grad, grad_low], axis=3).reshape(count, 3 * local_width)
    in_terms = jnp.dot(all_grads, flat_in.T, preferred_element_type=jnp.float32).reshape(
        frames, rows, columns, width
    )
    out_flat = out_buf.reshape(count, local_width)
    out_terms = jnp.dot(out_flat, w_out, preferred_element_type=jnp.float32).reshape(
        frames, rows, columns, width
    )
    mixed_sum, grad_sum = (
        lax.psum_scatter(out_terms, "tensor", scatter_dimension=3, tiled=True),
        lax.psum_scatter(in_terms, "tensor", scatter_dimension=3, tiled=True),
    )
    mixed = mixed_sum.astype(jnp.bfloat16)
    in_grad = grad_sum.astype(jnp.bfloat16)
    return (mixed, in_grad)


def solution(mesh):
    in_specs = (
        P("tm", "height", None, "tensor"),
        P("tm", "height", None, "tensor"),
        P(None, None, "tensor"),
        P("tensor", None),
    )
    out_specs = (P("tm", "height", None, "tensor"), P("tm", "height", None, "tensor"))
    return jax.shard_map(shards, mesh=mesh, in_specs=in_specs, out_specs=out_specs, check_vma=False)
```

profile of v0, /device:TPU:22, one launch (start us, length us, event | category | flops | bytes accessed | tf_op | source)
XLA Modules:
  0.0 435.7 jit_solution(14222418332569755292)
XLA Ops:
  10.4 29.9 %all-gather.3.cloned.1.call-done = bf16[2,4,64,1024]{3,2,1,0:T(8,128)(2,1)} async-done(((bf16[2,4,64,256]{3,2,1,0:T(8,128)(2,1)}), bf16[2,4,64,1024]{3,2,1,0:T(8,128)(2,1)}) %all-gather.3.cloned.1.call-update) | async-done | bytes 1048592 | tf_op jit(solution)/shard_map/all_gather | solution.py:54
  40.3 2.2 convolution_convert_fusion.1
  43.9 5.5 %collective-permute-start = (bf16[1,4,64,512]{3,2,1,0:T(8,128)(2,1)S(1)}, bf16[1,4,64,512]{3,2,1,0:T(8,128)(2,1)S(1)}, u32[]{:S(2)}, u32[]{:S(2)}) collective-permute-start(bf16[1,4,64,512]{3,2,1,0:T(8,128)(2,1)S(1)} %bitcast.98), channel_id=1, source_target_pairs={{0,64},{64,128},{128,192},{1,65},{65,129},{129,193},{2,66},{66,130... | collective-permute-start | bytes 786440 | tf_op jit(solution)/shard_map/ppermute | solution.py:21
  49.5 8.8 %collective-permute-done.1 = bf16[1,4,64,512]{3,2,1,0:T(8,128)(2,1)S(1)} collective-permute-done((bf16[1,4,64,512]{3,2,1,0:T(8,128)(2,1)S(1)}, bf16[1,4,64,512]{3,2,1,0:T(8,128)(2,1)S(1)}, u32[]{:S(2)}, u32[]{:S(2)}) %collective-permute-start.1) | collective-permute-done | bytes 262176 | tf_op jit(solution)/shard_map/ppermute | solution.py:22
  59.4 1.9 collective-permute-start.2
  61.4 4.5 %collective-permute-start.3 = (bf16[4,3,64,512]{3,2,1,0:T(8,128)(2,1)S(1)}, bf16[4,3,64,512]{3,2,1,0:T(8,128)(2,1)}, u32[]{:S(2)}, u32[]{:S(2)}) collective-permute-start(bf16[4,3,64,512]{3,2,1,0:T(8,128)(2,1)S(1)} %get-tuple-element.452), channel_id=1, source_target_pairs={{4,0},{8,4},{12,8},{16,12},{20,16},{24,20},{28,24},{32,28},{36,32}... | collective-permute-start | bytes 2359304 | tf_op jit(solution)/shard_map/ppermute | solution.py:22
  67.2 4.4 %all-gather.5.cloned.1.call-done = bf16[2,4,64,1024]{3,2,1,0:T(8,128)(2,1)} async-done(((bf16[2,4,64,256]{3,2,1,0:T(8,128)(2,1)}), bf16[2,4,64,1024]{3,2,1,0:T(8,128)(2,1)}) %all-gather.5.cloned.1.call-update) | async-done | bytes 1048592 | tf_op jit(solution)/shard_map/all_gather | solution.py:55
  73.3 5.2 %collective-permute-done.2 = bf16[4,3,64,512]{3,2,1,0:T(8,128)(2,1)S(1)} collective-permute-done((bf16[4,3,64,512]{3,2,1,0:T(8,128)(2,1)}, bf16[4,3,64,512]{3,2,1,0:T(8,128)(2,1)S(1)}, u32[]{:S(2)}, u32[]{:S(2)}) %collective-permute-start.2) | collective-permute-done | bytes 786464 | tf_op jit(solution)/shard_map/ppermute | solution.py:21
  79.3 2.2 collective-permute-done.3
  81.6 1.9 pad_maximum_fusion
  83.5 12.3 %copy.50 = bf16[4,10,64,512]{2,1,0,3:T(8,128)(2,1)} copy(bf16[4,10,64,512]{3,2,1,0:T(8,128)(2,1)S(1)} %pad_maximum_fusion) | data formatting | bytes 5242880
  95.8 9.7 %pad.12.clone = bf16[4,10,70,512]{2,1,0,3:T(8,128)(2,1)} pad(bf16[4,10,64,512]{2,1,0,3:T(8,128)(2,1)} %copy.50, bf16[]{:T(256)} %constant.315.clone.1), padding=0_0x0_0x3_3x0_0 | pad | bytes 5488642 | tf_op jit(solution)/shard_map/jit(_pad)/pad | solution.py:68
  107.0 5.1 %broadcast_in_dim.68 = f32[4,10,70,512]{2,3,1,0:T(8,128)} broadcast(f32[]{:T(128)} %constant.316.clone.1), dimensions={} | broadcast | bytes 5734404 | tf_op jit(solution)/shard_map/broadcast_in_dim | solution.py:151
  112.1 176.4 %while.24 = (s32[]{:T(128)}, bf16[2,4,64,256]{3,2,1,0:T(8,128)(2,1)}, bf16[2,4,64,256]{3,2,1,0:T(8,128)(2,1)}, f32[4,10,70,512]{2,3,1,0:T(8,128)}, bf16[2,4,64,2...) while((s32[]{:T(128)}, ...), condition=%wide.region_4.5_spmd.clone, body=%wide.region_0.4_spmd.clone.sunk | while | flops 1150172800 | bytes 161390992 | solution.py:153
  112.6 2.1 constant_dynamic-slice_fusion.6
  117.0 5.9 %fusion.85 = (f32[512]{0:T(512)S(1)}, f32[512,2800]{0,1:T(8,128)S(1)}) fusion(bf16[512,64]{1,0:T(8,128)(2,1)S(1)} %bitcast.88, bf16[2800,64]{0,1:T(8,128)(2,1)S(1)} %reshape.336, pred[2800]{0:T(1024)(128)(4,1)S(1)} %and.252, s32[512]{0:T(512)S(1)} %get-tuple-element.621, s32[2800]{0:T(1024)S(1)} %get-tuple-element.622, ...), kind=kOutput, calls=%fused_computation.53.clone.1 | convolution fusion | flops 209305088 | bytes 6202928 | tf_op jit(solution)/shard_map/while/body/eval_jaxpr/dot_general | solution.py:114
  130.0 3.2 convert_bitcast_fusion.2
  137.0 3.0 dot_general.80
  140.0 1.8 dynamic_update_slice.57
  141.8 5.3 %dot_general.81 = bf16[4,10,70,512]{3,2,1,0:T(8,128)(2,1)} reshape(bf16[2800,512]{1,0:T(8,128)(2,1)} %get-tuple-element.561) | data formatting | bytes 5734400 | tf_op jit(solution)/shard_map/while/body/eval_jaxpr/dot_general | solution.py:137
  147.1 4.1 fusion.89
  151.2 3.9 fusion.90
  155.6 2.1 constant_dynamic-slice_fusion.6
  160.0 5.9 %fusion.85 = (f32[512]{0:T(512)S(1)}, f32[512,2800]{0,1:T(8,128)S(1)}) fusion(bf16[512,64]{1,0:T(8,128)(2,1)S(1)} %bitcast.88, bf16[2800,64]{0,1:T(8,128)(2,1)S(1)} %reshape.336, pred[2800]{0:T(1024)(128)(4,1)S(1)} %and.252, s32[512]{0:T(512)S(1)} %get-tuple-element.621, s32[2800]{0:T(1024)S(1)} %get-tuple-element.622, ...), kind=kOutput, calls=%fused_computation.53.clone.1 | convolution fusion | flops 209305088 | bytes 6202928 | tf_op jit(solution)/shard_map/while/body/eval_jaxpr/dot_general | solution.py:114
  169.7 1.8 dynamic_update_slice.56
  172.5 1.7 copy-done.2
  174.3 3.2 convert_bitcast_fusion.2
  181.3 3.0 dot_general.80
  184.3 3.1 dynamic_update_slice.57
  187.4 5.3 %dot_general.81 = bf16[4,10,70,512]{3,2,1,0:T(8,128)(2,1)} reshape(bf16[2800,512]{1,0:T(8,128)(2,1)} %get-tuple-element.561) | data formatting | bytes 5734400 | tf_op jit(solution)/shard_map/while/body/eval_jaxpr/dot_general | solution.py:137
  192.7 4.0 fusion.89
  196.7 3.9 fusion.90
  201.2 2.1 constant_dynamic-slice_fusion.6
  205.6 5.9 %fusion.85 = (f32[512]{0:T(512)S(1)}, f32[512,2800]{0,1:T(8,128)S(1)}) fusion(bf16[512,64]{1,0:T(8,128)(2,1)S(1)} %bitcast.88, bf16[2800,64]{0,1:T(8,128)(2,1)S(1)} %reshape.336, pred[2800]{0:T(1024)(128)(4,1)S(1)} %and.252, s32[512]{0:T(512)S(1)} %get-tuple-element.621, s32[2800]{0:T(1024)S(1)} %get-tuple-element.622, ...), kind=kOutput, calls=%fused_computation.53.clone.1 | convolution fusion | flops 209305088 | bytes 6202928 | tf_op jit(solution)/shard_map/while/body/eval_jaxpr/dot_general | solution.py:114
  216.7 1.7 copy-done.2
  218.5 3.2 convert_bitcast_fusion.2
  225.5 3.0 dot_general.80
  230.1 5.3 %dot_general.81 = bf16[4,10,70,512]{3,2,1,0:T(8,128)(2,1)} reshape(bf16[2800,512]{1,0:T(8,128)(2,1)} %get-tuple-element.561) | data formatting | bytes 5734400 | tf_op jit(solution)/shard_map/while/body/eval_jaxpr/dot_general | solution.py:137
  235.4 4.0 fusion.89
  239.5 3.9 fusion.90
  243.9 2.1 constant_dynamic-slice_fusion.6
  248.3 5.9 %fusion.85 = (f32[512]{0:T(512)S(1)}, f32[512,2800]{0,1:T(8,128)S(1)}) fusion(bf16[512,64]{1,0:T(8,128)(2,1)S(1)} %bitcast.88, bf16[2800,64]{0,1:T(8,128)(2,1)S(1)} %reshape.336, pred[2800]{0:T(1024)(128)(4,1)S(1)} %and.252, s32[512]{0:T(512)S(1)} %get-tuple-element.621, s32[2800]{0:T(1024)S(1)} %get-tuple-element.622, ...), kind=kOutput, calls=%fused_computation.53.clone.1 | convolution fusion | flops 209305088 | bytes 6202928 | tf_op jit(solution)/shard_map/while/body/eval_jaxpr/dot_general | solution.py:114
  258.0 1.8 dynamic_update_slice.56
  260.8 1.7 copy-done.2
  262.5 3.2 convert_bitcast_fusion.2
  269.6 3.0 dot_general.80
  272.5 2.5 dynamic_update_slice.57
  275.0 5.3 %dot_general.81 = bf16[4,10,70,512]{3,2,1,0:T(8,128)(2,1)} reshape(bf16[2800,512]{1,0:T(8,128)(2,1)} %get-tuple-element.561) | data formatting | bytes 5734400 | tf_op jit(solution)/shard_map/while/body/eval_jaxpr/dot_general | solution.py:137
  280.3 4.0 fusion.89
  284.4 3.9 fusion.90
  288.6 10.0 %copy.32 = f32[4,10,70,512]{3,2,1,0:T(8,128)} copy(f32[4,10,70,512]{2,3,1,0:T(8,128)} %get-tuple-element.320) | data formatting | bytes 11468800 | tf_op jit(solution)/shard_map/while | solution.py:153
  298.6 1.8 fusion.29
  300.4 2.2 fusion.33
  302.6 6.2 %collective-permute-start.4 = (f32[1,10,64,512]{3,2,1,0:T(8,128)S(1)}, f32[1,10,64,512]{3,2,1,0:T(8,128)S(1)}, u32[]{:S(2)}, u32[]{:S(2)}) collective-permute-start(f32[1,10,64,512]{3,2,1,0:T(8,128)S(1)} %get-tuple-element.448), channel_id=1, source_target_pairs={{0,64},{64,128},{128,192},{1,65},{65,129},{129,193},{2,66},{66,130... | collective-permute-start | bytes 3932168 | tf_op jit(solution)/shard_map/ppermute | solution.py:21
  310.1 2.2 slice.186
  312.3 25.5 %collective-permute-done.4 = f32[1,10,64,512]{3,2,1,0:T(8,128)S(1)} collective-permute-done((f32[1,10,64,512]{3,2,1,0:T(8,128)S(1)}, f32[1,10,64,512]{3,2,1,0:T(8,128)S(1)}, u32[]{:S(2)}, u32[]{:S(2)}) %collective-permute-start.4) | collective-permute-done | bytes 1310752 | tf_op jit(solution)/shard_map/ppermute | solution.py:21
  339.4 33.5 %collective-permute-done.5 = f32[1,10,64,512]{3,2,1,0:T(8,128)S(1)} collective-permute-done((f32[1,10,64,512]{3,2,1,0:T(8,128)S(1)}, f32[1,10,64,512]{3,2,1,0:T(8,128)S(1)}, u32[]{:S(2)}, u32[]{:S(2)}) %collective-permute-start.5) | collective-permute-done | bytes 1310752 | tf_op jit(solution)/shard_map/ppermute | solution.py:22
  373.4 1.9 collective-permute-start.6
  375.3 4.5 %collective-permute-start.7 = (f32[2,3,64,512]{3,2,1,0:T(8,128)S(1)}, f32[2,3,64,512]{3,2,1,0:T(8,128)S(1)}, u32[]{:S(2)}, u32[]{:S(2)}) collective-permute-start(f32[2,3,64,512]{3,2,1,0:T(8,128)S(1)} %get-tuple-element.449), channel_id=1, source_target_pairs={{4,0},{8,4},{12,8},{16,12},{20,16},{24,20},{28,24},{32,28},{36,32}... | collective-permute-start | bytes 2359304 | tf_op jit(solution)/shard_map/ppermute | solution.py:22
  380.0 14.5 %collective-permute-done.6 = f32[2,3,64,512]{3,2,1,0:T(8,128)S(1)} collective-permute-done((f32[2,3,64,512]{3,2,1,0:T(8,128)S(1)}, f32[2,3,64,512]{3,2,1,0:T(8,128)S(1)}, u32[]{:S(2)}, u32[]{:S(2)}) %collective-permute-start.6) | collective-permute-done | bytes 786464 | tf_op jit(solution)/shard_map/ppermute | solution.py:21
  395.0 2.4 fusion.25
  397.4 1.8 convert_element_type.69
  399.2 28.2 %reduce-scatter.5.cloned.1.call-done = f32[2,4,64,256]{3,2,1,0:T(8,128)} async-done(((f32[2,4,64,1024]{3,2,1,0:T(8,128)}), f32[2,4,64,256]{3,2,1,0:T(8,128)}) %reduce-scatter.5.cloned.1.call-update) | async-done | bytes 524304 | tf_op jit(solution)/shard_map/reduce_scatter | solution.py:174
  427.4 1.8 convert_element_type.71
  (262 shorter events, 64.7 us)
Async XLA Ops:
  7.2 64.4 %copy-start = (bf16[256,1024]{1,0:T(8,128)(2,1)S(1)}, bf16[256,1024]{1,0:T(8,128)(2,1)}, u32[]{:S(2)}) copy-start(bf16[256,1024]{1,0:T(8,128)(2,1)} %param.17) | copy-start | bytes 1572868
  7.2 33.1 %all-gather.3.cloned.1.call-start = ((), (), s32[]{:S(2)}) async-start(), calls=%async_computation.2 | async-start | bytes 1310720 | tf_op jit(solution)/shard_map/all_gather | solution.py:54
  7.9 63.7 %all-gather.5.cloned.1.call-start = ((), (), s32[]{:S(2)}) async-start(), calls=%async_computation.3 | async-start | bytes 1310720 | tf_op jit(solution)/shard_map/all_gather | solution.py:55
  8.7 388.7 %reduce-scatter.3.cloned.1.call-start = ((), (), s32[]{:S(2)}) async-start(), calls=%async_computation.4 | async-start | bytes 2621440 | tf_op jit(solution)/shard_map/reduce_scatter | solution.py:173
  10.4 32.2 %copy-start.16 = (bf16[1024,3,256]{0,2,1:T(8,128)(2,1)}, bf16[1024,3,256]{0,2,1:T(8,128)(2,1)S(1)}, u32[]{:S(2)}) copy-start(bf16[1024,3,256]{0,2,1:T(8,128)(2,1)S(1)} %copy.27) | copy-start | bytes 4718596
  42.6 24.6 %copy-start.11 = (bf16[512,768]{1,0:T(8,128)(2,1)}, bf16[512,768]{1,0:T(8,128)(2,1)S(1)}, u32[]{:S(2)}) copy-start(bf16[512,768]{1,0:T(8,128)(2,1)S(1)} %convolution_convert_fusion.1) | copy-start | bytes 2359300
  42.6 15.6 %collective-permute-start.1 = (bf16[1,4,64,512]{3,2,1,0:T(8,128)(2,1)S(1)}, bf16[1,4,64,512]{3,2,1,0:T(8,128)(2,1)S(1)}, u32[]{:S(2)}, u32[]{:S(2)}) collective-permute-start(bf16[1,4,64,512]{3,2,1,0:T(8,128)(2,1)S(1)} %bitcast.99), channel_id=1, source_target_pairs={{64,0},{128,64},{192,128},{65,1},{129,65},{193,129},{66,2},{130,66... | collective-permute-start | bytes 786440 | tf_op jit(solution)/shard_map/ppermute | solution.py:22
  43.9 14.3 %collective-permute-start = (bf16[1,4,64,512]{3,2,1,0:T(8,128)(2,1)S(1)}, bf16[1,4,64,512]{3,2,1,0:T(8,128)(2,1)S(1)}, u32[]{:S(2)}, u32[]{:S(2)}) collective-permute-start(bf16[1,4,64,512]{3,2,1,0:T(8,128)(2,1)S(1)} %bitcast.98), channel_id=1, source_target_pairs={{0,64},{64,128},{128,192},{1,65},{65,129},{129,193},{2,66},{66,130... | collective-permute-start | bytes 786440 | tf_op jit(solution)/shard_map/ppermute | solution.py:21
  49.5 10.0 %copy-start.10 = (bf16[512,512]{1,0:T(8,128)(2,1)}, bf16[512,512]{1,0:T(8,128)(2,1)S(1)}, u32[]{:S(2)}) copy-start(bf16[512,512]{1,0:T(8,128)(2,1)S(1)} %slice.182) | copy-start | bytes 1572868
  59.4 19.0 %collective-permute-start.2 = (bf16[4,3,64,512]{3,2,1,0:T(8,128)(2,1)}, bf16[4,3,64,512]{3,2,1,0:T(8,128)(2,1)S(1)}, u32[]{:S(2)}, u32[]{:S(2)}) collective-permute-start(bf16[4,3,64,512]{3,2,1,0:T(8,128)(2,1)} %get-tuple-element.451), channel_id=1, source_target_pairs={{0,4},{4,8},{8,12},{12,16},{16,20},{20,24},{24,28},{28,32},{32,36}... | collective-permute-start | bytes 2359304 | tf_op jit(solution)/shard_map/ppermute | solution.py:21
  61.4 20.2 %collective-permute-start.3 = (bf16[4,3,64,512]{3,2,1,0:T(8,128)(2,1)S(1)}, bf16[4,3,64,512]{3,2,1,0:T(8,128)(2,1)}, u32[]{:S(2)}, u32[]{:S(2)}) collective-permute-start(bf16[4,3,64,512]{3,2,1,0:T(8,128)(2,1)S(1)} %get-tuple-element.452), channel_id=1, source_target_pairs={{4,0},{8,4},{12,8},{16,12},{20,16},{24,20},{28,24},{32,28},{36,32}... | collective-permute-start | bytes 2359304 | tf_op jit(solution)/shard_map/ppermute | solution.py:22
  107.0 5.2 %slice-start = ((bf16[512,768]{1,0:T(8,128)(2,1)}), bf16[512,256]{1,0:T(8,128)(2,1)S(1)}, s32[]{:S(2)}) async-start(bf16[512,768]{1,0:T(8,128)(2,1)} %copy-done.11), calls=%async_computation.6 | async-start | bytes 524288 | tf_op jit(solution)/shard_map/slice | solution.py:61
  112.1 3.7 copy-start.14
  112.1 4.9 %copy-start.25 = (s32[2800]{0:T(1024)}, s32[2800]{0:T(1024)S(1)}, u32[]{:S(2)}) copy-start(s32[2800]{0:T(1024)S(1)} %get-tuple-element.618) | copy-start | bytes 33604 | tf_op jit(solution)/shard_map/while
  112.6 4.4 %copy-start.9 = (bf16[2,4,64,64]{3,2,1,0:T(8,128)(2,1)}, bf16[2,4,64,64]{3,2,1,0:T(8,128)(2,1)S(1)}, u32[]{:S(2)}) copy-start(bf16[2,4,64,64]{3,2,1,0:T(8,128)(2,1)S(1)} %get-tuple-element.555) | copy-start | bytes 196612 | tf_op jit(solution)/shard_map/while
  112.6 14.6 %copy-start.7 = (bf16[2,4,64,64]{3,2,1,0:T(8,128)(2,1)}, bf16[2,4,64,64]{3,2,1,0:T(8,128)(2,1)S(1)}, u32[]{:S(2)}) copy-start(bf16[2,4,64,64]{3,2,1,0:T(8,128)(2,1)S(1)} %get-tuple-element.559) | copy-start | bytes 196612 | tf_op jit(solution)/shard_map/while
  117.0 5.9 %copy-start.5 = (bf16[2800,64]{0,1:T(8,128)(2,1)}, bf16[2800,64]{0,1:T(8,128)(2,1)S(1)}, u32[]{:S(2)}) copy-start(bf16[2800,64]{0,1:T(8,128)(2,1)S(1)} %reshape.336) | copy-start | bytes 1075204 | tf_op jit(solution)/shard_map/while
  141.8 5.3 %copy-start.3 = (bf16[4,10,70,512]{3,2,1,0:T(8,128)(2,1)S(1)}, bf16[4,10,70,512]{3,2,1,0:T(8,128)(2,1)}, u32[]{:S(2)}) copy-start(bf16[4,10,70,512]{3,2,1,0:T(8,128)(2,1)} %dot_general.80) | copy-start | bytes 8601604 | tf_op jit(solution)/shard_map/while
  147.1 4.1 copy-start.4
  147.1 4.1 copy-start.8
  151.2 3.9 copy-start.13
  151.2 3.9 copy-start.15
  151.2 3.9 copy-start.26
  155.1 3.7 copy-start.14
  155.1 4.9 %copy-start.25 = (s32[2800]{0:T(1024)}, s32[2800]{0:T(1024)S(1)}, u32[]{:S(2)}) copy-start(s32[2800]{0:T(1024)S(1)} %get-tuple-element.618) | copy-start | bytes 33604 | tf_op jit(solution)/shard_map/while
  155.6 4.4 %copy-start.9 = (bf16[2,4,64,64]{3,2,1,0:T(8,128)(2,1)}, bf16[2,4,64,64]{3,2,1,0:T(8,128)(2,1)S(1)}, u32[]{:S(2)}) copy-start(bf16[2,4,64,64]{3,2,1,0:T(8,128)(2,1)S(1)} %get-tuple-element.555) | copy-start | bytes 196612 | tf_op jit(solution)/shard_map/while
  155.6 15.9 %copy-start.7 = (bf16[2,4,64,64]{3,2,1,0:T(8,128)(2,1)}, bf16[2,4,64,64]{3,2,1,0:T(8,128)(2,1)S(1)}, u32[]{:S(2)}) copy-start(bf16[2,4,64,64]{3,2,1,0:T(8,128)(2,1)S(1)} %get-tuple-element.559) | copy-start | bytes 196612 | tf_op jit(solution)/shard_map/while
  160.0 5.9 %copy-start.5 = (bf16[2800,64]{0,1:T(8,128)(2,1)}, bf16[2800,64]{0,1:T(8,128)(2,1)S(1)}, u32[]{:S(2)}) copy-start(bf16[2800,64]{0,1:T(8,128)(2,1)S(1)} %reshape.336) | copy-start | bytes 1075204 | tf_op jit(solution)/shard_map/while
  187.4 5.3 %copy-start.3 = (bf16[4,10,70,512]{3,2,1,0:T(8,128)(2,1)S(1)}, bf16[4,10,70,512]{3,2,1,0:T(8,128)(2,1)}, u32[]{:S(2)}) copy-start(bf16[4,10,70,512]{3,2,1,0:T(8,128)(2,1)} %dot_general.80) | copy-start | bytes 8601604 | tf_op jit(solution)/shard_map/while
  192.7 4.0 copy-start.4
  192.7 4.0 copy-start.8
  196.7 3.9 copy-start.13
  196.7 3.9 copy-start.15
  196.7 3.9 copy-start.26
  200.7 3.7 copy-start.14
  200.7 4.9 %copy-start.25 = (s32[2800]{0:T(1024)}, s32[2800]{0:T(1024)S(1)}, u32[]{:S(2)}) copy-start(s32[2800]{0:T(1024)S(1)} %get-tuple-element.618) | copy-start | bytes 33604 | tf_op jit(solution)/shard_map/while
  201.2 4.4 %copy-start.9 = (bf16[2,4,64,64]{3,2,1,0:T(8,128)(2,1)}, bf16[2,4,64,64]{3,2,1,0:T(8,128)(2,1)S(1)}, u32[]{:S(2)}) copy-start(bf16[2,4,64,64]{3,2,1,0:T(8,128)(2,1)S(1)} %get-tuple-element.555) | copy-start | bytes 196612 | tf_op jit(solution)/shard_map/while
  201.2 14.6 %copy-start.7 = (bf16[2,4,64,64]{3,2,1,0:T(8,128)(2,1)}, bf16[2,4,64,64]{3,2,1,0:T(8,128)(2,1)S(1)}, u32[]{:S(2)}) copy-start(bf16[2,4,64,64]{3,2,1,0:T(8,128)(2,1)S(1)} %get-tuple-element.559) | copy-start | bytes 196612 | tf_op jit(solution)/shard_map/while
  205.5 5.9 %copy-start.5 = (bf16[2800,64]{0,1:T(8,128)(2,1)}, bf16[2800,64]{0,1:T(8,128)(2,1)S(1)}, u32[]{:S(2)}) copy-start(bf16[2800,64]{0,1:T(8,128)(2,1)S(1)} %reshape.336) | copy-start | bytes 1075204 | tf_op jit(solution)/shard_map/while
  230.1 5.3 %copy-start.3 = (bf16[4,10,70,512]{3,2,1,0:T(8,128)(2,1)S(1)}, bf16[4,10,70,512]{3,2,1,0:T(8,128)(2,1)}, u32[]{:S(2)}) copy-start(bf16[4,10,70,512]{3,2,1,0:T(8,128)(2,1)} %dot_general.80) | copy-start | bytes 8601604 | tf_op jit(solution)/shard_map/while
  235.4 4.0 copy-start.4
  235.4 4.0 copy-start.8
  239.5 3.9 copy-start.13
  239.5 3.9 copy-start.15
  239.5 3.9 copy-start.26
  243.4 3.7 copy-start.14
  243.4 4.9 %copy-start.25 = (s32[2800]{0:T(1024)}, s32[2800]{0:T(1024)S(1)}, u32[]{:S(2)}) copy-start(s32[2800]{0:T(1024)S(1)} %get-tuple-element.618) | copy-start | bytes 33604 | tf_op jit(solution)/shard_map/while
  243.9 4.4 %copy-start.9 = (bf16[2,4,64,64]{3,2,1,0:T(8,128)(2,1)}, bf16[2,4,64,64]{3,2,1,0:T(8,128)(2,1)S(1)}, u32[]{:S(2)}) copy-start(bf16[2,4,64,64]{3,2,1,0:T(8,128)(2,1)S(1)} %get-tuple-element.555) | copy-start | bytes 196612 | tf_op jit(solution)/shard_map/while
  243.9 15.9 %copy-start.7 = (bf16[2,4,64,64]{3,2,1,0:T(8,128)(2,1)}, bf16[2,4,64,64]{3,2,1,0:T(8,128)(2,1)S(1)}, u32[]{:S(2)}) copy-start(bf16[2,4,64,64]{3,2,1,0:T(8,128)(2,1)S(1)} %get-tuple-element.559) | copy-start | bytes 196612 | tf_op jit(solution)/shard_map/while
  248.3 5.9 %copy-start.5 = (bf16[2800,64]{0,1:T(8,128)(2,1)}, bf16[2800,64]{0,1:T(8,128)(2,1)S(1)}, u32[]{:S(2)}) copy-start(bf16[2800,64]{0,1:T(8,128)(2,1)S(1)} %reshape.336) | copy-start | bytes 1075204 | tf_op jit(solution)/shard_map/while
  275.0 5.3 %copy-start.3 = (bf16[4,10,70,512]{3,2,1,0:T(8,128)(2,1)S(1)}, bf16[4,10,70,512]{3,2,1,0:T(8,128)(2,1)}, u32[]{:S(2)}) copy-start(bf16[4,10,70,512]{3,2,1,0:T(8,128)(2,1)} %dot_general.80) | copy-start | bytes 8601604 | tf_op jit(solution)/shard_map/while
  280.3 4.1 copy-start.4
  280.3 4.1 copy-start.8
  284.4 4.0 copy-start.13
  284.4 4.0 copy-start.15
  284.4 4.0 copy-start.26
  288.6 10.0 %copy-start.22 = (bf16[2,4,64,256]{3,2,1,0:T(8,128)(2,1)S(1)}, bf16[2,4,64,256]{3,2,1,0:T(8,128)(2,1)}, u32[]{:S(2)}) copy-start(bf16[2,4,64,256]{3,2,1,0:T(8,128)(2,1)} %get-tuple-element.318) | copy-start | bytes 786436
  300.4 127.0 %reduce-scatter.5.cloned.1.call-start = ((), (), s32[]{:S(2)}) async-start(), calls=%async_computation.5 | async-start | bytes 2621440 | tf_op jit(solution)/shard_map/reduce_scatter | solution.py:174
  302.6 35.1 %collective-permute-start.4 = (f32[1,10,64,512]{3,2,1,0:T(8,128)S(1)}, f32[1,10,64,512]{3,2,1,0:T(8,128)S(1)}, u32[]{:S(2)}, u32[]{:S(2)}) collective-permute-start(f32[1,10,64,512]{3,2,1,0:T(8,128)S(1)} %get-tuple-element.448), channel_id=1, source_target_pairs={{0,64},{64,128},{128,192},{1,65},{65,129},{129,193},{2,66},{66,130... | collective-permute-start | bytes 3932168 | tf_op jit(solution)/shard_map/ppermute | solution.py:21
  308.8 64.1 %collective-permute-start.5 = (f32[1,10,64,512]{3,2,1,0:T(8,128)S(1)}, f32[1,10,64,512]{3,2,1,0:T(8,128)S(1)}, u32[]{:S(2)}, u32[]{:S(2)}) collective-permute-start(f32[1,10,64,512]{3,2,1,0:T(8,128)S(1)} %get-tuple-element.447), channel_id=1, source_target_pairs={{64,0},{128,64},{192,128},{65,1},{129,65},{193,129},{66,2},{130,66... | collective-permute-start | bytes 3932168 | tf_op jit(solution)/shard_map/ppermute | solution.py:22
  373.4 21.1 %collective-permute-start.6 = (f32[2,3,64,512]{3,2,1,0:T(8,128)S(1)}, f32[2,3,64,512]{3,2,1,0:T(8,128)S(1)}, u32[]{:S(2)}, u32[]{:S(2)}) collective-permute-start(f32[2,3,64,512]{3,2,1,0:T(8,128)S(1)} %get-tuple-element.450), channel_id=1, source_target_pairs={{0,4},{4,8},{8,12},{12,16},{16,20},{20,24},{24,28},{28,32},{32,36}... | collective-permute-start | bytes 2359304 | tf_op jit(solution)/shard_map/ppermute | solution.py:21
  375.3 19.3 %collective-permute-start.7 = (f32[2,3,64,512]{3,2,1,0:T(8,128)S(1)}, f32[2,3,64,512]{3,2,1,0:T(8,128)S(1)}, u32[]{:S(2)}, u32[]{:S(2)}) collective-permute-start(f32[2,3,64,512]{3,2,1,0:T(8,128)S(1)} %get-tuple-element.449), channel_id=1, source_target_pairs={{4,0},{8,4},{12,8},{16,12},{20,16},{24,20},{28,24},{32,28},{36,32}... | collective-permute-start | bytes 2359304 | tf_op jit(solution)/shard_map/ppermute | solution.py:22
  379.9 15.0 %copy-start.17 = (bf16[1024,3,256]{0,2,1:T(8,128)(2,1)S(1)}, bf16[1024,3,256]{0,2,1:T(8,128)(2,1)}, u32[]{:S(2)}) copy-start(bf16[1024,3,256]{0,2,1:T(8,128)(2,1)} %copy-done.16) | copy-start | bytes 4718596
  380.0 15.0 %copy-start.24 = (bf16[2,4,64,256]{3,2,1,0:T(8,128)(2,1)S(1)}, bf16[2,4,64,256]{3,2,1,0:T(8,128)(2,1)}, u32[]{:S(2)}) copy-start(bf16[2,4,64,256]{3,2,1,0:T(8,128)(2,1)} %get-tuple-element.319) | copy-start | bytes 786436
  (27 other events, 52.0 us)
Sparse Core Ops, SparseCore 0:
  9.8 30.4 all-gather.2
  42.1 29.3 all-gather.4
  300.5 35.4 reduce-scatter.2
  397.5 29.8 reduce-scatter.4
where the time goes:
time: 441 us; the launch traced here: 436 us
  waiting for transfers between devices  154 us (35%)
  local copies, waits for them, and re-layouts  131 us (30%)
  matrix products  76.7 us (17%)
  other arithmetic  31.3 us (7%)
  starting transfers between devices  27.3 us (6%)
  between operations  14.1 us (3%)
    ppermute x4, waiting for transfers between devices, with_halo(): before = lax.ppermute(last, axis, up)  45.2 us
    ppermute x4, waiting for transfers between devices, with_halo(): after = lax.ppermute(initial, axis, down)  44.5 us
    all_gather x1, waiting for transfers between devices, shards(): lax.all_gather(tokens, 'tensor', axis=3, tiled=True)  29.9 us
    reduce_scatter x1, waiting for transfers between devices, shards(): lax.psum_scatter(in_terms, 'tensor', scatter_dimension=3, tiled=True)  28.2 us
    dot_general x4, matrix products, visit(): lax.dot_general(query_tile, key_tile, contract_last, preferred_element_ty...  23.7 us
    dot_general x4, local copies, waits for them, and re-layouts, visit(): lax.dot_general(probs_low, back_tile, contract_first, preferred_element_t...  21.1 us
    dot_general x4, matrix products, visit(): lax.dot_general(dscore, query_tile, contract_first, preferred_element_typ...  16.2 us
    dot_general x4, matrix products, visit(): lax.dot_general(probs_low, back_tile, contract_first, preferred_element_t...  15.6 us
  transfers between devices with their start and end apart: 12, of which 9 were waited for; matrix products, arithmetic and copies ran while one was open for 4% of the time, Pallas kernels for 0%

commit v1 on v0

v1 whole, which is shorter than its diff:
```python
import math

import jax
import jax.numpy as jnp
from jax import lax
from jax.experimental import pallas as pl
from jax.experimental.pallas import tpu as pltpu
from jax.sharding import PartitionSpec as P

NT = (((1,), (1,)), ((), ()))
NN = (((1,), (0,)), ((), ()))
F32, BF16 = jnp.float32, jnp.bfloat16
NEG_FILL = -1e30


def dot(a, b, dims=NN):
    return lax.dot_general(a, b, dims, preferred_element_type=F32)


def attend_body(valid, q, b, own, tmb, tma, hb, ha, bb, ba, ab, aa,
                att, dq, g_own, g_tmb, g_tma, g_hb, g_ha, g_bb, g_ba, g_ab, g_aa,
                ks, vs, kt, vt, dk, dv, s_buf, t_buf, p_buf, d_buf, bias):
    def put(frame, row, block):
        rows = block.shape[0]
        block = block.reshape(rows * 64, 512)
        at = pl.ds((frame * 10 + row) * 64, rows * 64)
        ks[at, :] = block[:, :256]
        vs[at, :] = block[:, 256:]

    for i in range(2):
        put(1 + i, 0, hb[i])
        put(1 + i, 3, own[i])
        put(1 + i, 7, ha[i])
    put(0, 0, bb[0])
    put(0, 3, tmb[0])
    put(0, 7, ba[0])
    put(3, 0, ab[0])
    put(3, 3, tma[0])
    put(3, 7, aa[0])

    row256 = lax.broadcasted_iota(jnp.int32, (256, 256), 0)
    lane256 = lax.broadcasted_iota(jnp.int32, (256, 256), 1)
    eye = jnp.where(row256 == lane256, 1.0, 0.0).astype(BF16)
    same_head = (row256 // 64) == (lane256 // 64)
    for i in range(5):
        at = pl.ds(i * 512, 512)
        kt[0, :, at] = dot(eye, ks[at, :], NT).astype(BF16)
        vt[0, :, at] = dot(eye, vs[at, :], NT).astype(BF16)
        width = 512 if i < 4 else 448
        src, dst = pl.ds(i * 512 + 64, width), pl.ds(i * 512, width)
        kt[1, :, dst] = dot(eye, ks[src, :], NT).astype(BF16)
        vt[1, :, dst] = dot(eye, vs[src, :], NT).astype(BF16)
    dk[...] = jnp.zeros_like(dk)
    dv[...] = jnp.zeros_like(dv)
    krow = lax.broadcasted_iota(jnp.int32, (64, 256), 0)
    qcol = lax.broadcasted_iota(jnp.int32, (64, 256), 1) % 64
    bias[0] = jnp.full((64, 256), NEG_FILL, F32)
    bias[1] = jnp.where(jnp.abs(krow - qcol) <= 3, 0.0, NEG_FILL)
    lane_head = lax.broadcasted_iota(jnp.int32, (64, 256), 1) // 64

    def spread(rows):
        return jnp.where(same_head, jnp.concatenate([rows] * 4, axis=0), jnp.zeros((), BF16))

    def gather(outT):
        out = outT.T
        res = out[0:64]
        for h in range(1, 4):
            res = jnp.where(lane_head == h, out[h * 64:(h + 1) * 64], res)
        return res

    def group(g, _):
        f, r = g // 4, g % 4
        par = r % 2
        mine = pl.ds(pl.multiple_of(g * 64, 64), 64)
        qbd = spread(q[mine, :])
        bbd = spread(b[mine, :])

        def rows_of(i):
            return pl.ds(pl.multiple_of(((f + i) * 10 + r) * 64, 64), 448)

        def lanes_of(i):
            return pl.ds(pl.multiple_of(((f + i) * 10 + r - par) * 64, 128), 448)

        top = jnp.full((64, 256), NEG_FILL, F32)
        for i in range(3):
            sc = dot(ks[rows_of(i), :], qbd, NT)
            for j in range(7):
                v = sc[j * 64:(j + 1) * 64] + bias[valid[f + i, r + j]]
                s_buf[pl.ds((i * 7 + j) * 64, 64), :] = v
                top = jnp.maximum(top, v)
        m = jnp.max(top, axis=0, keepdims=True)
        tot = jnp.zeros((64, 256), F32)
        for j in range(21):
            at = pl.ds(j * 64, 64)
            e = jnp.exp(s_buf[at, :] - m)
            s_buf[at, :] = e
            tot = tot + e
        inv = 1.0 / jnp.sum(tot, axis=0, keepdims=True)
        cen = jnp.zeros((64, 256), F32)
        for i in range(3):
            sl = dot(vs[rows_of(i), :], bbd, NT)
            for j in range(7):
                at = pl.ds((i * 7 + j) * 64, 64)
                p = s_buf[at, :] * inv
                s_buf[at, :] = p
                p_buf[at, :] = p.astype(BF16)
                x = sl[j * 64:(j + 1) * 64]
                t_buf[at, :] = x
                cen = cen + p * x
        c = jnp.sum(cen, axis=0, keepdims=True)
        for j in range(21):
            at = pl.ds(j * 64, 64)
            d_buf[at, :] = (s_buf[at, :] * (t_buf[at, :] - c)).astype(BF16)
        outT = jnp.zeros((256, 256), F32)
        dqT = jnp.zeros((256, 256), F32)
        for i in range(3):
            at = pl.ds(i * 448, 448)
            pb, db = p_buf[at, :], d_buf[at, :]
            outT = outT + dot(vt[par, :, lanes_of(i)], pb)
            dqT = dqT + dot(kt[par, :, lanes_of(i)], db)
            dv[rows_of(i), :] += dot(pb, bbd)
            dk[rows_of(i), :] += dot(db, qbd)
        att[mine, :] = gather(outT).astype(BF16)
        dq[mine, :] = (gather(dqT) * 0.125).astype(BF16)
        return 0

    lax.fori_loop(0, 8, group, 0)

    def take(frame, row, rows, out):
        at = pl.ds((frame * 10 + row) * 64, rows * 64)
        kv = jnp.concatenate([dk[at, :], dv[at, :]], axis=1)
        return kv.reshape(rows, 64, 512).astype(out.dtype)

    for i in range(2):
        g_hb[i] = take(1 + i, 0, 3, g_hb)
        g_own[i] = take(1 + i, 3, 4, g_own)
        g_ha[i] = take(1 + i, 7, 3, g_ha)
    g_bb[0] = take(0, 0, 3, g_bb)
    g_tmb[0] = take(0, 3, 4, g_tmb)
    g_ba[0] = take(0, 7, 3, g_ba)
    g_ab[0] = take(3, 0, 3, g_ab)
    g_tma[0] = take(3, 3, 4, g_tma)
    g_aa[0] = take(3, 7, 3, g_aa)


def attend(valid, q, b, own, pieces):
    S = jax.ShapeDtypeStruct
    frame, rows, corner = (1, 4, 64, 512), (2, 3, 64, 512), (1, 3, 64, 512)
    outs = (S((512, 256), BF16), S((512, 256), BF16), S((2, 4, 64, 512), F32),
            S(frame, BF16), S(frame, BF16), S(rows, BF16), S(rows, BF16),
            S(corner, BF16), S(corner, BF16), S(corner, BF16), S(corner, BF16))
    vm = pl.BlockSpec(memory_space=pltpu.VMEM)
    return pl.pallas_call(
        attend_body,
        out_shape=outs,
        in_specs=[pl.BlockSpec(memory_space=pltpu.SMEM)] + [vm] * 11,
        out_specs=(vm,) * 11,
        scratch_shapes=[
            pltpu.VMEM((2560, 256), BF16), pltpu.VMEM((2560, 256), BF16),
            pltpu.VMEM((2, 256, 2560), BF16), pltpu.VMEM((2, 256, 2560), BF16),
            pltpu.VMEM((2560, 256), F32), pltpu.VMEM((2560, 256), F32),
            pltpu.VMEM((1344, 256), F32), pltpu.VMEM((1344, 256), F32),
            pltpu.VMEM((1344, 256), BF16), pltpu.VMEM((1344, 256), BF16),
            pltpu.VMEM((2, 64, 256), F32),
        ],
        compiler_params=pltpu.CompilerParams(vmem_limit_bytes=32 * 1024 * 1024),
        cost_estimate=pl.CostEstimate(
            flops=8 * 6 * 2 * 1344 * 256 * 256, bytes_accessed=12 * 2**20, transcendentals=8 * 1344 * 256
        ),
        name="attend",
    )(valid, q, b, own, *pieces)


def project_body(idx, x0, x1, x2, x3, w, q, own, f0, f1, lo, hi, c0lo, c0hi, c1lo, c1hi):
    acc = None
    for i, x in enumerate((x0, x1, x2, x3)):
        at = pl.ds(pl.multiple_of(idx[i] * 256, 256), 256)
        part = [dot(x[...], w[n, at, :]) for n in range(3)]
        acc = part if acc is None else [a + b for a, b in zip(acc, part)]
    q[...] = acc[0].astype(BF16) * jnp.asarray(0.125, BF16)
    kv = jnp.concatenate([acc[1], acc[2]], axis=1).astype(BF16).reshape(2, 4, 64, 512)
    own[...] = kv
    f0[...] = kv[0:1]
    f1[...] = kv[1:2]
    lo[...] = kv[:, 0:3]
    hi[...] = kv[:, 1:4]
    c0lo[...] = kv[0:1, 0:3]
    c0hi[...] = kv[0:1, 1:4]
    c1lo[...] = kv[1:2, 0:3]
    c1hi[...] = kv[1:2, 1:4]


def back_body(idx, x0, x1, x2, x3, w, out):
    acc = None
    for i, x in enumerate((x0, x1, x2, x3)):
        part = dot(x[...], w[:, pl.ds(pl.multiple_of(idx[i] * 256, 256), 256)], NT)
        acc = part if acc is None else acc + part
    out[...] = acc.astype(BF16)


def mixed_body(idx, att, w, own, right, left, across):
    for i, out in enumerate((own, right, left, across)):
        block = w[:, pl.ds(pl.multiple_of(idx[i] * 256, 256), 256)]
        out[...] = dot(att[...], block).astype(out.dtype)


def grad_body(idx, dq, own, r1, r2, r3, r4, r5, r6, r7, r8, w, mine, right, left, across, kv):
    kv[...] = own[...]
    kv[1] += r1[0].astype(F32)
    kv[0] += r2[0].astype(F32)
    kv[:, 1:4] += r3[...].astype(F32)
    kv[:, 0:3] += r4[...].astype(F32)
    kv[1, 1:4] += r5[0].astype(F32)
    kv[1, 0:3] += r6[0].astype(F32)
    kv[0, 1:4] += r7[0].astype(F32)
    kv[0, 0:3] += r8[0].astype(F32)
    low = kv[...].reshape(512, 512).astype(BF16)
    for i, out in enumerate((mine, right, left, across)):
        at = pl.ds(pl.multiple_of(idx[i] * 256, 256), 256)
        total = dot(dq[...], w[0, at, :], NT)
        total = total + dot(low[:, :256], w[1, at, :], NT)
        total = total + dot(low[:, 256:], w[2, at, :], NT)
        out[...] = total.astype(out.dtype)


def sum_body(a, b, c, d, out):
    total = a[...] + b[...].astype(F32) + c[...].astype(F32) + d[...].astype(F32)
    out[...] = total.astype(BF16).reshape(out.shape)


def local_call(body, outs, idx, arrays, scratch=(), flops=0, name=None):
    vm = pl.BlockSpec(memory_space=pltpu.VMEM)
    specs = [vm] * len(arrays)
    args = list(arrays)
    if idx is not None:
        specs = [pl.BlockSpec(memory_space=pltpu.SMEM)] + specs
        args = [idx] + args
    size = sum(math.prod(a.shape) * a.dtype.itemsize for a in list(arrays) + list(outs))
    return pl.pallas_call(
        body,
        out_shape=tuple(outs),
        in_specs=specs,
        out_specs=(vm,) * len(outs),
        scratch_shapes=list(scratch),
        compiler_params=pltpu.CompilerParams(vmem_limit_bytes=24 * 1024 * 1024),
        cost_estimate=pl.CostEstimate(flops=flops, bytes_accessed=size, transcendentals=0),
        name=name,
    )(*args)


def shards(tokens, cotangent, w_qkv, w_out):
    S = jax.ShapeDtypeStruct
    n_x, n_t, n_h = (lax.axis_size(a) for a in ("tensor", "tm", "height"))
    x, t, h = (lax.axis_index(a) for a in ("tensor", "tm", "height"))
    idx = jnp.stack([x, (x + n_x - 1) % n_x, (x + 1) % n_x, (x + 2) % n_x]).astype(jnp.int32)
    idx_out = jnp.stack([x, (x + 1) % n_x, (x + n_x - 1) % n_x, (x + 2) % n_x]).astype(jnp.int32)
    frame_place = t * 2 + jnp.arange(4, dtype=jnp.int32) - 1
    row_place = h * 4 + jnp.arange(10, dtype=jnp.int32) - 3
    fine = ((frame_place >= 0) & (frame_place < 2 * n_t))[:, None]
    fine = fine & ((row_place >= 0) & (row_place < 4 * n_h))[None, :]
    valid = fine.astype(jnp.int32)

    def ring(array, by):
        return lax.ppermute(array, "tensor", [(i, (i + by) % n_x) for i in range(n_x)])

    def shift(array, dt, dh):
        pairs = [
            (i * n_h + j, ((i + dt) % n_t) * n_h + (j + dh) % n_h)
            for i in range(n_t)
            for j in range(n_h)
        ]
        return lax.ppermute(array, ("tm", "height"), pairs)

    tok = tokens.reshape(512, 256)
    flat = jnp.transpose(w_qkv, (1, 0, 2))
    t_parts = (ring(tok, 1), ring(tok, -1), ring(tok, 2))
    frame, rows, corner = (1, 4, 64, 512), (2, 3, 64, 512), (1, 3, 64, 512)
    q, own, f0, f1, lo, hi, c0lo, c0hi, c1lo, c1hi = local_call(
        project_body,
        (S((512, 256), BF16), S((2, 4, 64, 512), BF16), S(frame, BF16), S(frame, BF16),
         S(rows, BF16), S(rows, BF16), S(corner, BF16), S(corner, BF16), S(corner, BF16),
         S(corner, BF16)),
        idx, (tok, *t_parts, flat), flops=2 * 512 * 1024 * 768, name="project",
    )
    cot, _ = lax.optimization_barrier((cotangent.reshape(512, 256), t_parts[2]))
    c_parts = (ring(cot, 1), ring(cot, -1), ring(cot, 2))
    pieces = (
        shift(f1, 1, 0), shift(f0, -1, 0), shift(hi, 0, 1), shift(lo, 0, -1),
        shift(c1hi, 1, 1), shift(c1lo, 1, -1), shift(c0hi, -1, 1), shift(c0lo, -1, -1),
    )
    (b,) = local_call(
        back_body, (S((512, 256), BF16),), idx, (cot, *c_parts, w_out),
        flops=2 * 512 * 1024 * 256, name="back",
    )
    att, dq, g_own, g_tmb, g_tma, g_hb, g_ha, g_bb, g_ba, g_ab, g_aa = attend(
        valid, q, b, own, pieces
    )
    returned = (
        shift(g_tmb, -1, 0), shift(g_tma, 1, 0), shift(g_hb, 0, -1), shift(g_ha, 0, 1),
        shift(g_bb, -1, -1), shift(g_ba, -1, 1), shift(g_ab, 1, -1), shift(g_aa, 1, 1),
    )
    piece = S((512, 256), BF16)
    parts = (S((512, 256), F32), piece, piece, piece)
    m0, m1, m2, m3 = local_call(
        mixed_body, parts, idx_out, (att, w_out), flops=2 * 512 * 1024 * 256, name="mix",
    )
    out = (S((2, 4, 64, 256), BF16),)
    (mixed,) = local_call(sum_body, out, None, (m0, ring(m1, 1), ring(m2, -1), ring(m3, 2)), name="mixed_sum")
    g0, g1, g2, g3 = local_call(
        grad_body, parts, idx_out, (dq, g_own, *returned, flat),
        scratch=[pltpu.VMEM((2, 4, 64, 512), F32)], flops=2 * 512 * 1024 * 768, name="in_grad",
    )
    (in_grad,) = local_call(sum_body, out, None, (g0, ring(g1, 1), ring(g2, -1), ring(g3, 2)), name="in_grad_sum")
    return mixed, in_grad


def solution(mesh):
    in_specs = (
        P("tm", "height", None, "tensor"),
        P("tm", "height", None, "tensor"),
        P(None, None, "tensor"),
        P("tensor", None),
    )
    out_specs = (P("tm", "height", None, "tensor"), P("tm", "height", None, "tensor"))
    return jax.shard_map(shards, mesh=mesh, in_specs=in_specs, out_specs=out_specs, check_vma=False)
```

time: 441 us -> 166 us (0.38); the launches traced: 436 us -> 166 us
  local copies, waits for them, and re-layouts: 131 us -> 7.32 us
  waiting for transfers between devices: 154 us -> 76.4 us
  matrix products: 76.7 us -> 0 us
  other arithmetic: 31.3 us -> 0.24 us
  starting transfers between devices: 27.3 us -> 55.3 us
  Pallas kernels: 0 us -> 25.6 us
  between operations: 14.1 us -> 0.8 us
    dot_general x28 -> x0, matrix products: 76.7 us -> none  [the longest x4 23.7 us: visit(): lax.dot_general(query_tile, key_tile, contract_last, preferred_element_ty...]
    all_gather x2 -> x0, waiting for transfers between devices: 34.3 us -> none  [the longest x1 29.9 us: shards(): lax.all_gather(tokens, 'tensor', axis=3, tiled=True)]
    dot_general x8 -> x0, local copies, waits for them, and re-layouts: 33 us -> none  [the longest x4 21.1 us: visit(): lax.dot_general(probs_low, back_tile, contract_first, preferred_element_t...]
    ppermute x8 -> x28, starting transfers between devices: 27.1 us -> 55.3 us  [the longest x16 41.2 us: shift(): return lax.ppermute(array, ('tm', 'height'), pairs)]
    reduce_scatter x2 -> x0, waiting for transfers between devices: 28.2 us -> none  [the longest x1 28.2 us: shards(): lax.psum_scatter(in_terms, 'tensor', scatter_dimension=3, tiled=True)]
    pallas_call x0 -> x7, Pallas kernels: none -> 25.6 us  [the longest x1 18.1 us: attend(): pl.pallas_call(attend_body, out_shape=outs, in_specs=[pl.BlockSpec(memory...]
    while x137 -> x0, local copies, waits for them, and re-layouts: 24 us -> none
    convert_element_type x11 -> x1, other arithmetic: 22.9 us -> 0.07 us  [shards(): valid = fine.astype(jnp.int32)]
  transfers between devices with their start and end apart: 12 -> 28, of which waited for: 9 -> 13; matrix products, arithmetic and copies ran while one was open for 4% -> 0% of each run, Pallas kernels for 0% -> 3%
where the time goes in v1:
time: 166 us
  waiting for transfers between devices  76.4 us (46%)
  starting transfers between devices  55.3 us (33%)
  Pallas kernels  25.6 us (15%)
  local copies, waits for them, and re-layouts  7.32 us (4%)
    ppermute x16, waiting for transfers between devices, shift(): return lax.ppermute(array, ('tm', 'height'), pairs)  53.2 us
    ppermute x16, starting transfers between devices, shift(): return lax.ppermute(array, ('tm', 'height'), pairs)  41.2 us
    ppermute x12, waiting for transfers between devices, ring(): lax.ppermute(array, 'tensor', [(i, (i + by) % n_x) for i in range(n_x)])  23.2 us
    pallas_call x1, Pallas kernels, attend(): pl.pallas_call(attend_body, out_shape=outs, in_specs=[pl.BlockSpec(memory...  18.1 us
    ppermute x12, starting transfers between devices, ring(): lax.ppermute(array, 'tensor', [(i, (i + by) % n_x) for i in range(n_x)])  14.2 us
    pallas_call x6, Pallas kernels, local_call(): pl.pallas_call(body, out_shape=tuple(outs), in_specs=specs, out_specs=(vm...  7.45 us
    unnamed x34, local copies, waits for them, and re-layouts  7.32 us
  transfers between devices with their start and end apart: 28, of which 13 were waited for; matrix products, arithmetic and copies ran while one was open for 0% of the time, Pallas kernels for 3%

profile of v1, /device:TPU:22, one launch (start us, length us, event | category | flops | bytes accessed | tf_op | source)
XLA Modules:
  0.0 165.7 jit_solution(7988285622778087660)
XLA Ops:
  0.6 1.5 collective-permute-start.2
  2.1 3.2 %collective-permute-start = (bf16[512,256]{1,0:T(8,128)(2,1)}, bf16[512,256]{1,0:T(8,128)(2,1)S(1)}, u32[]{:S(2)}, u32[]{:S(2)}) collective-permute-start(bf16[512,256]{1,0:T(8,128)(2,1)} %bitcast.15), channel_id=1, source_target_pairs={{0,1},{1,2},{2,3},{3,0},{4,5},{5,6},{6,7},{7,4},{8,9},{9,10},{10,1... | collective-permute-start | bytes 786440 | tf_op jit(solution)/shard_map/ppermute | solution.py:264
  5.4 0.1 add_add_fusion.1.idx
  5.4 6.2 %collective-permute-done.2.x3 = bf16[512,256]{1,0:T(8,128)(2,1)S(1)} collective-permute-done((bf16[512,256]{1,0:T(8,128)(2,1)}, bf16[512,256]{1,0:T(8,128)(2,1)S(1)}, u32[]{:S(2)}, u32[]{:S(2)}) %collective-permute-start.2) | collective-permute-done | bytes 262176 | tf_op jit(solution)/shard_map/ppermute | solution.py:264
  11.7 4.4 %collective-permute-done.1.x2 = bf16[512,256]{1,0:T(8,128)(2,1)S(1)} collective-permute-done((bf16[512,256]{1,0:T(8,128)(2,1)}, bf16[512,256]{1,0:T(8,128)(2,1)S(1)}, u32[]{:S(2)}, u32[]{:S(2)}) %collective-permute-start.1) | collective-permute-done | bytes 262176 | tf_op jit(solution)/shard_map/ppermute | solution.py:264
  16.1 1.4 copy-done
  17.5 0.9 copy-done.4
  18.5 2.2 %project.1 = (bf16[512,256]{1,0:T(8,128)(2,1)S(1)}, bf16[2,4,64,512]{3,2,1,0:T(8,128)(2,1)S(1)}, bf16[1,4,64,512]{3,2,1,0:T(8,128)(2,1)S(1)}, bf16[1,4,64,512]{3...) custom-call(s32[4]{0:T(128)S(1)} %add_add_fusion.1.idx, ...), custom_call_target="tpu_custom_call" | custom-call | flops 805306368 | bytes 5505024 | tf_op jit(solution)/shard_map/project/pallas_call | solution.py:239
  20.7 0.7 copy-done.5
  21.4 0.7 copy-done.12
  22.1 0.8 copy-done.13
  22.9 0.7 copy-done.15
  23.6 2.9 %collective-permute-start.10 = (bf16[1,3,64,512]{3,2,1,0:T(8,128)(2,1)S(1)}, bf16[1,3,64,512]{3,2,1,0:T(8,128)(2,1)S(1)}, u32[]{:S(2)}, u32[]{:S(2)}) collective-permute-start(bf16[1,3,64,512]{3,2,1,0:T(8,128)(2,1)S(1)} %get-tuple-element.39), channel_id=1, source_target_pairs={{0,68},{4,72},{8,76},{12,80},{16,84},{20,88},{24,92},{28,96},{32,1... | collective-permute-start | bytes 589832 | tf_op jit(solution)/shard_map/ppermute | solution.py:272
  26.5 5.5 %collective-permute-start.11 = (bf16[1,3,64,512]{3,2,1,0:T(8,128)(2,1)}, bf16[1,3,64,512]{3,2,1,0:T(8,128)(2,1)S(1)}, u32[]{:S(2)}, u32[]{:S(2)}) collective-permute-start(bf16[1,3,64,512]{3,2,1,0:T(8,128)(2,1)} %get-tuple-element.40), channel_id=1, source_target_pairs={{0,124},{4,64},{8,68},{12,72},{16,76},{20,80},{24,84},{28,88},{32,... | collective-permute-start | bytes 589832 | tf_op jit(solution)/shard_map/ppermute | solution.py:272
  32.0 1.5 collective-permute-start.5
  33.5 5.8 %collective-permute-done.10.bb = bf16[1,3,64,512]{3,2,1,0:T(8,128)(2,1)S(1)} collective-permute-done((bf16[1,3,64,512]{3,2,1,0:T(8,128)(2,1)S(1)}, bf16[1,3,64,512]{3,2,1,0:T(8,128)(2,1)S(1)}, u32[]{:S(2)}, u32[]{:S(2)}) %collective-permute-start.10) | collective-permute-done | bytes 196640 | tf_op jit(solution)/shard_map/ppermute | solution.py:272
  39.3 0.7 copy-done.6
  40.0 0.3 collective-permute-start.3
  40.3 4.2 %collective-permute-done.11.ba = bf16[1,3,64,512]{3,2,1,0:T(8,128)(2,1)S(1)} collective-permute-done((bf16[1,3,64,512]{3,2,1,0:T(8,128)(2,1)}, bf16[1,3,64,512]{3,2,1,0:T(8,128)(2,1)S(1)}, u32[]{:S(2)}, u32[]{:S(2)}) %collective-permute-start.11) | collective-permute-done | bytes 196640 | tf_op jit(solution)/shard_map/ppermute | solution.py:272
  44.4 0.7 copy-done.8
  45.1 2.5 %collective-permute-start.8 = (bf16[2,3,64,512]{3,2,1,0:T(8,128)(2,1)S(1)}, bf16[2,3,64,512]{3,2,1,0:T(8,128)(2,1)S(1)}, u32[]{:S(2)}, u32[]{:S(2)}) collective-permute-start(bf16[2,3,64,512]{3,2,1,0:T(8,128)(2,1)S(1)} %get-tuple-element.37), channel_id=1, source_target_pairs={{0,4},{4,8},{8,12},{12,16},{16,20},{20,24},{24,28},{28,32},{32,36}... | collective-permute-start | bytes 1179656 | tf_op jit(solution)/shard_map/ppermute | solution.py:272
  47.7 0.7 copy-done.10
  48.4 0.5 collective-permute-start.9
  48.9 0.0 copy-start.16
  48.9 0.0 collective-permute-done.5.x3
  48.9 3.7 %collective-permute-start.6 = (bf16[1,4,64,512]{3,2,1,0:T(8,128)(2,1)}, bf16[1,4,64,512]{3,2,1,0:T(8,128)(2,1)S(1)}, u32[]{:S(2)}, u32[]{:S(2)}) collective-permute-start(bf16[1,4,64,512]{3,2,1,0:T(8,128)(2,1)} %copy-done.5), channel_id=1, source_target_pairs={{0,64},{4,68},{8,72},{12,76},{16,80},{20,84},{24,88},{28,92},{32,9... | collective-permute-start | bytes 786440 | tf_op jit(solution)/shard_map/ppermute | solution.py:272
  52.6 0.0 collective-permute-done.4.x2
  52.6 1.0 collective-permute-start.7
  53.6 2.2 %collective-permute-start.13 = (bf16[1,3,64,512]{3,2,1,0:T(8,128)(2,1)}, bf16[1,3,64,512]{3,2,1,0:T(8,128)(2,1)S(1)}, u32[]{:S(2)}, u32[]{:S(2)}) collective-permute-start(bf16[1,3,64,512]{3,2,1,0:T(8,128)(2,1)} %copy-done.12), channel_id=1, source_target_pairs={{0,252},{4,192},{8,196},{12,200},{16,204},{20,208},{24,212},{28,21... | collective-permute-start | bytes 589832 | tf_op jit(solution)/shard_map/ppermute | solution.py:272
  55.8 0.1 and_convert_fusion.valid
  55.9 1.0 back.1.b
  56.9 6.8 %collective-permute-done.13.aa = bf16[1,3,64,512]{3,2,1,0:T(8,128)(2,1)S(1)} collective-permute-done((bf16[1,3,64,512]{3,2,1,0:T(8,128)(2,1)}, bf16[1,3,64,512]{3,2,1,0:T(8,128)(2,1)S(1)}, u32[]{:S(2)}, u32[]{:S(2)}) %collective-permute-start.13) | collective-permute-done | bytes 196640 | tf_op jit(solution)/shard_map/ppermute | solution.py:272
  63.7 9.4 %collective-permute-done.6.tmb = bf16[1,4,64,512]{3,2,1,0:T(8,128)(2,1)S(1)} collective-permute-done((bf16[1,4,64,512]{3,2,1,0:T(8,128)(2,1)}, bf16[1,4,64,512]{3,2,1,0:T(8,128)(2,1)S(1)}, u32[]{:S(2)}, u32[]{:S(2)}) %collective-permute-start.6) | collective-permute-done | bytes 262176 | tf_op jit(solution)/shard_map/ppermute | solution.py:272
  73.2 0.0 collective-permute-done.7.tma
  73.2 0.0 collective-permute-done.8.hb
  73.2 0.0 copy-start.1
  73.2 18.1 %attend.1 = (bf16[512,256]{1,0:T(8,128)(2,1)S(1)}, bf16[512,256]{1,0:T(8,128)(2,1)S(1)}, f32[2,4,64,512]{3,2,1,0:T(8,128)S(1)}, bf16[1,4,64,512]{3,2,1,0:T(8,128...) custom-call(s32[4,10]{1,0:T(4,128)S(1)} %and_convert_fusion.valid, ...), custom_call_target="tpu_custom_call" | custom-call | flops 8455716864 | bytes 12582912 | tf_op jit(solution)/shard_map/attend/pallas_call | solution.py:153
  91.4 3.7 %collective-permute-start.21 = (bf16[1,3,64,512]{3,2,1,0:T(8,128)(2,1)S(1)}, bf16[1,3,64,512]{3,2,1,0:T(8,128)(2,1)S(1)}, u32[]{:S(2)}, u32[]{:S(2)}) collective-permute-start(bf16[1,3,64,512]{3,2,1,0:T(8,128)(2,1)S(1)} %get-tuple-element.54), channel_id=1, source_target_pairs={{0,252},{4,192},{8,196},{12,200},{16,204},{20,208},{24,212},{28,21... | collective-permute-start | bytes 589832 | tf_op jit(solution)/shard_map/ppermute | solution.py:272
  95.0 5.6 %collective-permute-start.22 = (bf16[1,3,64,512]{3,2,1,0:T(8,128)(2,1)S(1)}, bf16[1,3,64,512]{3,2,1,0:T(8,128)(2,1)S(1)}, u32[]{:S(2)}, u32[]{:S(2)}) collective-permute-start(bf16[1,3,64,512]{3,2,1,0:T(8,128)(2,1)S(1)} %get-tuple-element.55), channel_id=1, source_target_pairs={{0,196},{4,200},{8,204},{12,208},{16,212},{20,216},{24,220},{28,22... | collective-permute-start | bytes 589832 | tf_op jit(solution)/shard_map/ppermute | solution.py:272
  100.6 0.0 collective-permute-start.23
  100.6 3.1 %collective-permute-start.19 = (bf16[2,3,64,512]{3,2,1,0:T(8,128)(2,1)S(1)}, bf16[2,3,64,512]{3,2,1,0:T(8,128)(2,1)S(1)}, u32[]{:S(2)}, u32[]{:S(2)}) collective-permute-start(bf16[2,3,64,512]{3,2,1,0:T(8,128)(2,1)S(1)} %get-tuple-element.52), channel_id=1, source_target_pairs={{0,60},{4,0},{8,4},{12,8},{16,12},{20,16},{24,20},{28,24},{32,28},... | collective-permute-start | bytes 1179656 | tf_op jit(solution)/shard_map/ppermute | solution.py:272
  103.7 0.0 collective-permute-start.20
  103.7 8.4 %collective-permute-done.21.r5 = bf16[1,3,64,512]{3,2,1,0:T(8,128)(2,1)S(1)} collective-permute-done((bf16[1,3,64,512]{3,2,1,0:T(8,128)(2,1)S(1)}, bf16[1,3,64,512]{3,2,1,0:T(8,128)(2,1)S(1)}, u32[]{:S(2)}, u32[]{:S(2)}) %collective-permute-start.21) | collective-permute-done | bytes 196640 | tf_op jit(solution)/shard_map/ppermute | solution.py:272
  112.2 1.3 collective-permute-start.24
  113.5 0.0 collective-permute-done.22.r6
  113.5 8.5 %collective-permute-start.17 = (bf16[1,4,64,512]{3,2,1,0:T(8,128)(2,1)S(1)}, bf16[1,4,64,512]{3,2,1,0:T(8,128)(2,1)S(1)}, u32[]{:S(2)}, u32[]{:S(2)}) collective-permute-start(bf16[1,4,64,512]{3,2,1,0:T(8,128)(2,1)S(1)} %get-tuple-element.50), channel_id=1, source_target_pairs={{0,192},{4,196},{8,200},{12,204},{16,208},{20,212},{24,216},{28,22... | collective-permute-start | bytes 786440 | tf_op jit(solution)/shard_map/ppermute | solution.py:272
  122.0 0.0 collective-permute-done.23.r7
  122.0 0.7 collective-permute-start.18
  122.7 0.1 add_add_fusion.idx
  122.8 1.0 mix.1
  123.8 6.7 %collective-permute-done.24.r8 = bf16[1,3,64,512]{3,2,1,0:T(8,128)(2,1)S(1)} collective-permute-done((bf16[1,3,64,512]{3,2,1,0:T(8,128)(2,1)S(1)}, bf16[1,3,64,512]{3,2,1,0:T(8,128)(2,1)S(1)}, u32[]{:S(2)}, u32[]{:S(2)}) %collective-permute-start.24) | collective-permute-done | bytes 196640 | tf_op jit(solution)/shard_map/ppermute | solution.py:272
  130.5 0.0 collective-permute-start.14
  130.5 2.0 %collective-permute-start.15 = (bf16[512,256]{1,0:T(8,128)(2,1)S(1)}, bf16[512,256]{1,0:T(8,128)(2,1)S(1)}, u32[]{:S(2)}, u32[]{:S(2)}) collective-permute-start(bf16[512,256]{1,0:T(8,128)(2,1)S(1)} %get-tuple-element.46), channel_id=1, source_target_pairs={{0,3},{1,0},{2,1},{3,2},{4,7},{5,4},{6,5},{7,6},{8,11},{9,8},{10,9... | collective-permute-start | bytes 786440 | tf_op jit(solution)/shard_map/ppermute | solution.py:264
  132.5 11.8 %collective-permute-done.18.r2 = bf16[1,4,64,512]{3,2,1,0:T(8,128)(2,1)S(1)} collective-permute-done((bf16[1,4,64,512]{3,2,1,0:T(8,128)(2,1)S(1)}, bf16[1,4,64,512]{3,2,1,0:T(8,128)(2,1)S(1)}, u32[]{:S(2)}, u32[]{:S(2)}) %collective-permute-start.18) | collective-permute-done | bytes 262176 | tf_op jit(solution)/shard_map/ppermute | solution.py:272
  144.3 1.4 collective-permute-start.16
  145.8 1.6 in_grad.1
  147.3 2.1 %collective-permute-start.25 = (bf16[512,256]{1,0:T(8,128)(2,1)S(1)}, bf16[512,256]{1,0:T(8,128)(2,1)S(1)}, u32[]{:S(2)}, u32[]{:S(2)}) collective-permute-start(bf16[512,256]{1,0:T(8,128)(2,1)S(1)} %get-tuple-element.59), channel_id=1, source_target_pairs={{0,1},{1,2},{2,3},{3,0},{4,5},{5,6},{6,7},{7,4},{8,9},{9,10},{10,1... | collective-permute-start | bytes 786440 | tf_op jit(solution)/shard_map/ppermute | solution.py:264
  149.5 2.1 %collective-permute-start.27 = (bf16[512,256]{1,0:T(8,128)(2,1)S(1)}, bf16[512,256]{1,0:T(8,128)(2,1)S(1)}, u32[]{:S(2)}, u32[]{:S(2)}) collective-permute-start(bf16[512,256]{1,0:T(8,128)(2,1)S(1)} %get-tuple-element.61), channel_id=1, source_target_pairs={{0,2},{1,3},{2,0},{3,1},{4,6},{5,7},{6,4},{7,5},{8,10},{9,11},{10,... | collective-permute-start | bytes 786440 | tf_op jit(solution)/shard_map/ppermute | solution.py:264
  151.6 3.5 %collective-permute-done.16.d = bf16[512,256]{1,0:T(8,128)(2,1)S(1)} collective-permute-done((bf16[512,256]{1,0:T(8,128)(2,1)S(1)}, bf16[512,256]{1,0:T(8,128)(2,1)S(1)}, u32[]{:S(2)}, u32[]{:S(2)}) %collective-permute-start.16) | collective-permute-done | bytes 262176 | tf_op jit(solution)/shard_map/ppermute | solution.py:264
  155.1 0.8 mixed_sum.1
  155.9 2.6 %collective-permute-done.25.b = bf16[512,256]{1,0:T(8,128)(2,1)S(1)} collective-permute-done((bf16[512,256]{1,0:T(8,128)(2,1)S(1)}, bf16[512,256]{1,0:T(8,128)(2,1)S(1)}, u32[]{:S(2)}, u32[]{:S(2)}) %collective-permute-start.25) | collective-permute-done | bytes 262176 | tf_op jit(solution)/shard_map/ppermute | solution.py:264
  158.5 2.2 %collective-permute-done.26.c = bf16[512,256]{1,0:T(8,128)(2,1)S(1)} collective-permute-done((bf16[512,256]{1,0:T(8,128)(2,1)S(1)}, bf16[512,256]{1,0:T(8,128)(2,1)S(1)}, u32[]{:S(2)}, u32[]{:S(2)}) %collective-permute-start.26) | collective-permute-done | bytes 262176 | tf_op jit(solution)/shard_map/ppermute | solution.py:264
  160.8 4.1 %collective-permute-done.27.d = bf16[512,256]{1,0:T(8,128)(2,1)S(1)} collective-permute-done((bf16[512,256]{1,0:T(8,128)(2,1)S(1)}, bf16[512,256]{1,0:T(8,128)(2,1)S(1)}, u32[]{:S(2)}, u32[]{:S(2)}) %collective-permute-start.27) | collective-permute-done | bytes 262176 | tf_op jit(solution)/shard_map/ppermute | solution.py:264
  164.9 0.8 in_grad_sum.1
  (38 shorter events, 0.1 us)
Async XLA Ops:
  0.6 11.0 %collective-permute-start.2 = (bf16[512,256]{1,0:T(8,128)(2,1)}, bf16[512,256]{1,0:T(8,128)(2,1)S(1)}, u32[]{:S(2)}, u32[]{:S(2)}) collective-permute-start(bf16[512,256]{1,0:T(8,128)(2,1)} %bitcast.13), channel_id=1, source_target_pairs={{0,2},{1,3},{2,0},{3,1},{4,6},{5,7},{6,4},{7,5},{8,10},{9,11},{10,... | collective-permute-start | bytes 786440 | tf_op jit(solution)/shard_map/ppermute | solution.py:264
  2.1 14.0 %collective-permute-start.1 = (bf16[512,256]{1,0:T(8,128)(2,1)}, bf16[512,256]{1,0:T(8,128)(2,1)S(1)}, u32[]{:S(2)}, u32[]{:S(2)}) collective-permute-start(bf16[512,256]{1,0:T(8,128)(2,1)} %bitcast.14), channel_id=1, source_target_pairs={{0,3},{1,0},{2,1},{3,2},{4,7},{5,4},{6,5},{7,6},{8,11},{9,8},{10,9... | collective-permute-start | bytes 786440 | tf_op jit(solution)/shard_map/ppermute | solution.py:264
  2.1 14.0 %collective-permute-start = (bf16[512,256]{1,0:T(8,128)(2,1)}, bf16[512,256]{1,0:T(8,128)(2,1)S(1)}, u32[]{:S(2)}, u32[]{:S(2)}) collective-permute-start(bf16[512,256]{1,0:T(8,128)(2,1)} %bitcast.15), channel_id=1, source_target_pairs={{0,1},{1,2},{2,3},{3,0},{4,5},{5,6},{6,7},{7,4},{8,9},{9,10},{10,1... | collective-permute-start | bytes 786440 | tf_op jit(solution)/shard_map/ppermute | solution.py:264
  16.1 1.4 copy-start
  17.5 0.9 copy-start.4
  18.5 13.5 %copy-start.3 = (bf16[2,4,64,256]{3,2,1,0:T(8,128)(2,1)S(1)}, bf16[2,4,64,256]{3,2,1,0:T(8,128)(2,1)}, u32[]{:S(2)}) copy-start(bf16[2,4,64,256]{3,2,1,0:T(8,128)(2,1)} %param.5) | copy-start | bytes 786436
  18.5 37.5 %copy-start.2 = (bf16[256,1024]{1,0:T(8,128)(2,1)S(1)}, bf16[256,1024]{1,0:T(8,128)(2,1)}, u32[]{:S(2)}) copy-start(bf16[256,1024]{1,0:T(8,128)(2,1)} %w.3) | copy-start | bytes 1572868
  20.7 0.7 copy-start.5
  21.4 0.7 copy-start.12
  22.1 0.8 copy-start.13
  22.9 0.7 copy-start.15
  23.6 15.7 %collective-permute-start.10 = (bf16[1,3,64,512]{3,2,1,0:T(8,128)(2,1)S(1)}, bf16[1,3,64,512]{3,2,1,0:T(8,128)(2,1)S(1)}, u32[]{:S(2)}, u32[]{:S(2)}) collective-permute-start(bf16[1,3,64,512]{3,2,1,0:T(8,128)(2,1)S(1)} %get-tuple-element.39), channel_id=1, source_target_pairs={{0,68},{4,72},{8,76},{12,80},{16,84},{20,88},{24,92},{28,96},{32,1... | collective-permute-start | bytes 589832 | tf_op jit(solution)/shard_map/ppermute | solution.py:272
  26.5 18.0 %collective-permute-start.11 = (bf16[1,3,64,512]{3,2,1,0:T(8,128)(2,1)}, bf16[1,3,64,512]{3,2,1,0:T(8,128)(2,1)S(1)}, u32[]{:S(2)}, u32[]{:S(2)}) collective-permute-start(bf16[1,3,64,512]{3,2,1,0:T(8,128)(2,1)} %get-tuple-element.40), channel_id=1, source_target_pairs={{0,124},{4,64},{8,68},{12,72},{16,76},{20,80},{24,84},{28,88},{32,... | collective-permute-start | bytes 589832 | tf_op jit(solution)/shard_map/ppermute | solution.py:272
  32.0 15.7 %collective-permute-start.12 = (bf16[1,3,64,512]{3,2,1,0:T(8,128)(2,1)S(1)}, bf16[1,3,64,512]{3,2,1,0:T(8,128)(2,1)S(1)}, u32[]{:S(2)}, u32[]{:S(2)}) collective-permute-start(bf16[1,3,64,512]{3,2,1,0:T(8,128)(2,1)S(1)} %get-tuple-element.41), channel_id=1, source_target_pairs={{0,196},{4,200},{8,204},{12,208},{16,212},{20,216},{24,220},{28,22... | collective-permute-start | bytes 589832 | tf_op jit(solution)/shard_map/ppermute | solution.py:272
  32.0 16.9 %collective-permute-start.5 = (bf16[512,256]{1,0:T(8,128)(2,1)S(1)}, bf16[512,256]{1,0:T(8,128)(2,1)S(1)}, u32[]{:S(2)}, u32[]{:S(2)}) collective-permute-start(bf16[512,256]{1,0:T(8,128)(2,1)S(1)} %bitcast.9), channel_id=1, source_target_pairs={{0,2},{1,3},{2,0},{3,1},{4,6},{5,7},{6,4},{7,5},{8,10},{9,11},{10,... | collective-permute-start | bytes 786440 | tf_op jit(solution)/shard_map/ppermute | solution.py:264
  33.4 19.1 %collective-permute-start.4 = (bf16[512,256]{1,0:T(8,128)(2,1)S(1)}, bf16[512,256]{1,0:T(8,128)(2,1)S(1)}, u32[]{:S(2)}, u32[]{:S(2)}) collective-permute-start(bf16[512,256]{1,0:T(8,128)(2,1)S(1)} %bitcast.10), channel_id=1, source_target_pairs={{0,3},{1,0},{2,1},{3,2},{4,7},{5,4},{6,5},{7,6},{8,11},{9,8},{10,9... | collective-permute-start | bytes 786440 | tf_op jit(solution)/shard_map/ppermute | solution.py:264
  39.3 0.7 copy-start.6
  40.0 13.7 %collective-permute-start.3 = (bf16[512,256]{1,0:T(8,128)(2,1)S(1)}, bf16[512,256]{1,0:T(8,128)(2,1)S(1)}, u32[]{:S(2)}, u32[]{:S(2)}) collective-permute-start(bf16[512,256]{1,0:T(8,128)(2,1)S(1)} %bitcast.11), channel_id=1, source_target_pairs={{0,1},{1,2},{2,3},{3,0},{4,5},{5,6},{6,7},{7,4},{8,9},{9,10},{10,1... | collective-permute-start | bytes 786440 | tf_op jit(solution)/shard_map/ppermute | solution.py:264
  44.4 0.7 copy-start.8
  45.1 28.0 %collective-permute-start.8 = (bf16[2,3,64,512]{3,2,1,0:T(8,128)(2,1)S(1)}, bf16[2,3,64,512]{3,2,1,0:T(8,128)(2,1)S(1)}, u32[]{:S(2)}, u32[]{:S(2)}) collective-permute-start(bf16[2,3,64,512]{3,2,1,0:T(8,128)(2,1)S(1)} %get-tuple-element.37), channel_id=1, source_target_pairs={{0,4},{4,8},{8,12},{12,16},{16,20},{20,24},{24,28},{28,32},{32,36}... | collective-permute-start | bytes 1179656 | tf_op jit(solution)/shard_map/ppermute | solution.py:272
  47.7 0.7 copy-start.10
  48.4 24.8 %collective-permute-start.9 = (bf16[2,3,64,512]{3,2,1,0:T(8,128)(2,1)S(1)}, bf16[2,3,64,512]{3,2,1,0:T(8,128)(2,1)S(1)}, u32[]{:S(2)}, u32[]{:S(2)}) collective-permute-start(bf16[2,3,64,512]{3,2,1,0:T(8,128)(2,1)S(1)} %get-tuple-element.38), channel_id=1, source_target_pairs={{0,60},{4,0},{8,4},{12,8},{16,12},{20,16},{24,20},{28,24},{32,28},... | collective-permute-start | bytes 1179656 | tf_op jit(solution)/shard_map/ppermute | solution.py:272
  48.9 24.3 %copy-start.7 = (bf16[1,3,64,512]{3,2,1,0:T(8,128)(2,1)S(1)}, bf16[1,3,64,512]{3,2,1,0:T(8,128)(2,1)}, u32[]{:S(2)}) copy-start(bf16[1,3,64,512]{3,2,1,0:T(8,128)(2,1)} %copy-done.6) | copy-start | bytes 589828
  48.9 24.3 %copy-start.9 = (bf16[1,3,64,512]{3,2,1,0:T(8,128)(2,1)S(1)}, bf16[1,3,64,512]{3,2,1,0:T(8,128)(2,1)}, u32[]{:S(2)}) copy-start(bf16[1,3,64,512]{3,2,1,0:T(8,128)(2,1)} %copy-done.8) | copy-start | bytes 589828
  48.9 24.3 %copy-start.11 = (bf16[1,3,64,512]{3,2,1,0:T(8,128)(2,1)S(1)}, bf16[1,3,64,512]{3,2,1,0:T(8,128)(2,1)}, u32[]{:S(2)}) copy-start(bf16[1,3,64,512]{3,2,1,0:T(8,128)(2,1)} %copy-done.10) | copy-start | bytes 589828
  48.9 24.3 %copy-start.14 = (bf16[2,4,64,512]{3,2,1,0:T(8,128)(2,1)S(1)}, bf16[2,4,64,512]{3,2,1,0:T(8,128)(2,1)}, u32[]{:S(2)}) copy-start(bf16[2,4,64,512]{3,2,1,0:T(8,128)(2,1)} %copy-done.13) | copy-start | bytes 1572868
  48.9 24.3 %copy-start.16 = (bf16[512,256]{1,0:T(8,128)(2,1)S(1)}, bf16[512,256]{1,0:T(8,128)(2,1)}, u32[]{:S(2)}) copy-start(bf16[512,256]{1,0:T(8,128)(2,1)} %copy-done.15) | copy-start | bytes 786436
  48.9 24.2 %collective-permute-start.6 = (bf16[1,4,64,512]{3,2,1,0:T(8,128)(2,1)}, bf16[1,4,64,512]{3,2,1,0:T(8,128)(2,1)S(1)}, u32[]{:S(2)}, u32[]{:S(2)}) collective-permute-start(bf16[1,4,64,512]{3,2,1,0:T(8,128)(2,1)} %copy-done.5), channel_id=1, source_target_pairs={{0,64},{4,68},{8,72},{12,76},{16,80},{20,84},{24,88},{28,92},{32,9... | collective-permute-start | bytes 786440 | tf_op jit(solution)/shard_map/ppermute | solution.py:272
  52.6 20.6 %collective-permute-start.7 = (bf16[1,4,64,512]{3,2,1,0:T(8,128)(2,1)S(1)}, bf16[1,4,64,512]{3,2,1,0:T(8,128)(2,1)S(1)}, u32[]{:S(2)}, u32[]{:S(2)}) collective-permute-start(bf16[1,4,64,512]{3,2,1,0:T(8,128)(2,1)S(1)} %get-tuple-element.36), channel_id=1, source_target_pairs={{0,192},{4,196},{8,200},{12,204},{16,208},{20,212},{24,216},{28,22... | collective-permute-start | bytes 786440 | tf_op jit(solution)/shard_map/ppermute | solution.py:272
  53.6 10.1 %collective-permute-start.13 = (bf16[1,3,64,512]{3,2,1,0:T(8,128)(2,1)}, bf16[1,3,64,512]{3,2,1,0:T(8,128)(2,1)S(1)}, u32[]{:S(2)}, u32[]{:S(2)}) collective-permute-start(bf16[1,3,64,512]{3,2,1,0:T(8,128)(2,1)} %copy-done.12), channel_id=1, source_target_pairs={{0,252},{4,192},{8,196},{12,200},{16,204},{20,208},{24,212},{28,21... | collective-permute-start | bytes 589832 | tf_op jit(solution)/shard_map/ppermute | solution.py:272
  73.2 72.5 %copy-start.1 = (bf16[1024,3,256]{2,0,1:T(8,128)(2,1)S(1)}, bf16[1024,3,256]{2,0,1:T(8,128)(2,1)}, u32[]{:S(2)}) copy-start(bf16[1024,3,256]{2,0,1:T(8,128)(2,1)} %param.6) | copy-start | bytes 4718596
  91.4 20.8 %collective-permute-start.21 = (bf16[1,3,64,512]{3,2,1,0:T(8,128)(2,1)S(1)}, bf16[1,3,64,512]{3,2,1,0:T(8,128)(2,1)S(1)}, u32[]{:S(2)}, u32[]{:S(2)}) collective-permute-start(bf16[1,3,64,512]{3,2,1,0:T(8,128)(2,1)S(1)} %get-tuple-element.54), channel_id=1, source_target_pairs={{0,252},{4,192},{8,196},{12,200},{16,204},{20,208},{24,212},{28,21... | collective-permute-start | bytes 589832 | tf_op jit(solution)/shard_map/ppermute | solution.py:272
  95.0 18.4 %collective-permute-start.22 = (bf16[1,3,64,512]{3,2,1,0:T(8,128)(2,1)S(1)}, bf16[1,3,64,512]{3,2,1,0:T(8,128)(2,1)S(1)}, u32[]{:S(2)}, u32[]{:S(2)}) collective-permute-start(bf16[1,3,64,512]{3,2,1,0:T(8,128)(2,1)S(1)} %get-tuple-element.55), channel_id=1, source_target_pairs={{0,196},{4,200},{8,204},{12,208},{16,212},{20,216},{24,220},{28,22... | collective-permute-start | bytes 589832 | tf_op jit(solution)/shard_map/ppermute | solution.py:272
  100.6 21.4 %collective-permute-start.23 = (bf16[1,3,64,512]{3,2,1,0:T(8,128)(2,1)S(1)}, bf16[1,3,64,512]{3,2,1,0:T(8,128)(2,1)S(1)}, u32[]{:S(2)}, u32[]{:S(2)}) collective-permute-start(bf16[1,3,64,512]{3,2,1,0:T(8,128)(2,1)S(1)} %get-tuple-element.56), channel_id=1, source_target_pairs={{0,124},{4,64},{8,68},{12,72},{16,76},{20,80},{24,84},{28,88},{32,... | collective-permute-start | bytes 589832 | tf_op jit(solution)/shard_map/ppermute | solution.py:272
  100.6 45.1 %collective-permute-start.19 = (bf16[2,3,64,512]{3,2,1,0:T(8,128)(2,1)S(1)}, bf16[2,3,64,512]{3,2,1,0:T(8,128)(2,1)S(1)}, u32[]{:S(2)}, u32[]{:S(2)}) collective-permute-start(bf16[2,3,64,512]{3,2,1,0:T(8,128)(2,1)S(1)} %get-tuple-element.52), channel_id=1, source_target_pairs={{0,60},{4,0},{8,4},{12,8},{16,12},{20,16},{24,20},{28,24},{32,28},... | collective-permute-start | bytes 1179656 | tf_op jit(solution)/shard_map/ppermute | solution.py:272
  103.7 42.0 %collective-permute-start.20 = (bf16[2,3,64,512]{3,2,1,0:T(8,128)(2,1)S(1)}, bf16[2,3,64,512]{3,2,1,0:T(8,128)(2,1)S(1)}, u32[]{:S(2)}, u32[]{:S(2)}) collective-permute-start(bf16[2,3,64,512]{3,2,1,0:T(8,128)(2,1)S(1)} %get-tuple-element.53), channel_id=1, source_target_pairs={{0,4},{4,8},{8,12},{12,16},{16,20},{20,24},{24,28},{28,32},{32,36}... | collective-permute-start | bytes 1179656 | tf_op jit(solution)/shard_map/ppermute | solution.py:272
  112.2 18.3 %collective-permute-start.24 = (bf16[1,3,64,512]{3,2,1,0:T(8,128)(2,1)S(1)}, bf16[1,3,64,512]{3,2,1,0:T(8,128)(2,1)S(1)}, u32[]{:S(2)}, u32[]{:S(2)}) collective-permute-start(bf16[1,3,64,512]{3,2,1,0:T(8,128)(2,1)S(1)} %get-tuple-element.57), channel_id=1, source_target_pairs={{0,68},{4,72},{8,76},{12,80},{16,84},{20,88},{24,92},{28,96},{32,1... | collective-permute-start | bytes 589832 | tf_op jit(solution)/shard_map/ppermute | solution.py:272
  113.5 17.0 %collective-permute-start.17 = (bf16[1,4,64,512]{3,2,1,0:T(8,128)(2,1)S(1)}, bf16[1,4,64,512]{3,2,1,0:T(8,128)(2,1)S(1)}, u32[]{:S(2)}, u32[]{:S(2)}) collective-permute-start(bf16[1,4,64,512]{3,2,1,0:T(8,128)(2,1)S(1)} %get-tuple-element.50), channel_id=1, source_target_pairs={{0,192},{4,196},{8,200},{12,204},{16,208},{20,212},{24,216},{28,22... | collective-permute-start | bytes 786440 | tf_op jit(solution)/shard_map/ppermute | solution.py:272
  122.0 22.3 %collective-permute-start.18 = (bf16[1,4,64,512]{3,2,1,0:T(8,128)(2,1)S(1)}, bf16[1,4,64,512]{3,2,1,0:T(8,128)(2,1)S(1)}, u32[]{:S(2)}, u32[]{:S(2)}) collective-permute-start(bf16[1,4,64,512]{3,2,1,0:T(8,128)(2,1)S(1)} %get-tuple-element.51), channel_id=1, source_target_pairs={{0,64},{4,68},{8,72},{12,76},{16,80},{20,84},{24,88},{28,92},{32,9... | collective-permute-start | bytes 786440 | tf_op jit(solution)/shard_map/ppermute | solution.py:272
  130.5 19.0 %collective-permute-start.14 = (bf16[512,256]{1,0:T(8,128)(2,1)S(1)}, bf16[512,256]{1,0:T(8,128)(2,1)S(1)}, u32[]{:S(2)}, u32[]{:S(2)}) collective-permute-start(bf16[512,256]{1,0:T(8,128)(2,1)S(1)} %get-tuple-element.45), channel_id=1, source_target_pairs={{0,1},{1,2},{2,3},{3,0},{4,5},{5,6},{6,7},{7,4},{8,9},{9,10},{10,1... | collective-permute-start | bytes 786440 | tf_op jit(solution)/shard_map/ppermute | solution.py:264
  130.5 21.1 %collective-permute-start.15 = (bf16[512,256]{1,0:T(8,128)(2,1)S(1)}, bf16[512,256]{1,0:T(8,128)(2,1)S(1)}, u32[]{:S(2)}, u32[]{:S(2)}) collective-permute-start(bf16[512,256]{1,0:T(8,128)(2,1)S(1)} %get-tuple-element.46), channel_id=1, source_target_pairs={{0,3},{1,0},{2,1},{3,2},{4,7},{5,4},{6,5},{7,6},{8,11},{9,8},{10,9... | collective-permute-start | bytes 786440 | tf_op jit(solution)/shard_map/ppermute | solution.py:264
  144.3 10.7 %collective-permute-start.16 = (bf16[512,256]{1,0:T(8,128)(2,1)S(1)}, bf16[512,256]{1,0:T(8,128)(2,1)S(1)}, u32[]{:S(2)}, u32[]{:S(2)}) collective-permute-start(bf16[512,256]{1,0:T(8,128)(2,1)S(1)} %get-tuple-element.47), channel_id=1, source_target_pairs={{0,2},{1,3},{2,0},{3,1},{4,6},{5,7},{6,4},{7,5},{8,10},{9,11},{10,... | collective-permute-start | bytes 786440 | tf_op jit(solution)/shard_map/ppermute | solution.py:264
  147.3 11.2 %collective-permute-start.25 = (bf16[512,256]{1,0:T(8,128)(2,1)S(1)}, bf16[512,256]{1,0:T(8,128)(2,1)S(1)}, u32[]{:S(2)}, u32[]{:S(2)}) collective-permute-start(bf16[512,256]{1,0:T(8,128)(2,1)S(1)} %get-tuple-element.59), channel_id=1, source_target_pairs={{0,1},{1,2},{2,3},{3,0},{4,5},{5,6},{6,7},{7,4},{8,9},{9,10},{10,1... | collective-permute-start | bytes 786440 | tf_op jit(solution)/shard_map/ppermute | solution.py:264
  149.5 11.3 %collective-permute-start.26 = (bf16[512,256]{1,0:T(8,128)(2,1)S(1)}, bf16[512,256]{1,0:T(8,128)(2,1)S(1)}, u32[]{:S(2)}, u32[]{:S(2)}) collective-permute-start(bf16[512,256]{1,0:T(8,128)(2,1)S(1)} %get-tuple-element.60), channel_id=1, source_target_pairs={{0,3},{1,0},{2,1},{3,2},{4,7},{5,4},{6,5},{7,6},{8,11},{9,8},{10,9... | collective-permute-start | bytes 786440 | tf_op jit(solution)/shard_map/ppermute | solution.py:264
  149.5 15.4 %collective-permute-start.27 = (bf16[512,256]{1,0:T(8,128)(2,1)S(1)}, bf16[512,256]{1,0:T(8,128)(2,1)S(1)}, u32[]{:S(2)}, u32[]{:S(2)}) collective-permute-start(bf16[512,256]{1,0:T(8,128)(2,1)S(1)} %get-tuple-element.61), channel_id=1, source_target_pairs={{0,2},{1,3},{2,0},{3,1},{4,6},{5,7},{6,4},{7,5},{8,10},{9,11},{10,... | collective-permute-start | bytes 786440 | tf_op jit(solution)/shard_map/ppermute | solution.py:264

commit v2 on v1

v2 whole, which is shorter than its diff:
```python
import math

import jax
import jax.numpy as jnp
from jax import lax
from jax.experimental import pallas as pl
from jax.experimental.pallas import tpu as pltpu
from jax.sharding import PartitionSpec as P

NT = (((1,), (1,)), ((), ()))
NN = (((1,), (0,)), ((), ()))
F32, BF16 = jnp.float32, jnp.bfloat16
NEG_FILL = -1e30
MIB = 1024 * 1024


def dot(a, b, dims=NN):
    return lax.dot_general(a, b, dims, preferred_element_type=F32)


def attend_body(valid, q, b, own, tmb, tma, hb, ha,
                att, dq, g_own, g_tmb, g_tma, g_hb, g_ha,
                ks, vs, kt, vt, dk, dv, s_buf, t_buf, p_buf, d_buf, bias):
    def put(frame, row, block):
        rows = block.shape[0]
        block = block.reshape(rows * 64, 256)
        at = pl.ds((frame * 10 + row) * 64, rows * 64)
        ks[at, :] = block[:, :128]
        vs[at, :] = block[:, 128:]

    for i in range(4):
        put(i, 0, hb[i])
        put(i, 7, ha[i])
    put(0, 3, tmb[0])
    put(1, 3, own[0])
    put(2, 3, own[1])
    put(3, 3, tma[0])

    eye = jnp.where(
        lax.broadcasted_iota(jnp.int32, (128, 128), 0) == lax.broadcasted_iota(jnp.int32, (128, 128), 1),
        1.0, 0.0,
    ).astype(BF16)
    same_head = (lax.broadcasted_iota(jnp.int32, (256, 128), 0) // 128) == (
        lax.broadcasted_iota(jnp.int32, (256, 128), 1) // 64
    )
    for i in range(5):
        at = pl.ds(i * 512, 512)
        kt[:, at] = dot(eye, ks[at, :], NT).astype(BF16)
        vt[:, at] = dot(eye, vs[at, :], NT).astype(BF16)
    dk[...] = jnp.zeros_like(dk)
    dv[...] = jnp.zeros_like(dv)
    krow = lax.broadcasted_iota(jnp.int32, (64, 256), 0)
    lane = lax.broadcasted_iota(jnp.int32, (64, 256), 1)
    band = jnp.abs(krow - lane % 64) <= 3
    second = (lane // 64) % 2 == 1
    bias[0] = jnp.full((64, 256), NEG_FILL, F32)
    bias[1] = jnp.where(band, 0.0, NEG_FILL)
    bias[2] = jnp.where(band & ~second, 0.0, NEG_FILL)
    bias[3] = jnp.where(band & second, 0.0, NEG_FILL)
    first_head = lax.broadcasted_iota(jnp.int32, (128, 128), 1) < 64

    def spread(rows):
        return jnp.where(same_head, jnp.concatenate([rows] * 2, axis=0), jnp.zeros((), BF16))

    def gather(outT):
        out = outT.T
        return jnp.where(first_head, out[0:128], out[128:256])

    def group(g, _):
        f, r = g // 2, (g % 2) * 2
        mine = pl.ds(pl.multiple_of(g * 128, 128), 128)
        qbd = spread(q[mine, :])
        bbd = spread(b[mine, :])

        def keys_of(i):
            return pl.ds(pl.multiple_of(((f + i) * 10 + r) * 64, 128), 512)

        top = jnp.full((64, 256), NEG_FILL, F32)
        for i in range(3):
            sc = dot(ks[keys_of(i), :], qbd, NT)
            for j in range(8):
                kind = 2 if j == 0 else 3 if j == 7 else 1
                v = sc[j * 64:(j + 1) * 64] + bias[valid[f + i, r + j] * kind]
                s_buf[pl.ds((i * 8 + j) * 64, 64), :] = v
                top = jnp.maximum(top, v)
        m = jnp.max(top, axis=0, keepdims=True)
        tot = jnp.zeros((64, 256), F32)
        for j in range(24):
            at = pl.ds(j * 64, 64)
            e = jnp.exp(s_buf[at, :] - m)
            s_buf[at, :] = e
            tot = tot + e
        inv = 1.0 / jnp.sum(tot, axis=0, keepdims=True)
        cen = jnp.zeros((64, 256), F32)
        for i in range(3):
            sl = dot(vs[keys_of(i), :], bbd, NT)
            for j in range(8):
                at = pl.ds((i * 8 + j) * 64, 64)
                p = s_buf[at, :] * inv
                s_buf[at, :] = p
                p_buf[at, :] = p.astype(BF16)
                x = sl[j * 64:(j + 1) * 64]
                t_buf[at, :] = x
                cen = cen + p * x
        c = jnp.sum(cen, axis=0, keepdims=True)
        for j in range(24):
            at = pl.ds(j * 64, 64)
            d_buf[at, :] = (s_buf[at, :] * (t_buf[at, :] - c)).astype(BF16)
        outT = jnp.zeros((128, 256), F32)
        dqT = jnp.zeros((128, 256), F32)
        for i in range(3):
            at = pl.ds(i * 512, 512)
            pb, db = p_buf[at, :], d_buf[at, :]
            outT = outT + dot(vt[:, keys_of(i)], pb)
            dqT = dqT + dot(kt[:, keys_of(i)], db)
            dv[keys_of(i), :] += dot(pb, bbd)
            dk[keys_of(i), :] += dot(db, qbd)
        att[mine, :] = gather(outT).astype(BF16)
        dq[mine, :] = (gather(dqT) * 0.125).astype(BF16)
        return 0

    lax.fori_loop(0, 4, group, 0)

    def take(frame, row, rows, out):
        at = pl.ds((frame * 10 + row) * 64, rows * 64)
        kv = jnp.concatenate([dk[at, :], dv[at, :]], axis=1)
        return kv.reshape(rows, 64, 256).astype(out.dtype)

    for i in range(4):
        g_hb[i] = take(i, 0, 3, g_hb)
        g_ha[i] = take(i, 7, 3, g_ha)
    g_tmb[0] = take(0, 3, 4, g_tmb)
    g_own[0] = take(1, 3, 4, g_own)
    g_own[1] = take(2, 3, 4, g_own)
    g_tma[0] = take(3, 3, 4, g_tma)


def project_body(idx, x0, x1, x2, x3, w, q0, q1, own0, own1, f00, f10, f01, f11):
    acc = None
    for i, x in enumerate((x0, x1, x2, x3)):
        at = pl.ds(pl.multiple_of(idx[i] * 256, 256), 256)
        part = [dot(x[...], w[n, at, :]) for n in range(3)]
        acc = part if acc is None else [a + b for a, b in zip(acc, part)]
    query, keys, values = (a.astype(BF16) for a in acc)
    query = query * jnp.asarray(0.125, BF16)
    for half, (q, own, f0, f1) in enumerate(((q0, own0, f00, f10), (q1, own1, f01, f11))):
        at = slice(half * 128, half * 128 + 128)
        q[...] = query[:, at]
        kv = jnp.concatenate([keys[:, at], values[:, at]], axis=1).reshape(2, 4, 64, 256)
        own[...] = kv
        f0[...] = kv[0:1]
        f1[...] = kv[1:2]


def edges_body(tmb, own, tma, lo, hi):
    for i, (ref, at) in enumerate(((tmb, 0), (own, 0), (own, 1), (tma, 0))):
        lo[i] = ref[at, 0:3]
        hi[i] = ref[at, 1:4]


def fold_body(g_tmb, g_tma, r_hb, r_ha, s_tmb, s_tma, acc):
    for g, at, s in ((g_tmb, 0, s_tmb), (g_tma, 3, s_tma)):
        acc[...] = g[...]
        acc[0, 0:3] += r_hb[at].astype(F32)
        acc[0, 1:4] += r_ha[at].astype(F32)
        s[...] = acc[...].astype(BF16)


def back_body(idx, x0, x1, x2, x3, w, out0, out1):
    acc = None
    for i, x in enumerate((x0, x1, x2, x3)):
        part = dot(x[...], w[:, pl.ds(pl.multiple_of(idx[i] * 256, 256), 256)], NT)
        acc = part if acc is None else acc + part
    out0[...] = acc[:, :128].astype(BF16)
    out1[...] = acc[:, 128:].astype(BF16)


def mixed_body(idx, att0, att1, w, own, right, left, across):
    att = jnp.concatenate([att0[...], att1[...]], axis=1)
    for i, out in enumerate((own, right, left, across)):
        block = w[:, pl.ds(pl.multiple_of(idx[i] * 256, 256), 256)]
        out[...] = dot(att, block).astype(out.dtype)


def grad_body(idx, dq0, own0, hb0, ha0, tb0, ta0, dq1, own1, hb1, ha1, tb1, ta1, w,
              mine, right, left, across, kv):
    low = []
    for own, hb, ha, tb, ta in ((own0, hb0, ha0, tb0, ta0), (own1, hb1, ha1, tb1, ta1)):
        kv[...] = own[...]
        kv[:, 0:3] += hb[1:3].astype(F32)
        kv[:, 1:4] += ha[1:3].astype(F32)
        kv[0] += tb[0].astype(F32)
        kv[1] += ta[0].astype(F32)
        low.append(kv[...].reshape(512, 256).astype(BF16))
    dq = jnp.concatenate([dq0[...], dq1[...]], axis=1)
    dk = jnp.concatenate([low[0][:, :128], low[1][:, :128]], axis=1)
    dv = jnp.concatenate([low[0][:, 128:], low[1][:, 128:]], axis=1)
    for i, out in enumerate((mine, right, left, across)):
        at = pl.ds(pl.multiple_of(idx[i] * 256, 256), 256)
        total = dot(dq, w[0, at, :], NT)
        total = total + dot(dk, w[1, at, :], NT)
        total = total + dot(dv, w[2, at, :], NT)
        out[...] = total.astype(out.dtype)


def sum_body(a, b, c, d, out):
    total = a[...] + b[...].astype(F32) + c[...].astype(F32) + d[...].astype(F32)
    out[...] = total.astype(BF16).reshape(out.shape)


def local_call(body, outs, idx, arrays, scratch=(), flops=0, name=None, limit=12):
    vm = pl.BlockSpec(memory_space=pltpu.VMEM)
    specs = [vm] * len(arrays)
    args = list(arrays)
    if idx is not None:
        specs = [pl.BlockSpec(memory_space=pltpu.SMEM)] + specs
        args = [idx] + args
    size = sum(math.prod(a.shape) * a.dtype.itemsize for a in list(arrays) + list(outs))
    return pl.pallas_call(
        body,
        out_shape=tuple(outs),
        in_specs=specs,
        out_specs=(vm,) * len(outs),
        scratch_shapes=list(scratch),
        compiler_params=pltpu.CompilerParams(vmem_limit_bytes=limit * MIB),
        cost_estimate=pl.CostEstimate(flops=flops, bytes_accessed=size, transcendentals=0),
        name=name,
    )(*args)


def shards(tokens, cotangent, w_qkv, w_out):
    S = jax.ShapeDtypeStruct
    n_x, n_t, n_h = (lax.axis_size(a) for a in ("tensor", "tm", "height"))
    x, t, h = (lax.axis_index(a) for a in ("tensor", "tm", "height"))
    idx = jnp.stack([x, (x + n_x - 1) % n_x, (x + 1) % n_x, (x + 2) % n_x]).astype(jnp.int32)
    idx_out = jnp.stack([x, (x + 1) % n_x, (x + n_x - 1) % n_x, (x + 2) % n_x]).astype(jnp.int32)
    frame_place = t * 2 + jnp.arange(4, dtype=jnp.int32) - 1
    row_place = h * 4 + jnp.arange(10, dtype=jnp.int32) - 3
    fine = ((frame_place >= 0) & (frame_place < 2 * n_t))[:, None]
    fine = fine & ((row_place >= 0) & (row_place < 4 * n_h))[None, :]
    valid = fine.astype(jnp.int32)

    def ring(array, by):
        return lax.ppermute(array, "tensor", [(i, (i + by) % n_x) for i in range(n_x)])

    def frames(array, by):
        return lax.ppermute(array, "tm", [(i, (i + by) % n_t) for i in range(n_t)])

    def rows(array, by):
        return lax.ppermute(array, "height", [(i, (i + by) % n_h) for i in range(n_h)])

    tok = tokens.reshape(512, 256)
    flat = jnp.transpose(w_qkv, (1, 0, 2))
    t_parts = (ring(tok, 1), ring(tok, -1), ring(tok, 2))
    half = S((512, 128), BF16)
    pair, frame, edge = (2, 4, 64, 256), (1, 4, 64, 256), (4, 3, 64, 256)
    q0, q1, own0, own1, f00, f10, f01, f11 = local_call(
        project_body,
        (half, half, S(pair, BF16), S(pair, BF16)) + (S(frame, BF16),) * 4,
        idx, (tok, *t_parts, flat), flops=2 * 512 * 1024 * 768, name="project",
    )
    cot, _ = lax.optimization_barrier((cotangent.reshape(512, 256), q0))

    def surround(own, f0, f1):
        tmb, tma = frames(f1, 1), frames(f0, -1)
        lo, hi = local_call(edges_body, (S(edge, BF16),) * 2, None, (tmb, own, tma), name="edges")
        return own, tmb, tma, rows(hi, 1), rows(lo, -1)

    around0 = surround(own0, f00, f10)
    c_parts = (ring(cot, 1), ring(cot, -1), ring(cot, 2))
    around1 = surround(own1, f01, f11)
    b0, b1 = local_call(
        back_body, (half, half), idx, (cot, *c_parts, w_out),
        flops=2 * 512 * 1024 * 256, name="back",
    )

    def attend(q, b, around):
        return local_call(
            attend_body,
            (half, half, S(pair, F32), S(frame, F32), S(frame, F32), S(edge, BF16), S(edge, BF16)),
            valid, (q, b, *around),
            scratch=[
                pltpu.VMEM((2560, 128), BF16), pltpu.VMEM((2560, 128), BF16),
                pltpu.VMEM((128, 2560), BF16), pltpu.VMEM((128, 2560), BF16),
                pltpu.VMEM((2560, 128), F32), pltpu.VMEM((2560, 128), F32),
                pltpu.VMEM((1536, 256), F32), pltpu.VMEM((1536, 256), F32),
                pltpu.VMEM((1536, 256), BF16), pltpu.VMEM((1536, 256), BF16),
                pltpu.VMEM((4, 64, 256), F32),
            ],
            flops=4 * 6 * 2 * 1536 * 256 * 256 * 2, name="attend", limit=24,
        )

    def settle(g_tmb, g_tma, g_hb, g_ha):
        r_ha, r_hb = rows(g_hb, -1), rows(g_ha, 1)
        s_tmb, s_tma = local_call(
            fold_body, (S(frame, BF16),) * 2, None, (g_tmb, g_tma, r_hb, r_ha),
            scratch=[pltpu.VMEM(frame, F32)], name="fold",
        )
        return r_hb, r_ha, frames(s_tma, 1), frames(s_tmb, -1)

    att0, dq0, g_own0, *g0 = attend(q0, b0, around0)
    att1, dq1, g_own1, *g1 = attend(q1, b1, around1)
    back0 = settle(*g0)
    back1 = settle(*g1)
    piece = S((512, 256), BF16)
    parts = (S((512, 256), F32), piece, piece, piece)
    m0, m1, m2, m3 = local_call(
        mixed_body, parts, idx_out, (att0, att1, w_out), flops=2 * 512 * 1024 * 256, name="mix",
    )
    out = (S((2, 4, 64, 256), BF16),)
    (mixed,) = local_call(
        sum_body, out, None, (m0, ring(m1, 1), ring(m2, -1), ring(m3, 2)), name="mixed_sum"
    )
    e0, e1, e2, e3 = local_call(
        grad_body, parts, idx_out, (dq0, g_own0, *back0, dq1, g_own1, *back1, flat),
        scratch=[pltpu.VMEM(pair, F32)], flops=2 * 512 * 1024 * 768, name="in_grad", limit=16,
    )
    (in_grad,) = local_call(
        sum_body, out, None, (e0, ring(e1, 1), ring(e2, -1), ring(e3, 2)), name="in_grad_sum"
    )
    return mixed, in_grad


def solution(mesh):
    in_specs = (
        P("tm", "height", None, "tensor"),
        P("tm", "height", None, "tensor"),
        P(None, None, "tensor"),
        P("tensor", None),
    )
    out_specs = (P("tm", "height", None, "tensor"), P("tm", "height", None, "tensor"))
    return jax.shard_map(shards, mesh=mesh, in_specs=in_specs, out_specs=out_specs, check_vma=False)
```

time: 166 us -> 124 us (0.75)
  waiting for transfers between devices: 76.4 us -> 48.4 us
  starting transfers between devices: 55.3 us -> 43.6 us
  local copies, waits for them, and re-layouts: 7.32 us -> 3.68 us
    ppermute x16, waiting for transfers between devices: 53.2 us -> 17.2 us  [the longest x8 10.6 us: frames(): return lax.ppermute(array, 'tm', [(i, (i + by) % n_t) for i in range(n_t)])]
    pallas_call x1 -> x0, Pallas kernels: 18.1 us -> none  [attend(): pl.pallas_call(attend_body, out_shape=outs, in_specs=[pl.BlockSpec(memory...]
    pallas_call x6 -> x12, Pallas kernels: 7.45 us -> 25.6 us  [local_call(): pl.pallas_call(body, out_shape=tuple(outs), in_specs=specs, out_specs=(vm...]
    ppermute x16, starting transfers between devices: 41.2 us -> 27.6 us  [the longest x8 18.9 us: frames(): return lax.ppermute(array, 'tm', [(i, (i + by) % n_t) for i in range(n_t)])]
    ppermute x12, waiting for transfers between devices: 23.2 us -> 31.2 us  [ring(): lax.ppermute(array, 'tensor', [(i, (i + by) % n_x) for i in range(n_x)])]
    unnamed x34 -> x18, local copies, waits for them, and re-layouts: 7.32 us -> 3.68 us
    ppermute x12, starting transfers between devices: 14.2 us -> 16 us  [ring(): lax.ppermute(array, 'tensor', [(i, (i + by) % n_x) for i in range(n_x)])]
  transfers between devices with their start and end apart: 28 -> 28, of which waited for: 13 -> 12; matrix products, arithmetic and copies ran while one was open for 0% -> 0% of each run, Pallas kernels for 3% -> 18%
where the time goes in v2:
time: 124 us; the launch traced here: 122 us
  waiting for transfers between devices  48.4 us (39%)
  starting transfers between devices  43.6 us (35%)
  Pallas kernels  25.6 us (21%)
  local copies, waits for them, and re-layouts  3.68 us (3%)
    ppermute x12, waiting for transfers between devices, ring(): lax.ppermute(array, 'tensor', [(i, (i + by) % n_x) for i in range(n_x)])  31.2 us
    pallas_call x12, Pallas kernels, local_call(): pl.pallas_call(body, out_shape=tuple(outs), in_specs=specs, out_specs=(vm...  25.6 us
    ppermute x8, starting transfers between devices, frames(): return lax.ppermute(array, 'tm', [(i, (i + by) % n_t) for i in range(n_t)])  18.9 us
    ppermute x12, starting transfers between devices, ring(): lax.ppermute(array, 'tensor', [(i, (i + by) % n_x) for i in range(n_x)])  16 us
    ppermute x8, waiting for transfers between devices, frames(): return lax.ppermute(array, 'tm', [(i, (i + by) % n_t) for i in range(n_t)])  10.6 us
    ppermute x8, starting transfers between devices, rows(): lax.ppermute(array, 'height', [(i, (i + by) % n_h) for i in range(n_h)])  8.78 us
    ppermute x8, waiting for transfers between devices, rows(): lax.ppermute(array, 'height', [(i, (i + by) % n_h) for i in range(n_h)])  6.65 us
    unnamed x18, local copies, waits for them, and re-layouts  3.68 us
  transfers between devices with their start and end apart: 28, of which 12 were waited for; matrix products, arithmetic and copies ran while one was open for 0% of the time, Pallas kernels for 18%

profile of v2, /device:TPU:22, one launch (start us, length us, event | category | flops | bytes accessed | tf_op | source)
XLA Modules:
  0.0 122.4 jit_solution(13693365109026952873)
XLA Ops:
  0.6 1.5 %collective-permute-start.2 = (bf16[512,256]{1,0:T(8,128)(2,1)}, bf16[512,256]{1,0:T(8,128)(2,1)S(1)}, u32[]{:S(2)}, u32[]{:S(2)}) collective-permute-start(bf16[512,256]{1,0:T(8,128)(2,1)} %bitcast.13), channel_id=1, source_target_pairs={{0,2},{1,3},{2,0},{3,1},{4,6},{5,7},{6,4},{7,5},{8,10},{9,11},{10,... | collective-permute-start | bytes 786440 | tf_op jit(solution)/shard_map/ppermute | solution.py:244
  2.1 0.0 collective-permute-start.1
  2.1 3.2 %collective-permute-start = (bf16[512,256]{1,0:T(8,128)(2,1)}, bf16[512,256]{1,0:T(8,128)(2,1)S(1)}, u32[]{:S(2)}, u32[]{:S(2)}) collective-permute-start(bf16[512,256]{1,0:T(8,128)(2,1)} %bitcast.15), channel_id=1, source_target_pairs={{0,1},{1,2},{2,3},{3,0},{4,5},{5,6},{6,7},{7,4},{8,9},{9,10},{10,1... | collective-permute-start | bytes 786440 | tf_op jit(solution)/shard_map/ppermute | solution.py:244
  5.4 0.1 add_add_fusion.1.idx
  5.4 6.2 %collective-permute-done.2.x3 = bf16[512,256]{1,0:T(8,128)(2,1)S(1)} collective-permute-done((bf16[512,256]{1,0:T(8,128)(2,1)}, bf16[512,256]{1,0:T(8,128)(2,1)S(1)}, u32[]{:S(2)}, u32[]{:S(2)}) %collective-permute-start.2) | collective-permute-done | bytes 262176 | tf_op jit(solution)/shard_map/ppermute | solution.py:244
  11.7 4.4 %collective-permute-done.1.x2 = bf16[512,256]{1,0:T(8,128)(2,1)S(1)} collective-permute-done((bf16[512,256]{1,0:T(8,128)(2,1)}, bf16[512,256]{1,0:T(8,128)(2,1)S(1)}, u32[]{:S(2)}, u32[]{:S(2)}) %collective-permute-start.1) | collective-permute-done | bytes 262176 | tf_op jit(solution)/shard_map/ppermute | solution.py:244
  16.1 0.0 collective-permute-done.x1
  16.1 1.4 %copy-done = bf16[1024,3,256]{2,0,1:T(8,128)(2,1)S(1)} copy-done((bf16[1024,3,256]{2,0,1:T(8,128)(2,1)S(1)}, bf16[1024,3,256]{2,0,1:T(8,128)(2,1)}, u32[]{:S(2)}) %copy-start) | copy-done | bytes 1572888
  17.5 0.9 copy-done.4
  18.5 2.2 %project.1 = (bf16[512,128]{1,0:T(8,128)(2,1)S(1)}, bf16[512,128]{1,0:T(8,128)(2,1)S(1)}, bf16[2,4,64,256]{3,2,1,0:T(8,128)(2,1)S(1)}, bf16[2,4,64,256]{3,2,1,0:...) custom-call(s32[4]{0:T(128)S(1)} %add_add_fusion.1.idx, ...), custom_call_target="tpu_custom_call" | custom-call | flops 805306368 | bytes 3932160 | tf_op jit(solution)/shard_map/project/pallas_call | solution.py:219
  20.7 0.7 copy-done.5
  21.3 0.6 copy-done.7
  22.0 3.3 %collective-permute-start.10 = (bf16[1,4,64,256]{3,2,1,0:T(8,128)(2,1)S(1)}, bf16[1,4,64,256]{3,2,1,0:T(8,128)(2,1)S(1)}, u32[]{:S(2)}, u32[]{:S(2)}) collective-permute-start(bf16[1,4,64,256]{3,2,1,0:T(8,128)(2,1)S(1)} %get-tuple-element.55), channel_id=1, source_target_pairs={{0,64},{64,128},{128,192},{192,0},{1,65},{65,129},{129,193},{193,1... | collective-permute-start | bytes 393224 | tf_op jit(solution)/shard_map/ppermute | solution.py:247
  25.2 3.0 %collective-permute-start.11 = (bf16[1,4,64,256]{3,2,1,0:T(8,128)(2,1)S(1)}, bf16[1,4,64,256]{3,2,1,0:T(8,128)(2,1)S(1)}, u32[]{:S(2)}, u32[]{:S(2)}) collective-permute-start(bf16[1,4,64,256]{3,2,1,0:T(8,128)(2,1)S(1)} %get-tuple-element.56), channel_id=1, source_target_pairs={{0,192},{64,0},{128,64},{192,128},{1,193},{65,1},{129,65},{193,129... | collective-permute-start | bytes 393224 | tf_op jit(solution)/shard_map/ppermute | solution.py:247
  28.3 1.5 %collective-permute-start.6 = (bf16[1,4,64,256]{3,2,1,0:T(8,128)(2,1)}, bf16[1,4,64,256]{3,2,1,0:T(8,128)(2,1)S(1)}, u32[]{:S(2)}, u32[]{:S(2)}) collective-permute-start(bf16[1,4,64,256]{3,2,1,0:T(8,128)(2,1)} %get-tuple-element.47), channel_id=1, source_target_pairs={{0,64},{64,128},{128,192},{192,0},{1,65},{65,129},{129,193},{193,1... | collective-permute-start | bytes 393224 | tf_op jit(solution)/shard_map/ppermute | solution.py:247
  29.7 2.7 %collective-permute-start.7 = (bf16[1,4,64,256]{3,2,1,0:T(8,128)(2,1)S(1)}, bf16[1,4,64,256]{3,2,1,0:T(8,128)(2,1)S(1)}, u32[]{:S(2)}, u32[]{:S(2)}) collective-permute-start(bf16[1,4,64,256]{3,2,1,0:T(8,128)(2,1)S(1)} %get-tuple-element.48), channel_id=1, source_target_pairs={{0,192},{64,0},{128,64},{192,128},{1,193},{65,1},{129,65},{193,129... | collective-permute-start | bytes 393224 | tf_op jit(solution)/shard_map/ppermute | solution.py:247
  32.4 0.1 collective-permute-done.10.tmb
  32.5 6.7 %collective-permute-done.11.tma = bf16[1,4,64,256]{3,2,1,0:T(8,128)(2,1)S(1)} collective-permute-done((bf16[1,4,64,256]{3,2,1,0:T(8,128)(2,1)S(1)}, bf16[1,4,64,256]{3,2,1,0:T(8,128)(2,1)S(1)}, u32[]{:S(2)}, u32[]{:S(2)}) %collective-permute-start.11) | collective-permute-done | bytes 131104 | tf_op jit(solution)/shard_map/ppermute | solution.py:247
  39.3 0.1 edges.3
  39.3 0.1 collective-permute-start.12
  39.4 2.6 %collective-permute-start.13 = (bf16[4,3,64,256]{3,2,1,0:T(8,128)(2,1)S(1)}, bf16[4,3,64,256]{3,2,1,0:T(8,128)(2,1)S(1)}, u32[]{:S(2)}, u32[]{:S(2)}) collective-permute-start(bf16[4,3,64,256]{3,2,1,0:T(8,128)(2,1)S(1)} %get-tuple-element.58), channel_id=1, source_target_pairs={{0,60},{4,0},{8,4},{12,8},{16,12},{20,16},{24,20},{28,24},{32,28},... | collective-permute-start | bytes 1179656 | tf_op jit(solution)/shard_map/ppermute | solution.py:250
  42.1 1.5 %collective-permute-start.5 = (bf16[512,256]{1,0:T(8,128)(2,1)S(1)}, bf16[512,256]{1,0:T(8,128)(2,1)S(1)}, u32[]{:S(2)}, u32[]{:S(2)}) collective-permute-start(bf16[512,256]{1,0:T(8,128)(2,1)S(1)} %bitcast.9), channel_id=1, source_target_pairs={{0,2},{1,3},{2,0},{3,1},{4,6},{5,7},{6,4},{7,5},{8,10},{9,11},{10,... | collective-permute-start | bytes 786440 | tf_op jit(solution)/shard_map/ppermute | solution.py:244
  43.6 3.2 %collective-permute-start.3 = (bf16[512,256]{1,0:T(8,128)(2,1)S(1)}, bf16[512,256]{1,0:T(8,128)(2,1)S(1)}, u32[]{:S(2)}, u32[]{:S(2)}) collective-permute-start(bf16[512,256]{1,0:T(8,128)(2,1)S(1)} %bitcast.11), channel_id=1, source_target_pairs={{0,1},{1,2},{2,3},{3,0},{4,5},{5,6},{6,7},{7,4},{8,9},{9,10},{10,1... | collective-permute-start | bytes 786440 | tf_op jit(solution)/shard_map/ppermute | solution.py:244
  46.8 0.1 and_convert_fusion.valid
  46.9 0.1 edges.2
  47.0 5.7 %collective-permute-done.5.x3 = bf16[512,256]{1,0:T(8,128)(2,1)S(1)} collective-permute-done((bf16[512,256]{1,0:T(8,128)(2,1)S(1)}, bf16[512,256]{1,0:T(8,128)(2,1)S(1)}, u32[]{:S(2)}, u32[]{:S(2)}) %collective-permute-start.5) | collective-permute-done | bytes 262176 | tf_op jit(solution)/shard_map/ppermute | solution.py:244
  52.7 2.7 %collective-permute-done.4.x2 = bf16[512,256]{1,0:T(8,128)(2,1)S(1)} collective-permute-done((bf16[512,256]{1,0:T(8,128)(2,1)S(1)}, bf16[512,256]{1,0:T(8,128)(2,1)S(1)}, u32[]{:S(2)}, u32[]{:S(2)}) %collective-permute-start.4) | collective-permute-done | bytes 262176 | tf_op jit(solution)/shard_map/ppermute | solution.py:244
  55.4 0.6 collective-permute-start.9
  56.1 1.0 back.1
  57.1 0.0 collective-permute-done.13.ha
  57.1 0.0 copy-start.6
  57.2 8.9 %attend.3 = (bf16[512,128]{1,0:T(8,128)(2,1)S(1)}, bf16[512,128]{1,0:T(8,128)(2,1)S(1)}, f32[2,4,64,256]{3,2,1,0:T(8,128)S(1)}, f32[1,4,64,256]{3,2,1,0:T(8,128)...) custom-call(s32[4,10]{1,0:T(4,128)S(1)} %and_convert_fusion.valid, ...), custom_call_target="tpu_custom_call" | custom-call | flops 9663676416 | bytes 3670016 | tf_op jit(solution)/shard_map/attend/pallas_call | solution.py:219
  66.1 0.1 collective-permute-start.21
  66.2 2.6 %collective-permute-start.22 = (bf16[4,3,64,256]{3,2,1,0:T(8,128)(2,1)S(1)}, bf16[4,3,64,256]{3,2,1,0:T(8,128)(2,1)S(1)}, u32[]{:S(2)}, u32[]{:S(2)}) collective-permute-start(bf16[4,3,64,256]{3,2,1,0:T(8,128)(2,1)S(1)} %get-tuple-element.75), channel_id=1, source_target_pairs={{0,60},{4,0},{8,4},{12,8},{16,12},{20,16},{24,20},{28,24},{32,28},... | collective-permute-start | bytes 1179656 | tf_op jit(solution)/shard_map/ppermute | solution.py:250
  68.8 0.0 collective-permute-done.8.hb
  68.8 0.0 collective-permute-done.9.ha
  68.8 8.9 %attend.2 = (bf16[512,128]{1,0:T(8,128)(2,1)S(1)}, bf16[512,128]{1,0:T(8,128)(2,1)S(1)}, f32[2,4,64,256]{3,2,1,0:T(8,128)S(1)}, f32[1,4,64,256]{3,2,1,0:T(8,128)...) custom-call(s32[4,10]{1,0:T(4,128)S(1)} %and_convert_fusion.valid, ...), custom_call_target="tpu_custom_call" | custom-call | flops 9663676416 | bytes 3670016 | tf_op jit(solution)/shard_map/attend/pallas_call | solution.py:219
  77.8 0.1 collective-permute-start.17
  77.8 2.6 %collective-permute-start.18 = (bf16[4,3,64,256]{3,2,1,0:T(8,128)(2,1)S(1)}, bf16[4,3,64,256]{3,2,1,0:T(8,128)(2,1)S(1)}, u32[]{:S(2)}, u32[]{:S(2)}) collective-permute-start(bf16[4,3,64,256]{3,2,1,0:T(8,128)(2,1)S(1)} %get-tuple-element.67), channel_id=1, source_target_pairs={{0,60},{4,0},{8,4},{12,8},{16,12},{20,16},{24,20},{28,24},{32,28},... | collective-permute-start | bytes 1179656 | tf_op jit(solution)/shard_map/ppermute | solution.py:250
  80.5 0.1 add_add_fusion.idx
  80.6 1.0 mix.1
  81.6 0.0 copy-start.1
  81.6 0.5 collective-permute-start.14
  82.1 0.1 fold.3
  82.1 4.0 %collective-permute-start.23 = (bf16[1,4,64,256]{3,2,1,0:T(8,128)(2,1)S(1)}, bf16[1,4,64,256]{3,2,1,0:T(8,128)(2,1)S(1)}, u32[]{:S(2)}, u32[]{:S(2)}) collective-permute-start(bf16[1,4,64,256]{3,2,1,0:T(8,128)(2,1)S(1)} %get-tuple-element.78), channel_id=1, source_target_pairs={{0,64},{64,128},{128,192},{192,0},{1,65},{65,129},{129,193},{193,1... | collective-permute-start | bytes 393224 | tf_op jit(solution)/shard_map/ppermute | solution.py:247
  86.2 0.2 collective-permute-start.24
  86.3 6.6 %collective-permute-done.17.r_hb.hb0 = bf16[4,3,64,256]{3,2,1,0:T(8,128)(2,1)S(1)} collective-permute-done((bf16[4,3,64,256]{3,2,1,0:T(8,128)(2,1)S(1)}, bf16[4,3,64,256]{3,2,1,0:T(8,128)(2,1)S(1)}, u32[]{:S(2)}, u32[]{:S(2)}) %collective-permute-start.17) | collective-permute-done | bytes 393248 | tf_op jit(solution)/shard_map/ppermute | solution.py:250
  93.0 0.0 collective-permute-done.18.r_ha.ha0
  93.0 0.1 fold.2
  93.1 3.4 %collective-permute-start.19 = (bf16[1,4,64,256]{3,2,1,0:T(8,128)(2,1)S(1)}, bf16[1,4,64,256]{3,2,1,0:T(8,128)(2,1)S(1)}, u32[]{:S(2)}, u32[]{:S(2)}) collective-permute-start(bf16[1,4,64,256]{3,2,1,0:T(8,128)(2,1)S(1)} %get-tuple-element.70), channel_id=1, source_target_pairs={{0,64},{64,128},{128,192},{192,0},{1,65},{65,129},{129,193},{193,1... | collective-permute-start | bytes 393224 | tf_op jit(solution)/shard_map/ppermute | solution.py:247
  96.4 0.8 collective-permute-start.20
  97.3 0.1 collective-permute-start.15
  97.4 2.0 %collective-permute-start.16 = (bf16[512,256]{1,0:T(8,128)(2,1)S(1)}, bf16[512,256]{1,0:T(8,128)(2,1)S(1)}, u32[]{:S(2)}, u32[]{:S(2)}) collective-permute-start(bf16[512,256]{1,0:T(8,128)(2,1)S(1)} %get-tuple-element.63), channel_id=1, source_target_pairs={{0,2},{1,3},{2,0},{3,1},{4,6},{5,7},{6,4},{7,5},{8,10},{9,11},{10,... | collective-permute-start | bytes 786440 | tf_op jit(solution)/shard_map/ppermute | solution.py:244
  99.4 1.0 collective-permute-done.19.tb0
  100.3 2.8 %collective-permute-done.20.ta0 = bf16[1,4,64,256]{3,2,1,0:T(8,128)(2,1)S(1)} collective-permute-done((bf16[1,4,64,256]{3,2,1,0:T(8,128)(2,1)S(1)}, bf16[1,4,64,256]{3,2,1,0:T(8,128)(2,1)S(1)}, u32[]{:S(2)}, u32[]{:S(2)}) %collective-permute-start.20) | collective-permute-done | bytes 131104 | tf_op jit(solution)/shard_map/ppermute | solution.py:247
  103.1 1.6 %in_grad.1 = (f32[512,256]{1,0:T(8,128)S(1)}, bf16[512,256]{1,0:T(8,128)(2,1)S(1)}, bf16[512,256]{1,0:T(8,128)(2,1)S(1)}, bf16[512,256]{1,0:T(8,128)(2,1)S(1)}) custom-call(s32[4]{0:T(128)S(1)} %add_add_fusion.idx, bf16[512,128]{1,0:T(8,128)(2,1)S(1)} %get-tuple-element.64.dq0, f32[2,4,64,256]{3,2,1,0:T(8,128)S(1)} %get-tuple-element.65.own0, ...), custom_call_target="tpu_custom_call" | custom-call | flops 805306368 | bytes 6291456 | tf_op jit(solution)/shard_map/in_grad/pallas_call | solution.py:219
  104.7 0.5 collective-permute-start.25
  105.2 1.6 %collective-permute-start.26 = (bf16[512,256]{1,0:T(8,128)(2,1)S(1)}, bf16[512,256]{1,0:T(8,128)(2,1)S(1)}, u32[]{:S(2)}, u32[]{:S(2)}) collective-permute-start(bf16[512,256]{1,0:T(8,128)(2,1)S(1)} %get-tuple-element.82), channel_id=1, source_target_pairs={{0,3},{1,0},{2,1},{3,2},{4,7},{5,4},{6,5},{7,6},{8,11},{9,8},{10,9... | collective-permute-start | bytes 786440 | tf_op jit(solution)/shard_map/ppermute | solution.py:244
  106.8 1.9 %collective-permute-start.27 = (bf16[512,256]{1,0:T(8,128)(2,1)S(1)}, bf16[512,256]{1,0:T(8,128)(2,1)S(1)}, u32[]{:S(2)}, u32[]{:S(2)}) collective-permute-start(bf16[512,256]{1,0:T(8,128)(2,1)S(1)} %get-tuple-element.83), channel_id=1, source_target_pairs={{0,2},{1,3},{2,0},{3,1},{4,6},{5,7},{6,4},{7,5},{8,10},{9,11},{10,... | collective-permute-start | bytes 786440 | tf_op jit(solution)/shard_map/ppermute | solution.py:244
  108.7 2.3 %collective-permute-done.15.c = bf16[512,256]{1,0:T(8,128)(2,1)S(1)} collective-permute-done((bf16[512,256]{1,0:T(8,128)(2,1)S(1)}, bf16[512,256]{1,0:T(8,128)(2,1)S(1)}, u32[]{:S(2)}, u32[]{:S(2)}) %collective-permute-start.15) | collective-permute-done | bytes 262176 | tf_op jit(solution)/shard_map/ppermute | solution.py:244
  111.0 0.8 mixed_sum.1
  111.8 2.2 %collective-permute-done.25.b = bf16[512,256]{1,0:T(8,128)(2,1)S(1)} collective-permute-done((bf16[512,256]{1,0:T(8,128)(2,1)S(1)}, bf16[512,256]{1,0:T(8,128)(2,1)S(1)}, u32[]{:S(2)}, u32[]{:S(2)}) %collective-permute-start.25) | collective-permute-done | bytes 262176 | tf_op jit(solution)/shard_map/ppermute | solution.py:244
  114.0 7.5 %collective-permute-done.26.c = bf16[512,256]{1,0:T(8,128)(2,1)S(1)} collective-permute-done((bf16[512,256]{1,0:T(8,128)(2,1)S(1)}, bf16[512,256]{1,0:T(8,128)(2,1)S(1)}, u32[]{:S(2)}, u32[]{:S(2)}) %collective-permute-start.26) | collective-permute-done | bytes 262176 | tf_op jit(solution)/shard_map/ppermute | solution.py:244
  121.5 0.8 in_grad_sum.1
  (27 shorter events, 0.1 us)
Async XLA Ops:
  0.6 11.0 %collective-permute-start.2 = (bf16[512,256]{1,0:T(8,128)(2,1)}, bf16[512,256]{1,0:T(8,128)(2,1)S(1)}, u32[]{:S(2)}, u32[]{:S(2)}) collective-permute-start(bf16[512,256]{1,0:T(8,128)(2,1)} %bitcast.13), channel_id=1, source_target_pairs={{0,2},{1,3},{2,0},{3,1},{4,6},{5,7},{6,4},{7,5},{8,10},{9,11},{10,... | collective-permute-start | bytes 786440 | tf_op jit(solution)/shard_map/ppermute | solution.py:244
  2.1 14.0 %collective-permute-start.1 = (bf16[512,256]{1,0:T(8,128)(2,1)}, bf16[512,256]{1,0:T(8,128)(2,1)S(1)}, u32[]{:S(2)}, u32[]{:S(2)}) collective-permute-start(bf16[512,256]{1,0:T(8,128)(2,1)} %bitcast.14), channel_id=1, source_target_pairs={{0,3},{1,0},{2,1},{3,2},{4,7},{5,4},{6,5},{7,6},{8,11},{9,8},{10,9... | collective-permute-start | bytes 786440 | tf_op jit(solution)/shard_map/ppermute | solution.py:244
  2.1 14.0 %collective-permute-start = (bf16[512,256]{1,0:T(8,128)(2,1)}, bf16[512,256]{1,0:T(8,128)(2,1)S(1)}, u32[]{:S(2)}, u32[]{:S(2)}) collective-permute-start(bf16[512,256]{1,0:T(8,128)(2,1)} %bitcast.15), channel_id=1, source_target_pairs={{0,1},{1,2},{2,3},{3,0},{4,5},{5,6},{6,7},{7,4},{8,9},{9,10},{10,1... | collective-permute-start | bytes 786440 | tf_op jit(solution)/shard_map/ppermute | solution.py:244
  16.1 1.4 %copy-start = (bf16[1024,3,256]{2,0,1:T(8,128)(2,1)S(1)}, bf16[1024,3,256]{2,0,1:T(8,128)(2,1)}, u32[]{:S(2)}) copy-start(bf16[1024,3,256]{2,0,1:T(8,128)(2,1)} %param.6) | copy-start | bytes 4718596
  17.5 0.9 copy-start.4
  18.5 23.6 %copy-start.3 = (bf16[2,4,64,256]{3,2,1,0:T(8,128)(2,1)S(1)}, bf16[2,4,64,256]{3,2,1,0:T(8,128)(2,1)}, u32[]{:S(2)}) copy-start(bf16[2,4,64,256]{3,2,1,0:T(8,128)(2,1)} %param.5) | copy-start | bytes 786436
  18.5 37.6 %copy-start.2 = (bf16[256,1024]{1,0:T(8,128)(2,1)S(1)}, bf16[256,1024]{1,0:T(8,128)(2,1)}, u32[]{:S(2)}) copy-start(bf16[256,1024]{1,0:T(8,128)(2,1)} %w.3) | copy-start | bytes 1572868
  20.7 0.7 copy-start.5
  21.3 0.6 copy-start.7
  22.0 10.6 %collective-permute-start.10 = (bf16[1,4,64,256]{3,2,1,0:T(8,128)(2,1)S(1)}, bf16[1,4,64,256]{3,2,1,0:T(8,128)(2,1)S(1)}, u32[]{:S(2)}, u32[]{:S(2)}) collective-permute-start(bf16[1,4,64,256]{3,2,1,0:T(8,128)(2,1)S(1)} %get-tuple-element.55), channel_id=1, source_target_pairs={{0,64},{64,128},{128,192},{192,0},{1,65},{65,129},{129,193},{193,1... | collective-permute-start | bytes 393224 | tf_op jit(solution)/shard_map/ppermute | solution.py:247
  25.2 14.0 %collective-permute-start.11 = (bf16[1,4,64,256]{3,2,1,0:T(8,128)(2,1)S(1)}, bf16[1,4,64,256]{3,2,1,0:T(8,128)(2,1)S(1)}, u32[]{:S(2)}, u32[]{:S(2)}) collective-permute-start(bf16[1,4,64,256]{3,2,1,0:T(8,128)(2,1)S(1)} %get-tuple-element.56), channel_id=1, source_target_pairs={{0,192},{64,0},{128,64},{192,128},{1,193},{65,1},{129,65},{193,129... | collective-permute-start | bytes 393224 | tf_op jit(solution)/shard_map/ppermute | solution.py:247
  28.3 15.3 %collective-permute-start.6 = (bf16[1,4,64,256]{3,2,1,0:T(8,128)(2,1)}, bf16[1,4,64,256]{3,2,1,0:T(8,128)(2,1)S(1)}, u32[]{:S(2)}, u32[]{:S(2)}) collective-permute-start(bf16[1,4,64,256]{3,2,1,0:T(8,128)(2,1)} %get-tuple-element.47), channel_id=1, source_target_pairs={{0,64},{64,128},{128,192},{192,0},{1,65},{65,129},{129,193},{193,1... | collective-permute-start | bytes 393224 | tf_op jit(solution)/shard_map/ppermute | solution.py:247
  29.7 13.9 %collective-permute-start.7 = (bf16[1,4,64,256]{3,2,1,0:T(8,128)(2,1)S(1)}, bf16[1,4,64,256]{3,2,1,0:T(8,128)(2,1)S(1)}, u32[]{:S(2)}, u32[]{:S(2)}) collective-permute-start(bf16[1,4,64,256]{3,2,1,0:T(8,128)(2,1)S(1)} %get-tuple-element.48), channel_id=1, source_target_pairs={{0,192},{64,0},{128,64},{192,128},{1,193},{65,1},{129,65},{193,129... | collective-permute-start | bytes 393224 | tf_op jit(solution)/shard_map/ppermute | solution.py:247
  39.3 17.8 %collective-permute-start.12 = (bf16[4,3,64,256]{3,2,1,0:T(8,128)(2,1)S(1)}, bf16[4,3,64,256]{3,2,1,0:T(8,128)(2,1)S(1)}, u32[]{:S(2)}, u32[]{:S(2)}) collective-permute-start(bf16[4,3,64,256]{3,2,1,0:T(8,128)(2,1)S(1)} %get-tuple-element.57), channel_id=1, source_target_pairs={{0,4},{4,8},{8,12},{12,16},{16,20},{20,24},{24,28},{28,32},{32,36}... | collective-permute-start | bytes 1179656 | tf_op jit(solution)/shard_map/ppermute | solution.py:250
  39.4 17.7 %collective-permute-start.13 = (bf16[4,3,64,256]{3,2,1,0:T(8,128)(2,1)S(1)}, bf16[4,3,64,256]{3,2,1,0:T(8,128)(2,1)S(1)}, u32[]{:S(2)}, u32[]{:S(2)}) collective-permute-start(bf16[4,3,64,256]{3,2,1,0:T(8,128)(2,1)S(1)} %get-tuple-element.58), channel_id=1, source_target_pairs={{0,60},{4,0},{8,4},{12,8},{16,12},{20,16},{24,20},{28,24},{32,28},... | collective-permute-start | bytes 1179656 | tf_op jit(solution)/shard_map/ppermute | solution.py:250
  42.1 15.1 %copy-start.8 = (bf16[512,128]{1,0:T(8,128)(2,1)S(1)}, bf16[512,128]{1,0:T(8,128)(2,1)}, u32[]{:S(2)}) copy-start(bf16[512,128]{1,0:T(8,128)(2,1)} %copy-done.7) | copy-start | bytes 393220
  42.1 10.6 %collective-permute-start.5 = (bf16[512,256]{1,0:T(8,128)(2,1)S(1)}, bf16[512,256]{1,0:T(8,128)(2,1)S(1)}, u32[]{:S(2)}, u32[]{:S(2)}) collective-permute-start(bf16[512,256]{1,0:T(8,128)(2,1)S(1)} %bitcast.9), channel_id=1, source_target_pairs={{0,2},{1,3},{2,0},{3,1},{4,6},{5,7},{6,4},{7,5},{8,10},{9,11},{10,... | collective-permute-start | bytes 786440 | tf_op jit(solution)/shard_map/ppermute | solution.py:244
  43.6 11.9 %collective-permute-start.4 = (bf16[512,256]{1,0:T(8,128)(2,1)S(1)}, bf16[512,256]{1,0:T(8,128)(2,1)S(1)}, u32[]{:S(2)}, u32[]{:S(2)}) collective-permute-start(bf16[512,256]{1,0:T(8,128)(2,1)S(1)} %bitcast.10), channel_id=1, source_target_pairs={{0,3},{1,0},{2,1},{3,2},{4,7},{5,4},{6,5},{7,6},{8,11},{9,8},{10,9... | collective-permute-start | bytes 786440 | tf_op jit(solution)/shard_map/ppermute | solution.py:244
  43.6 12.5 %collective-permute-start.3 = (bf16[512,256]{1,0:T(8,128)(2,1)S(1)}, bf16[512,256]{1,0:T(8,128)(2,1)S(1)}, u32[]{:S(2)}, u32[]{:S(2)}) collective-permute-start(bf16[512,256]{1,0:T(8,128)(2,1)S(1)} %bitcast.11), channel_id=1, source_target_pairs={{0,1},{1,2},{2,3},{3,0},{4,5},{5,6},{6,7},{7,4},{8,9},{9,10},{10,1... | collective-permute-start | bytes 786440 | tf_op jit(solution)/shard_map/ppermute | solution.py:244
  52.7 16.1 %collective-permute-start.8 = (bf16[4,3,64,256]{3,2,1,0:T(8,128)(2,1)S(1)}, bf16[4,3,64,256]{3,2,1,0:T(8,128)(2,1)S(1)}, u32[]{:S(2)}, u32[]{:S(2)}) collective-permute-start(bf16[4,3,64,256]{3,2,1,0:T(8,128)(2,1)S(1)} %get-tuple-element.49), channel_id=1, source_target_pairs={{0,4},{4,8},{8,12},{12,16},{16,20},{20,24},{24,28},{28,32},{32,36}... | collective-permute-start | bytes 1179656 | tf_op jit(solution)/shard_map/ppermute | solution.py:250
  55.4 13.4 %collective-permute-start.9 = (bf16[4,3,64,256]{3,2,1,0:T(8,128)(2,1)S(1)}, bf16[4,3,64,256]{3,2,1,0:T(8,128)(2,1)S(1)}, u32[]{:S(2)}, u32[]{:S(2)}) collective-permute-start(bf16[4,3,64,256]{3,2,1,0:T(8,128)(2,1)S(1)} %get-tuple-element.50), channel_id=1, source_target_pairs={{0,60},{4,0},{8,4},{12,8},{16,12},{20,16},{24,20},{28,24},{32,28},... | collective-permute-start | bytes 1179656 | tf_op jit(solution)/shard_map/ppermute | solution.py:250
  57.1 11.7 %copy-start.6 = (bf16[512,128]{1,0:T(8,128)(2,1)S(1)}, bf16[512,128]{1,0:T(8,128)(2,1)}, u32[]{:S(2)}) copy-start(bf16[512,128]{1,0:T(8,128)(2,1)} %copy-done.5) | copy-start | bytes 393220
  66.1 16.0 %collective-permute-start.21 = (bf16[4,3,64,256]{3,2,1,0:T(8,128)(2,1)S(1)}, bf16[4,3,64,256]{3,2,1,0:T(8,128)(2,1)S(1)}, u32[]{:S(2)}, u32[]{:S(2)}) collective-permute-start(bf16[4,3,64,256]{3,2,1,0:T(8,128)(2,1)S(1)} %get-tuple-element.74), channel_id=1, source_target_pairs={{0,4},{4,8},{8,12},{12,16},{16,20},{20,24},{24,28},{28,32},{32,36}... | collective-permute-start | bytes 1179656 | tf_op jit(solution)/shard_map/ppermute | solution.py:250
  66.2 15.9 %collective-permute-start.22 = (bf16[4,3,64,256]{3,2,1,0:T(8,128)(2,1)S(1)}, bf16[4,3,64,256]{3,2,1,0:T(8,128)(2,1)S(1)}, u32[]{:S(2)}, u32[]{:S(2)}) collective-permute-start(bf16[4,3,64,256]{3,2,1,0:T(8,128)(2,1)S(1)} %get-tuple-element.75), channel_id=1, source_target_pairs={{0,60},{4,0},{8,4},{12,8},{16,12},{20,16},{24,20},{28,24},{32,28},... | collective-permute-start | bytes 1179656 | tf_op jit(solution)/shard_map/ppermute | solution.py:250
  77.8 15.2 %collective-permute-start.17 = (bf16[4,3,64,256]{3,2,1,0:T(8,128)(2,1)S(1)}, bf16[4,3,64,256]{3,2,1,0:T(8,128)(2,1)S(1)}, u32[]{:S(2)}, u32[]{:S(2)}) collective-permute-start(bf16[4,3,64,256]{3,2,1,0:T(8,128)(2,1)S(1)} %get-tuple-element.66), channel_id=1, source_target_pairs={{0,4},{4,8},{8,12},{12,16},{16,20},{20,24},{24,28},{28,32},{32,36}... | collective-permute-start | bytes 1179656 | tf_op jit(solution)/shard_map/ppermute | solution.py:250
  77.8 15.1 %collective-permute-start.18 = (bf16[4,3,64,256]{3,2,1,0:T(8,128)(2,1)S(1)}, bf16[4,3,64,256]{3,2,1,0:T(8,128)(2,1)S(1)}, u32[]{:S(2)}, u32[]{:S(2)}) collective-permute-start(bf16[4,3,64,256]{3,2,1,0:T(8,128)(2,1)S(1)} %get-tuple-element.67), channel_id=1, source_target_pairs={{0,60},{4,0},{8,4},{12,8},{16,12},{20,16},{24,20},{28,24},{32,28},... | collective-permute-start | bytes 1179656 | tf_op jit(solution)/shard_map/ppermute | solution.py:250
  81.6 21.5 %copy-start.1 = (bf16[1024,3,256]{2,0,1:T(8,128)(2,1)S(1)}, bf16[1024,3,256]{2,0,1:T(8,128)(2,1)}, u32[]{:S(2)}) copy-start(bf16[1024,3,256]{2,0,1:T(8,128)(2,1)} %param.6) | copy-start | bytes 4718596
  81.6 25.2 %collective-permute-start.14 = (bf16[512,256]{1,0:T(8,128)(2,1)S(1)}, bf16[512,256]{1,0:T(8,128)(2,1)S(1)}, u32[]{:S(2)}, u32[]{:S(2)}) collective-permute-start(bf16[512,256]{1,0:T(8,128)(2,1)S(1)} %get-tuple-element.61), channel_id=1, source_target_pairs={{0,1},{1,2},{2,3},{3,0},{4,5},{5,6},{6,7},{7,4},{8,9},{9,10},{10,1... | collective-permute-start | bytes 786440 | tf_op jit(solution)/shard_map/ppermute | solution.py:244
  82.1 15.1 %collective-permute-start.23 = (bf16[1,4,64,256]{3,2,1,0:T(8,128)(2,1)S(1)}, bf16[1,4,64,256]{3,2,1,0:T(8,128)(2,1)S(1)}, u32[]{:S(2)}, u32[]{:S(2)}) collective-permute-start(bf16[1,4,64,256]{3,2,1,0:T(8,128)(2,1)S(1)} %get-tuple-element.78), channel_id=1, source_target_pairs={{0,64},{64,128},{128,192},{192,0},{1,65},{65,129},{129,193},{193,1... | collective-permute-start | bytes 393224 | tf_op jit(solution)/shard_map/ppermute | solution.py:247
  86.2 11.2 %collective-permute-start.24 = (bf16[1,4,64,256]{3,2,1,0:T(8,128)(2,1)S(1)}, bf16[1,4,64,256]{3,2,1,0:T(8,128)(2,1)S(1)}, u32[]{:S(2)}, u32[]{:S(2)}) collective-permute-start(bf16[1,4,64,256]{3,2,1,0:T(8,128)(2,1)S(1)} %get-tuple-element.79), channel_id=1, source_target_pairs={{0,192},{64,0},{128,64},{192,128},{1,193},{65,1},{129,65},{193,129... | collective-permute-start | bytes 393224 | tf_op jit(solution)/shard_map/ppermute | solution.py:247
  93.1 7.3 %collective-permute-start.19 = (bf16[1,4,64,256]{3,2,1,0:T(8,128)(2,1)S(1)}, bf16[1,4,64,256]{3,2,1,0:T(8,128)(2,1)S(1)}, u32[]{:S(2)}, u32[]{:S(2)}) collective-permute-start(bf16[1,4,64,256]{3,2,1,0:T(8,128)(2,1)S(1)} %get-tuple-element.70), channel_id=1, source_target_pairs={{0,64},{64,128},{128,192},{192,0},{1,65},{65,129},{129,193},{193,1... | collective-permute-start | bytes 393224 | tf_op jit(solution)/shard_map/ppermute | solution.py:247
  96.4 6.6 %collective-permute-start.20 = (bf16[1,4,64,256]{3,2,1,0:T(8,128)(2,1)S(1)}, bf16[1,4,64,256]{3,2,1,0:T(8,128)(2,1)S(1)}, u32[]{:S(2)}, u32[]{:S(2)}) collective-permute-start(bf16[1,4,64,256]{3,2,1,0:T(8,128)(2,1)S(1)} %get-tuple-element.71), channel_id=1, source_target_pairs={{0,192},{64,0},{128,64},{192,128},{1,193},{65,1},{129,65},{193,129... | collective-permute-start | bytes 393224 | tf_op jit(solution)/shard_map/ppermute | solution.py:247
  97.3 13.7 %collective-permute-start.15 = (bf16[512,256]{1,0:T(8,128)(2,1)S(1)}, bf16[512,256]{1,0:T(8,128)(2,1)S(1)}, u32[]{:S(2)}, u32[]{:S(2)}) collective-permute-start(bf16[512,256]{1,0:T(8,128)(2,1)S(1)} %get-tuple-element.62), channel_id=1, source_target_pairs={{0,3},{1,0},{2,1},{3,2},{4,7},{5,4},{6,5},{7,6},{8,11},{9,8},{10,9... | collective-permute-start | bytes 786440 | tf_op jit(solution)/shard_map/ppermute | solution.py:244
  97.4 13.6 %collective-permute-start.16 = (bf16[512,256]{1,0:T(8,128)(2,1)S(1)}, bf16[512,256]{1,0:T(8,128)(2,1)S(1)}, u32[]{:S(2)}, u32[]{:S(2)}) collective-permute-start(bf16[512,256]{1,0:T(8,128)(2,1)S(1)} %get-tuple-element.63), channel_id=1, source_target_pairs={{0,2},{1,3},{2,0},{3,1},{4,6},{5,7},{6,4},{7,5},{8,10},{9,11},{10,... | collective-permute-start | bytes 786440 | tf_op jit(solution)/shard_map/ppermute | solution.py:244
  104.7 9.3 %collective-permute-start.25 = (bf16[512,256]{1,0:T(8,128)(2,1)S(1)}, bf16[512,256]{1,0:T(8,128)(2,1)S(1)}, u32[]{:S(2)}, u32[]{:S(2)}) collective-permute-start(bf16[512,256]{1,0:T(8,128)(2,1)S(1)} %get-tuple-element.81), channel_id=1, source_target_pairs={{0,1},{1,2},{2,3},{3,0},{4,5},{5,6},{6,7},{7,4},{8,9},{9,10},{10,1... | collective-permute-start | bytes 786440 | tf_op jit(solution)/shard_map/ppermute | solution.py:244
  105.2 16.3 %collective-permute-start.26 = (bf16[512,256]{1,0:T(8,128)(2,1)S(1)}, bf16[512,256]{1,0:T(8,128)(2,1)S(1)}, u32[]{:S(2)}, u32[]{:S(2)}) collective-permute-start(bf16[512,256]{1,0:T(8,128)(2,1)S(1)} %get-tuple-element.82), channel_id=1, source_target_pairs={{0,3},{1,0},{2,1},{3,2},{4,7},{5,4},{6,5},{7,6},{8,11},{9,8},{10,9... | collective-permute-start | bytes 786440 | tf_op jit(solution)/shard_map/ppermute | solution.py:244
  106.8 14.7 %collective-permute-start.27 = (bf16[512,256]{1,0:T(8,128)(2,1)S(1)}, bf16[512,256]{1,0:T(8,128)(2,1)S(1)}, u32[]{:S(2)}, u32[]{:S(2)}) collective-permute-start(bf16[512,256]{1,0:T(8,128)(2,1)S(1)} %get-tuple-element.83), channel_id=1, source_target_pairs={{0,2},{1,3},{2,0},{3,1},{4,6},{5,7},{6,4},{7,5},{8,10},{9,11},{10,... | collective-permute-start | bytes 786440 | tf_op jit(solution)/shard_map/ppermute | solution.py:244

commit v3 on v2

--- a/solution.py
+++ b/solution.py
@@ -1,3 +1,4 @@
+import functools
 import math
 
 import jax
@@ -18,9 +19,9 @@
     return lax.dot_general(a, b, dims, preferred_element_type=F32)
 
 
-def attend_body(valid, q, b, own, tmb, tma, hb, ha,
+def attend_body(half, valid, q, b, f0, f1, tmb, tma, hb, ha,
                 att, dq, g_own, g_tmb, g_tma, g_hb, g_ha,
-                ks, vs, kt, vt, dk, dv, s_buf, t_buf, p_buf, d_buf, bias):
+                ks, vs, kt, vt, dk, dv, s_buf0, s_buf1, p_buf0, p_buf1, d_buf0, d_buf1, bias):
     def put(frame, row, block):
         rows = block.shape[0]
         block = block.reshape(rows * 64, 256)
@@ -31,10 +32,9 @@
     for i in range(4):
         put(i, 0, hb[i])
         put(i, 7, ha[i])
-    put(0, 3, tmb[0])
-    put(1, 3, own[0])
-    put(2, 3, own[1])
-    put(3, 3, tma[0])
+    lanes = pl.ds(half * 256, 256)
+    for i, ref in enumerate((tmb, f0, f1, tma)):
+        put(i, 3, ref[0, :, :, lanes])
 
     eye = jnp.where(
         lax.broadcasted_iota(jnp.int32, (128, 128), 0) == lax.broadcasted_iota(jnp.int32, (128, 128), 1),
@@ -45,10 +45,8 @@
     )
     for i in range(5):
         at = pl.ds(i * 512, 512)
-        kt[:, at] = dot(eye, ks[at, :], NT).astype(BF16)
-        vt[:, at] = dot(eye, vs[at, :], NT).astype(BF16)
-    dk[...] = jnp.zeros_like(dk)
-    dv[...] = jnp.zeros_like(dv)
+        kt[:, at] = ks[at, :].T
+        vt[:, at] = vs[at, :].T
     krow = lax.broadcasted_iota(jnp.int32, (64, 256), 0)
     lane = lax.broadcasted_iota(jnp.int32, (64, 256), 1)
     band = jnp.abs(krow - lane % 64) <= 3
@@ -66,24 +64,42 @@
         out = outT.T
         return jnp.where(first_head, out[0:128], out[128:256])
 
-    def group(g, _):
+    bufs = ((s_buf0, p_buf0, d_buf0), (s_buf1, p_buf1, d_buf1))
+
+    def span(g, i):
         f, r = g // 2, (g % 2) * 2
-        mine = pl.ds(pl.multiple_of(g * 128, 128), 128)
-        qbd = spread(q[mine, :])
-        bbd = spread(b[mine, :])
-
-        def keys_of(i):
-            return pl.ds(pl.multiple_of(((f + i) * 10 + r) * 64, 128), 512)
-
+        return ((f + i) * 10 + r) * 64
+
+    def keys_of(g, i):
+        return pl.ds(span(g, i), 512)
+
+    def add_to(ref, g, i, term):
+        f, r = g // 2, (g % 2) * 2
+        seen = 6 if r == 2 else 0
+        if f == 1 and i < 2:
+            seen = 8
+        at = span(g, i)
+        if seen:
+            ref[pl.ds(at, seen * 64), :] += term[: seen * 64]
+        if seen < 8:
+            ref[pl.ds(at + seen * 64, 512 - seen * 64), :] = term[seen * 64:]
+
+    def scores(g):
+        s_buf = bufs[g % 2][0]
+        f, r = g // 2, (g % 2) * 2
+        qbd = spread(q[pl.ds(g * 128, 128), :])
         top = jnp.full((64, 256), NEG_FILL, F32)
         for i in range(3):
-            sc = dot(ks[keys_of(i), :], qbd, NT)
+            sc = dot(ks[keys_of(g, i), :], qbd, NT)
             for j in range(8):
                 kind = 2 if j == 0 else 3 if j == 7 else 1
                 v = sc[j * 64:(j + 1) * 64] + bias[valid[f + i, r + j] * kind]
                 s_buf[pl.ds((i * 8 + j) * 64, 64), :] = v
                 top = jnp.maximum(top, v)
-        m = jnp.max(top, axis=0, keepdims=True)
+        return jnp.max(top, axis=0, keepdims=True)
+
+    def weights(g, m):
+        s_buf, p_buf, _ = bufs[g % 2]
         tot = jnp.zeros((64, 256), F32)
         for j in range(24):
             at = pl.ds(j * 64, 64)
@@ -91,35 +107,53 @@
             s_buf[at, :] = e
             tot = tot + e
         inv = 1.0 / jnp.sum(tot, axis=0, keepdims=True)
-        cen = jnp.zeros((64, 256), F32)
+        for j in range(24):
+            at = pl.ds(j * 64, 64)
+            p_buf[at, :] = (s_buf[at, :] * inv).astype(BF16)
+        return inv
+
+    def values(g):
+        p_buf = bufs[g % 2][1]
+        mine = pl.ds(g * 128, 128)
+        bbd = spread(b[mine, :])
+        outT = jnp.zeros((128, 256), F32)
         for i in range(3):
-            sl = dot(vs[keys_of(i), :], bbd, NT)
+            pb = p_buf[pl.ds(i * 512, 512), :]
+            outT = outT + dot(vt[:, keys_of(g, i)], pb)
+            add_to(dv, g, i, dot(pb, bbd))
+        att[mine, :] = gather(outT).astype(BF16)
+        return jnp.sum(outT * dot(eye, bbd, NT), axis=0, keepdims=True)
+
+    def slopes(g, inv, c):
+        s_buf, _, d_buf = bufs[g % 2]
+        bbd = spread(b[pl.ds(g * 128, 128), :])
+        for i in range(3):
+            sl = dot(vs[keys_of(g, i), :], bbd, NT)
             for j in range(8):
                 at = pl.ds((i * 8 + j) * 64, 64)
-                p = s_buf[at, :] * inv
-                s_buf[at, :] = p
-                p_buf[at, :] = p.astype(BF16)
-                x = sl[j * 64:(j + 1) * 64]
-                t_buf[at, :] = x
-                cen = cen + p * x
-        c = jnp.sum(cen, axis=0, keepdims=True)
-        for j in range(24):
-            at = pl.ds(j * 64, 64)
-            d_buf[at, :] = (s_buf[at, :] * (t_buf[at, :] - c)).astype(BF16)
-        outT = jnp.zeros((128, 256), F32)
+                d_buf[at, :] = (s_buf[at, :] * inv * (sl[j * 64:(j + 1) * 64] - c)).astype(BF16)
+
+    def grads(g):
+        d_buf = bufs[g % 2][2]
+        mine = pl.ds(g * 128, 128)
+        qbd = spread(q[mine, :])
         dqT = jnp.zeros((128, 256), F32)
         for i in range(3):
-            at = pl.ds(i * 512, 512)
-            pb, db = p_buf[at, :], d_buf[at, :]
-            outT = outT + dot(vt[:, keys_of(i)], pb)
-            dqT = dqT + dot(kt[:, keys_of(i)], db)
-            dv[keys_of(i), :] += dot(pb, bbd)
-            dk[keys_of(i), :] += dot(db, qbd)
-        att[mine, :] = gather(outT).astype(BF16)
+            db = d_buf[pl.ds(i * 512, 512), :]
+            dqT = dqT + dot(kt[:, keys_of(g, i)], db)
+            add_to(dk, g, i, dot(db, qbd))
         dq[mine, :] = (gather(dqT) * 0.125).astype(BF16)
-        return 0
-
-    lax.fori_loop(0, 4, group, 0)
+
+    m = scores(0)
+    for g in range(4):
+        inv = weights(g, m)
+        if g > 0:
+            grads(g - 1)
+        if g < 3:
+            m = scores(g + 1)
+        c = values(g)
+        slopes(g, inv, c)
+    grads(3)
 
     def take(frame, row, rows, out):
         at = pl.ds((frame * 10 + row) * 64, rows * 64)
@@ -135,27 +169,33 @@
     g_tma[0] = take(3, 3, 4, g_tma)
 
 
-def project_body(idx, x0, x1, x2, x3, w, q0, q1, own0, own1, f00, f10, f01, f11):
+def stage_body(w, x, w_out, x_out):
+    w_out[...] = w[...]
+    x_out[...] = x[...]
+
+
+def project_body(idx, x0, x1, x2, x3, w, f0, f1):
     acc = None
     for i, x in enumerate((x0, x1, x2, x3)):
         at = pl.ds(pl.multiple_of(idx[i] * 256, 256), 256)
-        part = [dot(x[...], w[n, at, :]) for n in range(3)]
+        part = [dot(x[...], w[n, at, :]) for n in (1, 2)]
         acc = part if acc is None else [a + b for a, b in zip(acc, part)]
-    query, keys, values = (a.astype(BF16) for a in acc)
-    query = query * jnp.asarray(0.125, BF16)
-    for half, (q, own, f0, f1) in enumerate(((q0, own0, f00, f10), (q1, own1, f01, f11))):
+    keys, values = (a.astype(BF16) for a in acc)
+    halves = []
+    for half in range(2):
         at = slice(half * 128, half * 128 + 128)
-        q[...] = query[:, at]
-        kv = jnp.concatenate([keys[:, at], values[:, at]], axis=1).reshape(2, 4, 64, 256)
-        own[...] = kv
-        f0[...] = kv[0:1]
-        f1[...] = kv[1:2]
-
-
-def edges_body(tmb, own, tma, lo, hi):
-    for i, (ref, at) in enumerate(((tmb, 0), (own, 0), (own, 1), (tma, 0))):
-        lo[i] = ref[at, 0:3]
-        hi[i] = ref[at, 1:4]
+        halves += [keys[:, at], values[:, at]]
+    kv = jnp.concatenate(halves, axis=1).reshape(2, 4, 64, 512)
+    f0[...] = kv[0:1]
+    f1[...] = kv[1:2]
+
+
+def edges_body(tmb, f0, f1, tma, lo0, hi0, lo1, hi1):
+    for half, (lo, hi) in enumerate(((lo0, hi0), (lo1, hi1))):
+        lanes = pl.ds(half * 256, 256)
+        for i, ref in enumerate((tmb, f0, f1, tma)):
+            lo[i] = ref[0, 0:3, :, lanes]
+            hi[i] = ref[0, 1:4, :, lanes]
 
 
 def fold_body(g_tmb, g_tma, r_hb, r_ha, s_tmb, s_tma, acc):
@@ -164,6 +204,16 @@
         acc[0, 0:3] += r_hb[at].astype(F32)
         acc[0, 1:4] += r_ha[at].astype(F32)
         s[...] = acc[...].astype(BF16)
+
+
+def query_body(idx, x0, x1, x2, x3, w, out0, out1):
+    acc = None
+    for i, x in enumerate((x0, x1, x2, x3)):
+        part = dot(x[...], w[0, pl.ds(pl.multiple_of(idx[i] * 256, 256), 256), :])
+        acc = part if acc is None else acc + part
+    query = acc.astype(BF16) * jnp.asarray(0.125, BF16)
+    out0[...] = query[:, :128]
+    out1[...] = query[:, 128:]
 
 
 def back_body(idx, x0, x1, x2, x3, w, out0, out1):
@@ -208,14 +258,13 @@
     out[...] = total.astype(BF16).reshape(out.shape)
 
 
-def local_call(body, outs, idx, arrays, scratch=(), flops=0, name=None, limit=12):
+def local_call(body, outs, idx, arrays, scratch=(), flops=0, name=None, limit=8):
     vm = pl.BlockSpec(memory_space=pltpu.VMEM)
     specs = [vm] * len(arrays)
     args = list(arrays)
     if idx is not None:
         specs = [pl.BlockSpec(memory_space=pltpu.SMEM)] + specs
         args = [idx] + args
-    size = sum(math.prod(a.shape) * a.dtype.itemsize for a in list(arrays) + list(outs))
     return pl.pallas_call(
         body,
         out_shape=tuple(outs),
@@ -223,7 +272,7 @@
         out_specs=(vm,) * len(outs),
         scratch_shapes=list(scratch),
         compiler_params=pltpu.CompilerParams(vmem_limit_bytes=limit * MIB),
-        cost_estimate=pl.CostEstimate(flops=flops, bytes_accessed=size, transcendentals=0),
+        cost_estimate=pl.CostEstimate(flops=flops, bytes_accessed=0, transcendentals=0),
         name=name,
     )(*args)
 
@@ -249,34 +298,41 @@
     def rows(array, by):
         return lax.ppermute(array, "height", [(i, (i + by) % n_h) for i in range(n_h)])
 
+    pair, frame, edge = (2, 4, 64, 256), (1, 4, 64, 256), (4, 3, 64, 256)
+    half = S((512, 128), BF16)
+    piece = S((512, 256), BF16)
     tok = tokens.reshape(512, 256)
+    cot = cotangent.reshape(512, 256)
+    t_parts = (ring(tok, 1), ring(tok, -1), ring(tok, 2))
     flat = jnp.transpose(w_qkv, (1, 0, 2))
-    t_parts = (ring(tok, 1), ring(tok, -1), ring(tok, 2))
-    half = S((512, 128), BF16)
-    pair, frame, edge = (2, 4, 64, 256), (1, 4, 64, 256), (4, 3, 64, 256)
-    q0, q1, own0, own1, f00, f10, f01, f11 = local_call(
-        project_body,
-        (half, half, S(pair, BF16), S(pair, BF16)) + (S(frame, BF16),) * 4,
-        idx, (tok, *t_parts, flat), flops=2 * 512 * 1024 * 768, name="project",
-    )
-    cot, _ = lax.optimization_barrier((cotangent.reshape(512, 256), q0))
-
-    def surround(own, f0, f1):
-        tmb, tma = frames(f1, 1), frames(f0, -1)
-        lo, hi = local_call(edges_body, (S(edge, BF16),) * 2, None, (tmb, own, tma), name="edges")
-        return own, tmb, tma, rows(hi, 1), rows(lo, -1)
-
-    around0 = surround(own0, f00, f10)
-    c_parts = (ring(cot, 1), ring(cot, -1), ring(cot, 2))
-    around1 = surround(own1, f01, f11)
+    w_near, tok_near = local_call(stage_body, (S(flat.shape, BF16), piece), None, (flat, tok), name="stage")
+    wide = S((1, 4, 64, 512), BF16)
+    f0, f1 = local_call(
+        project_body, (wide, wide),
+        idx, (tok_near, *t_parts, w_near), name="project",
+    )
+    tmb, tma = frames(f1, 1), frames(f0, -1)
+    tok_late, _ = lax.optimization_barrier((tok_near, f0))
+    q0, q1 = local_call(
+        query_body, (half, half), idx, (tok_late, *t_parts, w_near), name="query",
+    )
+    cot_late, _ = lax.optimization_barrier((cot, f0))
+    c_parts = (ring(cot_late, 1), ring(cot_late, -1), ring(cot_late, 2))
+    tmb, tma, c_parts = lax.optimization_barrier((tmb, tma, c_parts))
     b0, b1 = local_call(
         back_body, (half, half), idx, (cot, *c_parts, w_out),
-        flops=2 * 512 * 1024 * 256, name="back",
-    )
-
-    def attend(q, b, around):
+        name="back",
+    )
+    lo0, hi0, lo1, hi1 = local_call(
+        edges_body, (S(edge, BF16),) * 4, None, (tmb, f0, f1, tma), name="edges"
+    )
+    hb0, ha0 = rows(hi0, 1), rows(lo0, -1)
+    hi1, lo1, hb0, ha0 = lax.optimization_barrier((hi1, lo1, hb0, ha0))
+    hb1, ha1 = rows(hi1, 1), rows(lo1, -1)
+
+    def attend(n, q, b, *around):
         return local_call(
-            attend_body,
+            functools.partial(attend_body, n),
             (half, half, S(pair, F32), S(frame, F32), S(frame, F32), S(edge, BF16), S(edge, BF16)),
             valid, (q, b, *around),
             scratch=[
@@ -285,9 +341,10 @@
                 pltpu.VMEM((2560, 128), F32), pltpu.VMEM((2560, 128), F32),
                 pltpu.VMEM((1536, 256), F32), pltpu.VMEM((1536, 256), F32),
                 pltpu.VMEM((1536, 256), BF16), pltpu.VMEM((1536, 256), BF16),
+                pltpu.VMEM((1536, 256), BF16), pltpu.VMEM((1536, 256), BF16),
                 pltpu.VMEM((4, 64, 256), F32),
             ],
-            flops=4 * 6 * 2 * 1536 * 256 * 256 * 2, name="attend", limit=24,
+            flops=4 * 6 * 2 * 1536 * 256 * 256 * 2, name="attend", limit=20,
         )
 
     def settle(g_tmb, g_tma, g_hb, g_ha):
@@ -296,16 +353,17 @@
             fold_body, (S(frame, BF16),) * 2, None, (g_tmb, g_tma, r_hb, r_ha),
             scratch=[pltpu.VMEM(frame, F32)], name="fold",
         )
-        return r_hb, r_ha, frames(s_tma, 1), frames(s_tmb, -1)
-
-    att0, dq0, g_own0, *g0 = attend(q0, b0, around0)
-    att1, dq1, g_own1, *g1 = attend(q1, b1, around1)
+        return r_hb, r_ha, frames(s_tma, 1), frames(s_tmb, -1), s_tma
+
+    att0, dq0, g_own0, *g0 = attend(0, q0, b0, f0, f1, tmb, tma, hb0, ha0)
+    att1, dq1, g_own1, *g1 = attend(1, q1, b1, f0, f1, tmb, tma, hb1, ha1)
     back0 = settle(*g0)
-    back1 = settle(*g1)
-    piece = S((512, 256), BF16)
+    att0, _ = lax.optimization_barrier((att0, back0[4]))
+    back0 = back0[:4]
+    back1 = settle(*g1)[:4]
     parts = (S((512, 256), F32), piece, piece, piece)
     m0, m1, m2, m3 = local_call(
-        mixed_body, parts, idx_out, (att0, att1, w_out), flops=2 * 512 * 1024 * 256, name="mix",
+        mixed_body, parts, idx_out, (att0, att1, w_out), name="mix",
     )
     out = (S((2, 4, 64, 256), BF16),)
     (mixed,) = local_call(
@@ -313,7 +371,7 @@
     )
     e0, e1, e2, e3 = local_call(
         grad_body, parts, idx_out, (dq0, g_own0, *back0, dq1, g_own1, *back1, flat),
-        scratch=[pltpu.VMEM(pair, F32)], flops=2 * 512 * 1024 * 768, name="in_grad", limit=16,
+        scratch=[pltpu.VMEM(pair, F32)], name="in_grad", limit=14,
     )
     (in_grad,) = local_call(
         sum_body, out, None, (e0, ring(e1, 1), ring(e2, -1), ring(e3, 2)), name="in_grad_sum"

time: 124 us -> 115 us (0.927); the launches traced: 122 us -> 115 us
  starting transfers between devices: 43.6 us -> 38 us
  Pallas kernels: 25.6 us -> 22.3 us
  waiting for transfers between devices: 48.4 us -> 51.1 us
  local copies, waits for them, and re-layouts: 3.68 us -> 2.37 us
    ppermute x8, waiting for transfers between devices: 6.65 us -> 13.6 us  [rows(): lax.ppermute(array, 'height', [(i, (i + by) % n_h) for i in range(n_h)])]
    ppermute x12, waiting for transfers between devices: 31.2 us -> 26.9 us  [ring(): lax.ppermute(array, 'tensor', [(i, (i + by) % n_x) for i in range(n_x)])]
    ppermute x8 -> x6, starting transfers between devices: 18.9 us -> 14.8 us  [frames(): return lax.ppermute(array, 'tm', [(i, (i + by) % n_t) for i in range(n_t)])]
    ppermute x12, starting transfers between devices: 16 us -> 12.1 us  [ring(): lax.ppermute(array, 'tensor', [(i, (i + by) % n_x) for i in range(n_x)])]
    pallas_call x12 -> x13, Pallas kernels: 25.6 us -> 22.3 us  [local_call(): pl.pallas_call(body, out_shape=tuple(outs), in_specs=specs, out_specs=(vm...]
    ppermute x8, starting transfers between devices: 8.78 us -> 11 us  [rows(): lax.ppermute(array, 'height', [(i, (i + by) % n_h) for i in range(n_h)])]
    unnamed x18 -> x10, local copies, waits for them, and re-layouts: 3.68 us -> 2.37 us
    ppermute x8 -> x6, waiting for transfers between devices: 10.6 us -> 10.6 us  [frames(): return lax.ppermute(array, 'tm', [(i, (i + by) % n_t) for i in range(n_t)])]
  transfers between devices with their start and end apart: 28 -> 26, of which waited for: 12 -> 11; matrix products, arithmetic and copies ran while one was open for 0% -> 0% of each run, Pallas kernels for 18% -> 17%
where the time goes in v3:
time: 115 us
  waiting for transfers between devices  51.1 us (44%)
  starting transfers between devices  38 us (33%)
  Pallas kernels  22.3 us (19%)
  local copies, waits for them, and re-layouts  2.37 us (2%)
    ppermute x12, waiting for transfers between devices, ring(): lax.ppermute(array, 'tensor', [(i, (i + by) % n_x) for i in range(n_x)])  26.9 us
    pallas_call x13, Pallas kernels, local_call(): pl.pallas_call(body, out_shape=tuple(outs), in_specs=specs, out_specs=(vm...  22.3 us
    ppermute x6, starting transfers between devices, frames(): return lax.ppermute(array, 'tm', [(i, (i + by) % n_t) for i in range(n_t)])  14.8 us
    ppermute x8, waiting for transfers between devices, rows(): lax.ppermute(array, 'height', [(i, (i + by) % n_h) for i in range(n_h)])  13.6 us
    ppermute x12, starting transfers between devices, ring(): lax.ppermute(array, 'tensor', [(i, (i + by) % n_x) for i in range(n_x)])  12.1 us
    ppermute x8, starting transfers between devices, rows(): lax.ppermute(array, 'height', [(i, (i + by) % n_h) for i in range(n_h)])  11 us
    ppermute x6, waiting for transfers between devices, frames(): return lax.ppermute(array, 'tm', [(i, (i + by) % n_t) for i in range(n_t)])  10.6 us
    unnamed x10, local copies, waits for them, and re-layouts  2.37 us
  transfers between devices with their start and end apart: 26, of which 11 were waited for; matrix products, arithmetic and copies ran while one was open for 0% of the time, Pallas kernels for 17%

profile of v3, /device:TPU:22, one launch (start us, length us, event | category | flops | bytes accessed | tf_op | source)
XLA Modules:
  0.0 114.7 jit_solution(12396186000303906581)
XLA Ops:
  0.6 0.6 collective-permute-start
  1.2 1.5 %collective-permute-start.1 = (bf16[512,256]{1,0:T(8,128)(2,1)}, bf16[512,256]{1,0:T(8,128)(2,1)S(1)}, u32[]{:S(2)}, u32[]{:S(2)}) collective-permute-start(bf16[512,256]{1,0:T(8,128)(2,1)} %bitcast.10), channel_id=1, source_target_pairs={{0,3},{1,0},{2,1},{3,2},{4,7},{5,4},{6,5},{7,6},{8,11},{9,8},{10,9... | collective-permute-start | bytes 786440 | tf_op jit(solution)/shard_map/ppermute | solution.py:293
  2.7 1.4 %collective-permute-start.2 = (bf16[512,256]{1,0:T(8,128)(2,1)}, bf16[512,256]{1,0:T(8,128)(2,1)S(1)}, u32[]{:S(2)}, u32[]{:S(2)}) collective-permute-start(bf16[512,256]{1,0:T(8,128)(2,1)} %bitcast.11), channel_id=1, source_target_pairs={{0,2},{1,3},{2,0},{3,1},{4,6},{5,7},{6,4},{7,5},{8,10},{9,11},{10,... | collective-permute-start | bytes 786440 | tf_op jit(solution)/shard_map/ppermute | solution.py:293
  4.1 1.4 %copy-done = bf16[1024,3,256]{2,0,1:T(8,128)(2,1)S(1)} copy-done((bf16[1024,3,256]{2,0,1:T(8,128)(2,1)S(1)}, bf16[1024,3,256]{2,0,1:T(8,128)(2,1)}, u32[]{:S(2)}) %copy-start) | copy-done | bytes 1572888
  5.5 0.9 copy-done.3
  6.5 0.1 stage.1
  6.6 0.0 copy-start.4
  6.7 0.1 add_add_fusion.1.idx
  6.7 3.4 %collective-permute-done.x1 = bf16[512,256]{1,0:T(8,128)(2,1)S(1)} collective-permute-done((bf16[512,256]{1,0:T(8,128)(2,1)}, bf16[512,256]{1,0:T(8,128)(2,1)S(1)}, u32[]{:S(2)}, u32[]{:S(2)}) %collective-permute-start) | collective-permute-done | bytes 262176 | tf_op jit(solution)/shard_map/ppermute | solution.py:293
  10.1 5.9 %collective-permute-done.1.x2 = bf16[512,256]{1,0:T(8,128)(2,1)S(1)} collective-permute-done((bf16[512,256]{1,0:T(8,128)(2,1)}, bf16[512,256]{1,0:T(8,128)(2,1)S(1)}, u32[]{:S(2)}, u32[]{:S(2)}) %collective-permute-start.1) | collective-permute-done | bytes 262176 | tf_op jit(solution)/shard_map/ppermute | solution.py:293
  16.0 0.0 collective-permute-done.2.x3
  16.0 1.3 %project.1 = (bf16[1,4,64,512]{3,2,1,0:T(8,128)(2,1)S(1)}, bf16[1,4,64,512]{3,2,1,0:T(8,128)(2,1)S(1)}) custom-call(s32[4]{0:T(128)S(1)} %add_add_fusion.1.idx, bf16[512,256]{1,0:T(8,128)(2,1)S(1)} %get-tuple-element.55.x0, bf16[512,256]{1,0:T(8,128)(2,1)S(1)} %collective-permute-done.x1, bf16[512,256]{1,0:T(8,128)(2,1)S(1)} %collective-permute-done.1.x2, ...), custom_call_target="tpu_custom_call" | custom-call | tf_op jit(solution)/shard_map/project/pallas_call | solution.py:268
  17.3 3.3 %collective-permute-start.3 = (bf16[1,4,64,512]{3,2,1,0:T(8,128)(2,1)S(1)}, bf16[1,4,64,512]{3,2,1,0:T(8,128)(2,1)}, u32[]{:S(2)}, u32[]{:S(2)}) collective-permute-start(bf16[1,4,64,512]{3,2,1,0:T(8,128)(2,1)S(1)} %get-tuple-element.57.f1), channel_id=1, source_target_pairs={{0,64},{64,128},{128,192},{192,0},{1,65},{65,129},{129,193},{193,1... | collective-permute-start | bytes 786440 | tf_op jit(solution)/shard_map/ppermute | solution.py:296
  20.6 3.1 %collective-permute-start.4 = (bf16[1,4,64,512]{3,2,1,0:T(8,128)(2,1)S(1)}, bf16[1,4,64,512]{3,2,1,0:T(8,128)(2,1)}, u32[]{:S(2)}, u32[]{:S(2)}) collective-permute-start(bf16[1,4,64,512]{3,2,1,0:T(8,128)(2,1)S(1)} %get-tuple-element.54.f0), channel_id=1, source_target_pairs={{0,192},{64,0},{128,64},{192,128},{1,193},{65,1},{129,65},{193,129... | collective-permute-start | bytes 786440 | tf_op jit(solution)/shard_map/ppermute | solution.py:296
  23.7 1.3 %collective-permute-start.5 = (bf16[512,256]{1,0:T(8,128)(2,1)S(1)}, bf16[512,256]{1,0:T(8,128)(2,1)}, u32[]{:S(2)}, u32[]{:S(2)}) collective-permute-start(bf16[512,256]{1,0:T(8,128)(2,1)S(1)} %bitcast.13), channel_id=1, source_target_pairs={{0,1},{1,2},{2,3},{3,0},{4,5},{5,6},{6,7},{7,4},{8,9},{9,10},{10,1... | collective-permute-start | bytes 786440 | tf_op jit(solution)/shard_map/ppermute | solution.py:293
  25.0 0.8 collective-permute-start.6
  25.7 1.8 %collective-permute-start.7 = (bf16[512,256]{1,0:T(8,128)(2,1)S(1)}, bf16[512,256]{1,0:T(8,128)(2,1)}, u32[]{:S(2)}, u32[]{:S(2)}) collective-permute-start(bf16[512,256]{1,0:T(8,128)(2,1)S(1)} %bitcast.15), channel_id=1, source_target_pairs={{0,2},{1,3},{2,0},{3,1},{4,6},{5,7},{6,4},{7,5},{8,10},{9,11},{10,... | collective-permute-start | bytes 786440 | tf_op jit(solution)/shard_map/ppermute | solution.py:293
  27.6 3.0 %collective-permute-done.3.tmb = bf16[1,4,64,512]{3,2,1,0:T(8,128)(2,1)} collective-permute-done((bf16[1,4,64,512]{3,2,1,0:T(8,128)(2,1)S(1)}, bf16[1,4,64,512]{3,2,1,0:T(8,128)(2,1)}, u32[]{:S(2)}, u32[]{:S(2)}) %collective-permute-start.3) | collective-permute-done | bytes 262176 | tf_op jit(solution)/shard_map/ppermute | solution.py:296
  30.6 4.8 %collective-permute-done.4.tma = bf16[1,4,64,512]{3,2,1,0:T(8,128)(2,1)} collective-permute-done((bf16[1,4,64,512]{3,2,1,0:T(8,128)(2,1)S(1)}, bf16[1,4,64,512]{3,2,1,0:T(8,128)(2,1)}, u32[]{:S(2)}, u32[]{:S(2)}) %collective-permute-start.4) | collective-permute-done | bytes 262176 | tf_op jit(solution)/shard_map/ppermute | solution.py:296
  35.4 3.1 %collective-permute-done.6.x2 = bf16[512,256]{1,0:T(8,128)(2,1)} collective-permute-done((bf16[512,256]{1,0:T(8,128)(2,1)S(1)}, bf16[512,256]{1,0:T(8,128)(2,1)}, u32[]{:S(2)}, u32[]{:S(2)}) %collective-permute-start.6) | collective-permute-done | bytes 262176 | tf_op jit(solution)/shard_map/ppermute | solution.py:293
  38.5 1.1 edges.1
  39.7 0.0 copy-start.2
  39.7 0.1 collective-permute-start.8
  39.8 2.6 %collective-permute-start.9 = (bf16[4,3,64,256]{3,2,1,0:T(8,128)(2,1)S(1)}, bf16[4,3,64,256]{3,2,1,0:T(8,128)(2,1)S(1)}, u32[]{:S(2)}, u32[]{:S(2)}) collective-permute-start(bf16[4,3,64,256]{3,2,1,0:T(8,128)(2,1)S(1)} %get-tuple-element.68), channel_id=1, source_target_pairs={{0,60},{4,0},{8,4},{12,8},{16,12},{20,16},{24,20},{28,24},{32,28},... | collective-permute-start | bytes 1179656 | tf_op jit(solution)/shard_map/ppermute | solution.py:299
  42.4 0.1 and_convert_fusion.valid
  42.5 1.0 query.1
  43.5 1.6 %back.1 = (bf16[512,128]{1,0:T(8,128)(2,1)S(1)}, bf16[512,128]{1,0:T(8,128)(2,1)S(1)}) custom-call(s32[4]{0:T(128)S(1)} %add_add_fusion.1.idx, bf16[512,256]{1,0:T(8,128)(2,1)S(1)} %bitcast.16, bf16[512,256]{1,0:T(8,128)(2,1)} %collective-permute-done.5.x1, bf16[512,256]{1,0:T(8,128)(2,1)} %collective-permute-done.6.x2, ...), custom_call_target="tpu_custom_call" | custom-call | tf_op jit(solution)/shard_map/back/pallas_call | solution.py:268
  45.1 6.7 %collective-permute-done.8.hb = bf16[4,3,64,256]{3,2,1,0:T(8,128)(2,1)S(1)} collective-permute-done((bf16[4,3,64,256]{3,2,1,0:T(8,128)(2,1)S(1)}, bf16[4,3,64,256]{3,2,1,0:T(8,128)(2,1)S(1)}, u32[]{:S(2)}, u32[]{:S(2)}) %collective-permute-start.8) | collective-permute-done | bytes 393248 | tf_op jit(solution)/shard_map/ppermute | solution.py:299
  51.8 0.0 collective-permute-done.9.ha
  51.8 0.1 collective-permute-start.12
  51.9 2.5 %collective-permute-start.13 = (bf16[4,3,64,256]{3,2,1,0:T(8,128)(2,1)S(1)}, bf16[4,3,64,256]{3,2,1,0:T(8,128)(2,1)S(1)}, u32[]{:S(2)}, u32[]{:S(2)}) collective-permute-start(bf16[4,3,64,256]{3,2,1,0:T(8,128)(2,1)S(1)} %get-tuple-element.81), channel_id=1, source_target_pairs={{0,60},{4,0},{8,4},{12,8},{16,12},{20,16},{24,20},{28,24},{32,28},... | collective-permute-start | bytes 1179656 | tf_op jit(solution)/shard_map/ppermute | solution.py:299
  54.4 6.4 %attend.2 = (bf16[512,128]{1,0:T(8,128)(2,1)S(1)}, bf16[512,128]{1,0:T(8,128)(2,1)S(1)}, f32[2,4,64,256]{3,2,1,0:T(8,128)S(1)}, f32[1,4,64,256]{3,2,1,0:T(8,128)...) custom-call(s32[4,10]{1,0:T(4,128)S(1)} %and_convert_fusion.valid, ...), custom_call_target="tpu_custom_call" | custom-call | flops 9663676416 | tf_op jit(solution)/shard_map/attend/pallas_call | solution.py:268
  60.8 0.1 collective-permute-start.10
  60.9 2.6 %collective-permute-start.11 = (bf16[4,3,64,256]{3,2,1,0:T(8,128)(2,1)S(1)}, bf16[4,3,64,256]{3,2,1,0:T(8,128)(2,1)S(1)}, u32[]{:S(2)}, u32[]{:S(2)}) collective-permute-start(bf16[4,3,64,256]{3,2,1,0:T(8,128)(2,1)S(1)} %get-tuple-element.75), channel_id=1, source_target_pairs={{0,60},{4,0},{8,4},{12,8},{16,12},{20,16},{24,20},{28,24},{32,28},... | collective-permute-start | bytes 1179656 | tf_op jit(solution)/shard_map/ppermute | solution.py:299
  63.6 0.1 collective-permute-done.12.hb
  63.6 0.0 collective-permute-done.13.ha
  63.6 6.4 %attend.3 = (bf16[512,128]{1,0:T(8,128)(2,1)S(1)}, bf16[512,128]{1,0:T(8,128)(2,1)S(1)}, f32[2,4,64,256]{3,2,1,0:T(8,128)S(1)}, f32[1,4,64,256]{3,2,1,0:T(8,128)...) custom-call(s32[4,10]{1,0:T(4,128)S(1)} %and_convert_fusion.valid, ...), custom_call_target="tpu_custom_call" | custom-call | flops 9663676416 | tf_op jit(solution)/shard_map/attend/pallas_call | solution.py:268
  70.0 0.3 collective-permute-start.19
  70.3 2.6 %collective-permute-start.20 = (bf16[4,3,64,256]{3,2,1,0:T(8,128)(2,1)S(1)}, bf16[4,3,64,256]{3,2,1,0:T(8,128)(2,1)S(1)}, u32[]{:S(2)}, u32[]{:S(2)}) collective-permute-start(bf16[4,3,64,256]{3,2,1,0:T(8,128)(2,1)S(1)} %get-tuple-element.93), channel_id=1, source_target_pairs={{0,60},{4,0},{8,4},{12,8},{16,12},{20,16},{24,20},{28,24},{32,28},... | collective-permute-start | bytes 1179656 | tf_op jit(solution)/shard_map/ppermute | solution.py:299
  73.0 0.1 add_add_fusion.idx
  73.0 0.0 collective-permute-done.11.r_ha.ha0
  73.1 0.1 fold.2
  73.1 1.0 mix.1
  74.1 0.4 collective-permute-start.14
  74.5 2.3 %collective-permute-start.17 = (bf16[1,4,64,256]{3,2,1,0:T(8,128)(2,1)S(1)}, bf16[1,4,64,256]{3,2,1,0:T(8,128)(2,1)S(1)}, u32[]{:S(2)}, u32[]{:S(2)}) collective-permute-start(bf16[1,4,64,256]{3,2,1,0:T(8,128)(2,1)S(1)} %get-tuple-element.76), channel_id=1, source_target_pairs={{0,64},{64,128},{128,192},{192,0},{1,65},{65,129},{129,193},{193,1... | collective-permute-start | bytes 393224 | tf_op jit(solution)/shard_map/ppermute | solution.py:296
  76.8 1.8 %collective-permute-start.18 = (bf16[1,4,64,256]{3,2,1,0:T(8,128)(2,1)S(1)}, bf16[1,4,64,256]{3,2,1,0:T(8,128)(2,1)S(1)}, u32[]{:S(2)}, u32[]{:S(2)}) collective-permute-start(bf16[1,4,64,256]{3,2,1,0:T(8,128)(2,1)S(1)} %get-tuple-element.89), channel_id=1, source_target_pairs={{0,192},{64,0},{128,64},{192,128},{1,193},{65,1},{129,65},{193,129... | collective-permute-start | bytes 393224 | tf_op jit(solution)/shard_map/ppermute | solution.py:296
  78.6 6.8 %collective-permute-done.19.r_hb.hb1 = bf16[4,3,64,256]{3,2,1,0:T(8,128)(2,1)S(1)} collective-permute-done((bf16[4,3,64,256]{3,2,1,0:T(8,128)(2,1)S(1)}, bf16[4,3,64,256]{3,2,1,0:T(8,128)(2,1)S(1)}, u32[]{:S(2)}, u32[]{:S(2)}) %collective-permute-start.19) | collective-permute-done | bytes 393248 | tf_op jit(solution)/shard_map/ppermute | solution.py:299
  85.5 0.1 fold.3
  85.5 1.4 %collective-permute-start.21 = (bf16[1,4,64,256]{3,2,1,0:T(8,128)(2,1)S(1)}, bf16[1,4,64,256]{3,2,1,0:T(8,128)(2,1)S(1)}, u32[]{:S(2)}, u32[]{:S(2)}) collective-permute-start(bf16[1,4,64,256]{3,2,1,0:T(8,128)(2,1)S(1)} %get-tuple-element.96), channel_id=1, source_target_pairs={{0,64},{64,128},{128,192},{192,0},{1,65},{65,129},{129,193},{193,1... | collective-permute-start | bytes 393224 | tf_op jit(solution)/shard_map/ppermute | solution.py:296
  87.0 2.8 %collective-permute-start.22 = (bf16[1,4,64,256]{3,2,1,0:T(8,128)(2,1)S(1)}, bf16[1,4,64,256]{3,2,1,0:T(8,128)(2,1)S(1)}, u32[]{:S(2)}, u32[]{:S(2)}) collective-permute-start(bf16[1,4,64,256]{3,2,1,0:T(8,128)(2,1)S(1)} %get-tuple-element.97), channel_id=1, source_target_pairs={{0,192},{64,0},{128,64},{192,128},{1,193},{65,1},{129,65},{193,129... | collective-permute-start | bytes 393224 | tf_op jit(solution)/shard_map/ppermute | solution.py:296
  89.8 0.0 collective-permute-done.17.tb0
  89.8 0.0 collective-permute-start.15
  89.8 1.8 %collective-permute-start.16 = (bf16[512,256]{1,0:T(8,128)(2,1)S(1)}, bf16[512,256]{1,0:T(8,128)(2,1)S(1)}, u32[]{:S(2)}, u32[]{:S(2)}) collective-permute-start(bf16[512,256]{1,0:T(8,128)(2,1)S(1)} %get-tuple-element.86), channel_id=1, source_target_pairs={{0,2},{1,3},{2,0},{3,1},{4,6},{5,7},{6,4},{7,5},{8,10},{9,11},{10,... | collective-permute-start | bytes 786440 | tf_op jit(solution)/shard_map/ppermute | solution.py:293
  91.5 2.8 %collective-permute-done.21.tb1 = bf16[1,4,64,256]{3,2,1,0:T(8,128)(2,1)S(1)} collective-permute-done((bf16[1,4,64,256]{3,2,1,0:T(8,128)(2,1)S(1)}, bf16[1,4,64,256]{3,2,1,0:T(8,128)(2,1)S(1)}, u32[]{:S(2)}, u32[]{:S(2)}) %collective-permute-start.21) | collective-permute-done | bytes 131104 | tf_op jit(solution)/shard_map/ppermute | solution.py:296
  94.3 0.0 collective-permute-done.22.ta1
  94.3 1.6 %in_grad.1 = (f32[512,256]{1,0:T(8,128)S(1)}, bf16[512,256]{1,0:T(8,128)(2,1)S(1)}, bf16[512,256]{1,0:T(8,128)(2,1)S(1)}, bf16[512,256]{1,0:T(8,128)(2,1)S(1)}) custom-call(s32[4]{0:T(128)S(1)} %add_add_fusion.idx, bf16[512,128]{1,0:T(8,128)(2,1)S(1)} %get-tuple-element.87.dq0, f32[2,4,64,256]{3,2,1,0:T(8,128)S(1)} %get-tuple-element.88.own0, ...), custom_call_target="tpu_custom_call" | custom-call | tf_op jit(solution)/shard_map/in_grad/pallas_call | solution.py:268
  95.9 0.1 collective-permute-start.23
  96.1 2.0 %collective-permute-start.24 = (bf16[512,256]{1,0:T(8,128)(2,1)S(1)}, bf16[512,256]{1,0:T(8,128)(2,1)S(1)}, u32[]{:S(2)}, u32[]{:S(2)}) collective-permute-start(bf16[512,256]{1,0:T(8,128)(2,1)S(1)} %get-tuple-element.100), channel_id=1, source_target_pairs={{0,3},{1,0},{2,1},{3,2},{4,7},{5,4},{6,5},{7,6},{8,11},{9,8},{10,9... | collective-permute-start | bytes 786440 | tf_op jit(solution)/shard_map/ppermute | solution.py:293
  98.1 0.5 collective-permute-start.25
  98.6 6.5 %collective-permute-done.15.c = bf16[512,256]{1,0:T(8,128)(2,1)S(1)} collective-permute-done((bf16[512,256]{1,0:T(8,128)(2,1)S(1)}, bf16[512,256]{1,0:T(8,128)(2,1)S(1)}, u32[]{:S(2)}, u32[]{:S(2)}) %collective-permute-start.15) | collective-permute-done | bytes 262176 | tf_op jit(solution)/shard_map/ppermute | solution.py:293
  105.1 0.8 mixed_sum.1
  105.9 8.0 %collective-permute-done.24.c = bf16[512,256]{1,0:T(8,128)(2,1)S(1)} collective-permute-done((bf16[512,256]{1,0:T(8,128)(2,1)S(1)}, bf16[512,256]{1,0:T(8,128)(2,1)S(1)}, u32[]{:S(2)}, u32[]{:S(2)}) %collective-permute-start.24) | collective-permute-done | bytes 262176 | tf_op jit(solution)/shard_map/ppermute | solution.py:293
  113.9 0.0 collective-permute-done.25.d
  113.9 0.8 in_grad_sum.1
  (16 shorter events, 0.0 us)
Async XLA Ops:
  0.6 9.5 %collective-permute-start = (bf16[512,256]{1,0:T(8,128)(2,1)}, bf16[512,256]{1,0:T(8,128)(2,1)S(1)}, u32[]{:S(2)}, u32[]{:S(2)}) collective-permute-start(bf16[512,256]{1,0:T(8,128)(2,1)} %bitcast.9), channel_id=1, source_target_pairs={{0,1},{1,2},{2,3},{3,0},{4,5},{5,6},{6,7},{7,4},{8,9},{9,10},{10,1... | collective-permute-start | bytes 786440 | tf_op jit(solution)/shard_map/ppermute | solution.py:293
  1.2 14.8 %collective-permute-start.1 = (bf16[512,256]{1,0:T(8,128)(2,1)}, bf16[512,256]{1,0:T(8,128)(2,1)S(1)}, u32[]{:S(2)}, u32[]{:S(2)}) collective-permute-start(bf16[512,256]{1,0:T(8,128)(2,1)} %bitcast.10), channel_id=1, source_target_pairs={{0,3},{1,0},{2,1},{3,2},{4,7},{5,4},{6,5},{7,6},{8,11},{9,8},{10,9... | collective-permute-start | bytes 786440 | tf_op jit(solution)/shard_map/ppermute | solution.py:293
  2.7 13.3 %collective-permute-start.2 = (bf16[512,256]{1,0:T(8,128)(2,1)}, bf16[512,256]{1,0:T(8,128)(2,1)S(1)}, u32[]{:S(2)}, u32[]{:S(2)}) collective-permute-start(bf16[512,256]{1,0:T(8,128)(2,1)} %bitcast.11), channel_id=1, source_target_pairs={{0,2},{1,3},{2,0},{3,1},{4,6},{5,7},{6,4},{7,5},{8,10},{9,11},{10,... | collective-permute-start | bytes 786440 | tf_op jit(solution)/shard_map/ppermute | solution.py:293
  4.1 1.4 %copy-start = (bf16[1024,3,256]{2,0,1:T(8,128)(2,1)S(1)}, bf16[1024,3,256]{2,0,1:T(8,128)(2,1)}, u32[]{:S(2)}) copy-start(bf16[1024,3,256]{2,0,1:T(8,128)(2,1)} %param.6) | copy-start | bytes 4718596
  5.5 0.9 copy-start.3
  6.6 17.1 %copy-start.4 = (bf16[2,4,64,256]{3,2,1,0:T(8,128)(2,1)S(1)}, bf16[2,4,64,256]{3,2,1,0:T(8,128)(2,1)}, u32[]{:S(2)}) copy-start(bf16[2,4,64,256]{3,2,1,0:T(8,128)(2,1)} %param.5) | copy-start | bytes 786436
  17.3 13.4 %collective-permute-start.3 = (bf16[1,4,64,512]{3,2,1,0:T(8,128)(2,1)S(1)}, bf16[1,4,64,512]{3,2,1,0:T(8,128)(2,1)}, u32[]{:S(2)}, u32[]{:S(2)}) collective-permute-start(bf16[1,4,64,512]{3,2,1,0:T(8,128)(2,1)S(1)} %get-tuple-element.57.f1), channel_id=1, source_target_pairs={{0,64},{64,128},{128,192},{192,0},{1,65},{65,129},{129,193},{193,1... | collective-permute-start | bytes 786440 | tf_op jit(solution)/shard_map/ppermute | solution.py:296
  20.6 14.8 %collective-permute-start.4 = (bf16[1,4,64,512]{3,2,1,0:T(8,128)(2,1)S(1)}, bf16[1,4,64,512]{3,2,1,0:T(8,128)(2,1)}, u32[]{:S(2)}, u32[]{:S(2)}) collective-permute-start(bf16[1,4,64,512]{3,2,1,0:T(8,128)(2,1)S(1)} %get-tuple-element.54.f0), channel_id=1, source_target_pairs={{0,192},{64,0},{128,64},{192,128},{1,193},{65,1},{129,65},{193,129... | collective-permute-start | bytes 786440 | tf_op jit(solution)/shard_map/ppermute | solution.py:296
  23.7 11.7 %collective-permute-start.5 = (bf16[512,256]{1,0:T(8,128)(2,1)S(1)}, bf16[512,256]{1,0:T(8,128)(2,1)}, u32[]{:S(2)}, u32[]{:S(2)}) collective-permute-start(bf16[512,256]{1,0:T(8,128)(2,1)S(1)} %bitcast.13), channel_id=1, source_target_pairs={{0,1},{1,2},{2,3},{3,0},{4,5},{5,6},{6,7},{7,4},{8,9},{9,10},{10,1... | collective-permute-start | bytes 786440 | tf_op jit(solution)/shard_map/ppermute | solution.py:293
  25.0 13.5 %collective-permute-start.6 = (bf16[512,256]{1,0:T(8,128)(2,1)S(1)}, bf16[512,256]{1,0:T(8,128)(2,1)}, u32[]{:S(2)}, u32[]{:S(2)}) collective-permute-start(bf16[512,256]{1,0:T(8,128)(2,1)S(1)} %bitcast.14), channel_id=1, source_target_pairs={{0,3},{1,0},{2,1},{3,2},{4,7},{5,4},{6,5},{7,6},{8,11},{9,8},{10,9... | collective-permute-start | bytes 786440 | tf_op jit(solution)/shard_map/ppermute | solution.py:293
  25.7 12.8 %collective-permute-start.7 = (bf16[512,256]{1,0:T(8,128)(2,1)S(1)}, bf16[512,256]{1,0:T(8,128)(2,1)}, u32[]{:S(2)}, u32[]{:S(2)}) collective-permute-start(bf16[512,256]{1,0:T(8,128)(2,1)S(1)} %bitcast.15), channel_id=1, source_target_pairs={{0,2},{1,3},{2,0},{3,1},{4,6},{5,7},{6,4},{7,5},{8,10},{9,11},{10,... | collective-permute-start | bytes 786440 | tf_op jit(solution)/shard_map/ppermute | solution.py:293
  39.7 3.8 %copy-start.2 = (bf16[256,1024]{1,0:T(8,128)(2,1)S(1)}, bf16[256,1024]{1,0:T(8,128)(2,1)}, u32[]{:S(2)}) copy-start(bf16[256,1024]{1,0:T(8,128)(2,1)} %w.3) | copy-start | bytes 1572868
  39.7 12.1 %collective-permute-start.8 = (bf16[4,3,64,256]{3,2,1,0:T(8,128)(2,1)S(1)}, bf16[4,3,64,256]{3,2,1,0:T(8,128)(2,1)S(1)}, u32[]{:S(2)}, u32[]{:S(2)}) collective-permute-start(bf16[4,3,64,256]{3,2,1,0:T(8,128)(2,1)S(1)} %get-tuple-element.67), channel_id=1, source_target_pairs={{0,4},{4,8},{8,12},{12,16},{16,20},{20,24},{24,28},{28,32},{32,36}... | collective-permute-start | bytes 1179656 | tf_op jit(solution)/shard_map/ppermute | solution.py:299
  39.8 12.0 %collective-permute-start.9 = (bf16[4,3,64,256]{3,2,1,0:T(8,128)(2,1)S(1)}, bf16[4,3,64,256]{3,2,1,0:T(8,128)(2,1)S(1)}, u32[]{:S(2)}, u32[]{:S(2)}) collective-permute-start(bf16[4,3,64,256]{3,2,1,0:T(8,128)(2,1)S(1)} %get-tuple-element.68), channel_id=1, source_target_pairs={{0,60},{4,0},{8,4},{12,8},{16,12},{20,16},{24,20},{28,24},{32,28},... | collective-permute-start | bytes 1179656 | tf_op jit(solution)/shard_map/ppermute | solution.py:299
  51.8 11.8 %collective-permute-start.12 = (bf16[4,3,64,256]{3,2,1,0:T(8,128)(2,1)S(1)}, bf16[4,3,64,256]{3,2,1,0:T(8,128)(2,1)S(1)}, u32[]{:S(2)}, u32[]{:S(2)}) collective-permute-start(bf16[4,3,64,256]{3,2,1,0:T(8,128)(2,1)S(1)} %get-tuple-element.80), channel_id=1, source_target_pairs={{0,4},{4,8},{8,12},{12,16},{16,20},{20,24},{24,28},{28,32},{32,36}... | collective-permute-start | bytes 1179656 | tf_op jit(solution)/shard_map/ppermute | solution.py:299
  51.9 11.7 %collective-permute-start.13 = (bf16[4,3,64,256]{3,2,1,0:T(8,128)(2,1)S(1)}, bf16[4,3,64,256]{3,2,1,0:T(8,128)(2,1)S(1)}, u32[]{:S(2)}, u32[]{:S(2)}) collective-permute-start(bf16[4,3,64,256]{3,2,1,0:T(8,128)(2,1)S(1)} %get-tuple-element.81), channel_id=1, source_target_pairs={{0,60},{4,0},{8,4},{12,8},{16,12},{20,16},{24,20},{28,24},{32,28},... | collective-permute-start | bytes 1179656 | tf_op jit(solution)/shard_map/ppermute | solution.py:299
  60.8 12.2 %collective-permute-start.10 = (bf16[4,3,64,256]{3,2,1,0:T(8,128)(2,1)S(1)}, bf16[4,3,64,256]{3,2,1,0:T(8,128)(2,1)S(1)}, u32[]{:S(2)}, u32[]{:S(2)}) collective-permute-start(bf16[4,3,64,256]{3,2,1,0:T(8,128)(2,1)S(1)} %get-tuple-element.74), channel_id=1, source_target_pairs={{0,4},{4,8},{8,12},{12,16},{16,20},{20,24},{24,28},{28,32},{32,36}... | collective-permute-start | bytes 1179656 | tf_op jit(solution)/shard_map/ppermute | solution.py:299
  60.9 12.1 %collective-permute-start.11 = (bf16[4,3,64,256]{3,2,1,0:T(8,128)(2,1)S(1)}, bf16[4,3,64,256]{3,2,1,0:T(8,128)(2,1)S(1)}, u32[]{:S(2)}, u32[]{:S(2)}) collective-permute-start(bf16[4,3,64,256]{3,2,1,0:T(8,128)(2,1)S(1)} %get-tuple-element.75), channel_id=1, source_target_pairs={{0,60},{4,0},{8,4},{12,8},{16,12},{20,16},{24,20},{28,24},{32,28},... | collective-permute-start | bytes 1179656 | tf_op jit(solution)/shard_map/ppermute | solution.py:299
  70.0 15.4 %collective-permute-start.19 = (bf16[4,3,64,256]{3,2,1,0:T(8,128)(2,1)S(1)}, bf16[4,3,64,256]{3,2,1,0:T(8,128)(2,1)S(1)}, u32[]{:S(2)}, u32[]{:S(2)}) collective-permute-start(bf16[4,3,64,256]{3,2,1,0:T(8,128)(2,1)S(1)} %get-tuple-element.92), channel_id=1, source_target_pairs={{0,4},{4,8},{8,12},{12,16},{16,20},{20,24},{24,28},{28,32},{32,36}... | collective-permute-start | bytes 1179656 | tf_op jit(solution)/shard_map/ppermute | solution.py:299
  70.3 15.1 %collective-permute-start.20 = (bf16[4,3,64,256]{3,2,1,0:T(8,128)(2,1)S(1)}, bf16[4,3,64,256]{3,2,1,0:T(8,128)(2,1)S(1)}, u32[]{:S(2)}, u32[]{:S(2)}) collective-permute-start(bf16[4,3,64,256]{3,2,1,0:T(8,128)(2,1)S(1)} %get-tuple-element.93), channel_id=1, source_target_pairs={{0,60},{4,0},{8,4},{12,8},{16,12},{20,16},{24,20},{28,24},{32,28},... | collective-permute-start | bytes 1179656 | tf_op jit(solution)/shard_map/ppermute | solution.py:299
  73.1 21.3 %copy-start.1 = (bf16[1024,3,256]{2,0,1:T(8,128)(2,1)S(1)}, bf16[1024,3,256]{2,0,1:T(8,128)(2,1)}, u32[]{:S(2)}) copy-start(bf16[1024,3,256]{2,0,1:T(8,128)(2,1)} %param.6) | copy-start | bytes 4718596
  74.1 23.9 %collective-permute-start.14 = (bf16[512,256]{1,0:T(8,128)(2,1)S(1)}, bf16[512,256]{1,0:T(8,128)(2,1)S(1)}, u32[]{:S(2)}, u32[]{:S(2)}) collective-permute-start(bf16[512,256]{1,0:T(8,128)(2,1)S(1)} %get-tuple-element.84), channel_id=1, source_target_pairs={{0,1},{1,2},{2,3},{3,0},{4,5},{5,6},{6,7},{7,4},{8,9},{9,10},{10,1... | collective-permute-start | bytes 786440 | tf_op jit(solution)/shard_map/ppermute | solution.py:293
  74.5 15.2 %collective-permute-start.17 = (bf16[1,4,64,256]{3,2,1,0:T(8,128)(2,1)S(1)}, bf16[1,4,64,256]{3,2,1,0:T(8,128)(2,1)S(1)}, u32[]{:S(2)}, u32[]{:S(2)}) collective-permute-start(bf16[1,4,64,256]{3,2,1,0:T(8,128)(2,1)S(1)} %get-tuple-element.76), channel_id=1, source_target_pairs={{0,64},{64,128},{128,192},{192,0},{1,65},{65,129},{129,193},{193,1... | collective-permute-start | bytes 393224 | tf_op jit(solution)/shard_map/ppermute | solution.py:296
  76.8 12.9 %collective-permute-start.18 = (bf16[1,4,64,256]{3,2,1,0:T(8,128)(2,1)S(1)}, bf16[1,4,64,256]{3,2,1,0:T(8,128)(2,1)S(1)}, u32[]{:S(2)}, u32[]{:S(2)}) collective-permute-start(bf16[1,4,64,256]{3,2,1,0:T(8,128)(2,1)S(1)} %get-tuple-element.89), channel_id=1, source_target_pairs={{0,192},{64,0},{128,64},{192,128},{1,193},{65,1},{129,65},{193,129... | collective-permute-start | bytes 393224 | tf_op jit(solution)/shard_map/ppermute | solution.py:296
  85.5 8.8 %collective-permute-start.21 = (bf16[1,4,64,256]{3,2,1,0:T(8,128)(2,1)S(1)}, bf16[1,4,64,256]{3,2,1,0:T(8,128)(2,1)S(1)}, u32[]{:S(2)}, u32[]{:S(2)}) collective-permute-start(bf16[1,4,64,256]{3,2,1,0:T(8,128)(2,1)S(1)} %get-tuple-element.96), channel_id=1, source_target_pairs={{0,64},{64,128},{128,192},{192,0},{1,65},{65,129},{129,193},{193,1... | collective-permute-start | bytes 393224 | tf_op jit(solution)/shard_map/ppermute | solution.py:296
  87.0 7.4 %collective-permute-start.22 = (bf16[1,4,64,256]{3,2,1,0:T(8,128)(2,1)S(1)}, bf16[1,4,64,256]{3,2,1,0:T(8,128)(2,1)S(1)}, u32[]{:S(2)}, u32[]{:S(2)}) collective-permute-start(bf16[1,4,64,256]{3,2,1,0:T(8,128)(2,1)S(1)} %get-tuple-element.97), channel_id=1, source_target_pairs={{0,192},{64,0},{128,64},{192,128},{1,193},{65,1},{129,65},{193,129... | collective-permute-start | bytes 393224 | tf_op jit(solution)/shard_map/ppermute | solution.py:296
  89.8 15.3 %collective-permute-start.15 = (bf16[512,256]{1,0:T(8,128)(2,1)S(1)}, bf16[512,256]{1,0:T(8,128)(2,1)S(1)}, u32[]{:S(2)}, u32[]{:S(2)}) collective-permute-start(bf16[512,256]{1,0:T(8,128)(2,1)S(1)} %get-tuple-element.85), channel_id=1, source_target_pairs={{0,3},{1,0},{2,1},{3,2},{4,7},{5,4},{6,5},{7,6},{8,11},{9,8},{10,9... | collective-permute-start | bytes 786440 | tf_op jit(solution)/shard_map/ppermute | solution.py:293
  89.8 15.3 %collective-permute-start.16 = (bf16[512,256]{1,0:T(8,128)(2,1)S(1)}, bf16[512,256]{1,0:T(8,128)(2,1)S(1)}, u32[]{:S(2)}, u32[]{:S(2)}) collective-permute-start(bf16[512,256]{1,0:T(8,128)(2,1)S(1)} %get-tuple-element.86), channel_id=1, source_target_pairs={{0,2},{1,3},{2,0},{3,1},{4,6},{5,7},{6,4},{7,5},{8,10},{9,11},{10,... | collective-permute-start | bytes 786440 | tf_op jit(solution)/shard_map/ppermute | solution.py:293
  95.9 10.0 %collective-permute-start.23 = (bf16[512,256]{1,0:T(8,128)(2,1)S(1)}, bf16[512,256]{1,0:T(8,128)(2,1)S(1)}, u32[]{:S(2)}, u32[]{:S(2)}) collective-permute-start(bf16[512,256]{1,0:T(8,128)(2,1)S(1)} %get-tuple-element.99), channel_id=1, source_target_pairs={{0,1},{1,2},{2,3},{3,0},{4,5},{5,6},{6,7},{7,4},{8,9},{9,10},{10,1... | collective-permute-start | bytes 786440 | tf_op jit(solution)/shard_map/ppermute | solution.py:293
  96.1 17.8 %collective-permute-start.24 = (bf16[512,256]{1,0:T(8,128)(2,1)S(1)}, bf16[512,256]{1,0:T(8,128)(2,1)S(1)}, u32[]{:S(2)}, u32[]{:S(2)}) collective-permute-start(bf16[512,256]{1,0:T(8,128)(2,1)S(1)} %get-tuple-element.100), channel_id=1, source_target_pairs={{0,3},{1,0},{2,1},{3,2},{4,7},{5,4},{6,5},{7,6},{8,11},{9,8},{10,9... | collective-permute-start | bytes 786440 | tf_op jit(solution)/shard_map/ppermute | solution.py:293
  98.1 15.9 %collective-permute-start.25 = (bf16[512,256]{1,0:T(8,128)(2,1)S(1)}, bf16[512,256]{1,0:T(8,128)(2,1)S(1)}, u32[]{:S(2)}, u32[]{:S(2)}) collective-permute-start(bf16[512,256]{1,0:T(8,128)(2,1)S(1)} %get-tuple-element.101), channel_id=1, source_target_pairs={{0,2},{1,3},{2,0},{3,1},{4,6},{5,7},{6,4},{7,5},{8,10},{9,11},{10,... | collective-permute-start | bytes 786440 | tf_op jit(solution)/shard_map/ppermute | solution.py:293

commit v4 on v3

--- a/solution.py
+++ b/solution.py
@@ -36,6 +36,7 @@
     for i, ref in enumerate((tmb, f0, f1, tma)):
         put(i, 3, ref[0, :, :, lanes])
 
+    vt[pl.ds(128, 16), :] = jnp.ones((16, 2560), BF16)
     eye = jnp.where(
         lax.broadcasted_iota(jnp.int32, (128, 128), 0) == lax.broadcasted_iota(jnp.int32, (128, 128), 1),
         1.0, 0.0,
@@ -46,7 +47,7 @@
     for i in range(5):
         at = pl.ds(i * 512, 512)
         kt[:, at] = ks[at, :].T
-        vt[:, at] = vs[at, :].T
+        vt[pl.ds(0, 128), at] = vs[at, :].T
     krow = lax.broadcasted_iota(jnp.int32, (64, 256), 0)
     lane = lax.broadcasted_iota(jnp.int32, (64, 256), 1)
     band = jnp.abs(krow - lane % 64) <= 3
@@ -116,13 +117,14 @@
         p_buf = bufs[g % 2][1]
         mine = pl.ds(g * 128, 128)
         bbd = spread(b[mine, :])
-        outT = jnp.zeros((128, 256), F32)
+        sums = jnp.zeros((144, 256), F32)
         for i in range(3):
             pb = p_buf[pl.ds(i * 512, 512), :]
-            outT = outT + dot(vt[:, keys_of(g, i)], pb)
+            sums = sums + dot(vt[:, keys_of(g, i)], pb)
             add_to(dv, g, i, dot(pb, bbd))
+        outT = sums[:128]
         att[mine, :] = gather(outT).astype(BF16)
-        return jnp.sum(outT * dot(eye, bbd, NT), axis=0, keepdims=True)
+        return jnp.sum(outT * dot(eye, bbd, NT), axis=0, keepdims=True) / sums[128:129]
 
     def slopes(g, inv, c):
         s_buf, _, d_buf = bufs[g % 2]
@@ -337,7 +339,7 @@
             valid, (q, b, *around),
             scratch=[
                 pltpu.VMEM((2560, 128), BF16), pltpu.VMEM((2560, 128), BF16),
-                pltpu.VMEM((128, 2560), BF16), pltpu.VMEM((128, 2560), BF16),
+                pltpu.VMEM((128, 2560), BF16), pltpu.VMEM((144, 2560), BF16),
                 pltpu.VMEM((2560, 128), F32), pltpu.VMEM((2560, 128), F32),
                 pltpu.VMEM((1536, 256), F32), pltpu.VMEM((1536, 256), F32),
                 pltpu.VMEM((1536, 256), BF16), pltpu.VMEM((1536, 256), BF16),

time: 115 us -> 115 us (level)
  transfers between devices with their start and end apart: 26 -> 26, of which waited for: 11 -> 10; matrix products, arithmetic and copies ran while one was open for 0% -> 0% of each run, Pallas kernels for 17% -> 17%
where the time goes in v4:
time: 115 us
  waiting for transfers between devices  51 us (44%)
  starting transfers between devices  37.7 us (33%)
  Pallas kernels  22.8 us (20%)
  local copies, waits for them, and re-layouts  2.37 us (2%)
    ppermute x12, waiting for transfers between devices, ring(): lax.ppermute(array, 'tensor', [(i, (i + by) % n_x) for i in range(n_x)])  26.7 us
    pallas_call x13, Pallas kernels, local_call(): pl.pallas_call(body, out_shape=tuple(outs), in_specs=specs, out_specs=(vm...  22.8 us
    ppermute x6, starting transfers between devices, frames(): return lax.ppermute(array, 'tm', [(i, (i + by) % n_t) for i in range(n_t)])  14.8 us
    ppermute x8, waiting for transfers between devices, rows(): lax.ppermute(array, 'height', [(i, (i + by) % n_h) for i in range(n_h)])  13.5 us
    ppermute x12, starting transfers between devices, ring(): lax.ppermute(array, 'tensor', [(i, (i + by) % n_x) for i in range(n_x)])  12.1 us
    ppermute x8, starting transfers between devices, rows(): lax.ppermute(array, 'height', [(i, (i + by) % n_h) for i in range(n_h)])  10.8 us
    ppermute x6, waiting for transfers between devices, frames(): return lax.ppermute(array, 'tm', [(i, (i + by) % n_t) for i in range(n_t)])  10.7 us
    unnamed x10, local copies, waits for them, and re-layouts  2.37 us
  transfers between devices with their start and end apart: 26, of which 10 were waited for; matrix products, arithmetic and copies ran while one was open for 0% of the time, Pallas kernels for 17%

profile of v4, /device:TPU:22, one launch (start us, length us, event | category | flops | bytes accessed | tf_op | source)
XLA Modules:
  0.0 114.9 jit_solution(14938955014293089602)
XLA Ops:
  0.6 0.6 collective-permute-start
  1.2 1.5 %collective-permute-start.1 = (bf16[512,256]{1,0:T(8,128)(2,1)}, bf16[512,256]{1,0:T(8,128)(2,1)S(1)}, u32[]{:S(2)}, u32[]{:S(2)}) collective-permute-start(bf16[512,256]{1,0:T(8,128)(2,1)} %bitcast.10), channel_id=1, source_target_pairs={{0,3},{1,0},{2,1},{3,2},{4,7},{5,4},{6,5},{7,6},{8,11},{9,8},{10,9... | collective-permute-start | bytes 786440 | tf_op jit(solution)/shard_map/ppermute | solution.py:295
  2.7 1.4 %collective-permute-start.2 = (bf16[512,256]{1,0:T(8,128)(2,1)}, bf16[512,256]{1,0:T(8,128)(2,1)S(1)}, u32[]{:S(2)}, u32[]{:S(2)}) collective-permute-start(bf16[512,256]{1,0:T(8,128)(2,1)} %bitcast.11), channel_id=1, source_target_pairs={{0,2},{1,3},{2,0},{3,1},{4,6},{5,7},{6,4},{7,5},{8,10},{9,11},{10,... | collective-permute-start | bytes 786440 | tf_op jit(solution)/shard_map/ppermute | solution.py:295
  4.1 1.4 %copy-done = bf16[1024,3,256]{2,0,1:T(8,128)(2,1)S(1)} copy-done((bf16[1024,3,256]{2,0,1:T(8,128)(2,1)S(1)}, bf16[1024,3,256]{2,0,1:T(8,128)(2,1)}, u32[]{:S(2)}) %copy-start) | copy-done | bytes 1572888
  5.5 0.9 copy-done.3
  6.5 0.1 stage.1
  6.6 0.0 copy-start.4
  6.7 0.1 add_add_fusion.1.idx
  6.7 3.4 %collective-permute-done.x1 = bf16[512,256]{1,0:T(8,128)(2,1)S(1)} collective-permute-done((bf16[512,256]{1,0:T(8,128)(2,1)}, bf16[512,256]{1,0:T(8,128)(2,1)S(1)}, u32[]{:S(2)}, u32[]{:S(2)}) %collective-permute-start) | collective-permute-done | bytes 262176 | tf_op jit(solution)/shard_map/ppermute | solution.py:295
  10.1 5.9 %collective-permute-done.1.x2 = bf16[512,256]{1,0:T(8,128)(2,1)S(1)} collective-permute-done((bf16[512,256]{1,0:T(8,128)(2,1)}, bf16[512,256]{1,0:T(8,128)(2,1)S(1)}, u32[]{:S(2)}, u32[]{:S(2)}) %collective-permute-start.1) | collective-permute-done | bytes 262176 | tf_op jit(solution)/shard_map/ppermute | solution.py:295
  16.0 0.0 collective-permute-done.2.x3
  16.0 1.3 %project.1 = (bf16[1,4,64,512]{3,2,1,0:T(8,128)(2,1)S(1)}, bf16[1,4,64,512]{3,2,1,0:T(8,128)(2,1)S(1)}) custom-call(s32[4]{0:T(128)S(1)} %add_add_fusion.1.idx, bf16[512,256]{1,0:T(8,128)(2,1)S(1)} %get-tuple-element.55.x0, bf16[512,256]{1,0:T(8,128)(2,1)S(1)} %collective-permute-done.x1, bf16[512,256]{1,0:T(8,128)(2,1)S(1)} %collective-permute-done.1.x2, ...), custom_call_target="tpu_custom_call" | custom-call | tf_op jit(solution)/shard_map/project/pallas_call | solution.py:270
  17.3 3.3 %collective-permute-start.3 = (bf16[1,4,64,512]{3,2,1,0:T(8,128)(2,1)S(1)}, bf16[1,4,64,512]{3,2,1,0:T(8,128)(2,1)}, u32[]{:S(2)}, u32[]{:S(2)}) collective-permute-start(bf16[1,4,64,512]{3,2,1,0:T(8,128)(2,1)S(1)} %get-tuple-element.57.f1), channel_id=1, source_target_pairs={{0,64},{64,128},{128,192},{192,0},{1,65},{65,129},{129,193},{193,1... | collective-permute-start | bytes 786440 | tf_op jit(solution)/shard_map/ppermute | solution.py:298
  20.6 3.1 %collective-permute-start.4 = (bf16[1,4,64,512]{3,2,1,0:T(8,128)(2,1)S(1)}, bf16[1,4,64,512]{3,2,1,0:T(8,128)(2,1)}, u32[]{:S(2)}, u32[]{:S(2)}) collective-permute-start(bf16[1,4,64,512]{3,2,1,0:T(8,128)(2,1)S(1)} %get-tuple-element.54.f0), channel_id=1, source_target_pairs={{0,192},{64,0},{128,64},{192,128},{1,193},{65,1},{129,65},{193,129... | collective-permute-start | bytes 786440 | tf_op jit(solution)/shard_map/ppermute | solution.py:298
  23.7 1.3 %collective-permute-start.5 = (bf16[512,256]{1,0:T(8,128)(2,1)S(1)}, bf16[512,256]{1,0:T(8,128)(2,1)}, u32[]{:S(2)}, u32[]{:S(2)}) collective-permute-start(bf16[512,256]{1,0:T(8,128)(2,1)S(1)} %bitcast.13), channel_id=1, source_target_pairs={{0,1},{1,2},{2,3},{3,0},{4,5},{5,6},{6,7},{7,4},{8,9},{9,10},{10,1... | collective-permute-start | bytes 786440 | tf_op jit(solution)/shard_map/ppermute | solution.py:295
  25.0 0.8 collective-permute-start.6
  25.7 1.8 %collective-permute-start.7 = (bf16[512,256]{1,0:T(8,128)(2,1)S(1)}, bf16[512,256]{1,0:T(8,128)(2,1)}, u32[]{:S(2)}, u32[]{:S(2)}) collective-permute-start(bf16[512,256]{1,0:T(8,128)(2,1)S(1)} %bitcast.15), channel_id=1, source_target_pairs={{0,2},{1,3},{2,0},{3,1},{4,6},{5,7},{6,4},{7,5},{8,10},{9,11},{10,... | collective-permute-start | bytes 786440 | tf_op jit(solution)/shard_map/ppermute | solution.py:295
  27.6 3.0 %collective-permute-done.3.tmb = bf16[1,4,64,512]{3,2,1,0:T(8,128)(2,1)} collective-permute-done((bf16[1,4,64,512]{3,2,1,0:T(8,128)(2,1)S(1)}, bf16[1,4,64,512]{3,2,1,0:T(8,128)(2,1)}, u32[]{:S(2)}, u32[]{:S(2)}) %collective-permute-start.3) | collective-permute-done | bytes 262176 | tf_op jit(solution)/shard_map/ppermute | solution.py:298
  30.6 4.8 %collective-permute-done.4.tma = bf16[1,4,64,512]{3,2,1,0:T(8,128)(2,1)} collective-permute-done((bf16[1,4,64,512]{3,2,1,0:T(8,128)(2,1)S(1)}, bf16[1,4,64,512]{3,2,1,0:T(8,128)(2,1)}, u32[]{:S(2)}, u32[]{:S(2)}) %collective-permute-start.4) | collective-permute-done | bytes 262176 | tf_op jit(solution)/shard_map/ppermute | solution.py:298
  35.4 0.0 collective-permute-done.5.x1
  35.4 3.1 %collective-permute-done.6.x2 = bf16[512,256]{1,0:T(8,128)(2,1)} collective-permute-done((bf16[512,256]{1,0:T(8,128)(2,1)S(1)}, bf16[512,256]{1,0:T(8,128)(2,1)}, u32[]{:S(2)}, u32[]{:S(2)}) %collective-permute-start.6) | collective-permute-done | bytes 262176 | tf_op jit(solution)/shard_map/ppermute | solution.py:295
  38.5 1.1 edges.1
  39.7 0.0 copy-start.2
  39.7 0.1 collective-permute-start.8
  39.8 2.6 %collective-permute-start.9 = (bf16[4,3,64,256]{3,2,1,0:T(8,128)(2,1)S(1)}, bf16[4,3,64,256]{3,2,1,0:T(8,128)(2,1)S(1)}, u32[]{:S(2)}, u32[]{:S(2)}) collective-permute-start(bf16[4,3,64,256]{3,2,1,0:T(8,128)(2,1)S(1)} %get-tuple-element.68), channel_id=1, source_target_pairs={{0,60},{4,0},{8,4},{12,8},{16,12},{20,16},{24,20},{28,24},{32,28},... | collective-permute-start | bytes 1179656 | tf_op jit(solution)/shard_map/ppermute | solution.py:301
  42.4 0.1 and_convert_fusion.valid
  42.5 1.0 query.1
  43.5 1.6 %back.1 = (bf16[512,128]{1,0:T(8,128)(2,1)S(1)}, bf16[512,128]{1,0:T(8,128)(2,1)S(1)}) custom-call(s32[4]{0:T(128)S(1)} %add_add_fusion.1.idx, bf16[512,256]{1,0:T(8,128)(2,1)S(1)} %bitcast.16, bf16[512,256]{1,0:T(8,128)(2,1)} %collective-permute-done.5.x1, bf16[512,256]{1,0:T(8,128)(2,1)} %collective-permute-done.6.x2, ...), custom_call_target="tpu_custom_call" | custom-call | tf_op jit(solution)/shard_map/back/pallas_call | solution.py:270
  45.1 6.7 %collective-permute-done.8.hb = bf16[4,3,64,256]{3,2,1,0:T(8,128)(2,1)S(1)} collective-permute-done((bf16[4,3,64,256]{3,2,1,0:T(8,128)(2,1)S(1)}, bf16[4,3,64,256]{3,2,1,0:T(8,128)(2,1)S(1)}, u32[]{:S(2)}, u32[]{:S(2)}) %collective-permute-start.8) | collective-permute-done | bytes 393248 | tf_op jit(solution)/shard_map/ppermute | solution.py:301
  51.8 0.0 collective-permute-done.9.ha
  51.8 0.1 collective-permute-start.12
  51.9 2.5 %collective-permute-start.13 = (bf16[4,3,64,256]{3,2,1,0:T(8,128)(2,1)S(1)}, bf16[4,3,64,256]{3,2,1,0:T(8,128)(2,1)S(1)}, u32[]{:S(2)}, u32[]{:S(2)}) collective-permute-start(bf16[4,3,64,256]{3,2,1,0:T(8,128)(2,1)S(1)} %get-tuple-element.81), channel_id=1, source_target_pairs={{0,60},{4,0},{8,4},{12,8},{16,12},{20,16},{24,20},{28,24},{32,28},... | collective-permute-start | bytes 1179656 | tf_op jit(solution)/shard_map/ppermute | solution.py:301
  54.4 6.6 %attend.2 = (bf16[512,128]{1,0:T(8,128)(2,1)S(1)}, bf16[512,128]{1,0:T(8,128)(2,1)S(1)}, f32[2,4,64,256]{3,2,1,0:T(8,128)S(1)}, f32[1,4,64,256]{3,2,1,0:T(8,128)...) custom-call(s32[4,10]{1,0:T(4,128)S(1)} %and_convert_fusion.valid, ...), custom_call_target="tpu_custom_call" | custom-call | flops 9663676416 | tf_op jit(solution)/shard_map/attend/pallas_call | solution.py:270
  61.1 0.1 collective-permute-start.10
  61.2 2.6 %collective-permute-start.11 = (bf16[4,3,64,256]{3,2,1,0:T(8,128)(2,1)S(1)}, bf16[4,3,64,256]{3,2,1,0:T(8,128)(2,1)S(1)}, u32[]{:S(2)}, u32[]{:S(2)}) collective-permute-start(bf16[4,3,64,256]{3,2,1,0:T(8,128)(2,1)S(1)} %get-tuple-element.75), channel_id=1, source_target_pairs={{0,60},{4,0},{8,4},{12,8},{16,12},{20,16},{24,20},{28,24},{32,28},... | collective-permute-start | bytes 1179656 | tf_op jit(solution)/shard_map/ppermute | solution.py:301
  63.8 0.0 collective-permute-done.12.hb
  63.8 6.7 %attend.3 = (bf16[512,128]{1,0:T(8,128)(2,1)S(1)}, bf16[512,128]{1,0:T(8,128)(2,1)S(1)}, f32[2,4,64,256]{3,2,1,0:T(8,128)S(1)}, f32[1,4,64,256]{3,2,1,0:T(8,128)...) custom-call(s32[4,10]{1,0:T(4,128)S(1)} %and_convert_fusion.valid, ...), custom_call_target="tpu_custom_call" | custom-call | flops 9663676416 | tf_op jit(solution)/shard_map/attend/pallas_call | solution.py:270
  70.5 0.1 collective-permute-start.19
  70.6 2.6 %collective-permute-start.20 = (bf16[4,3,64,256]{3,2,1,0:T(8,128)(2,1)S(1)}, bf16[4,3,64,256]{3,2,1,0:T(8,128)(2,1)S(1)}, u32[]{:S(2)}, u32[]{:S(2)}) collective-permute-start(bf16[4,3,64,256]{3,2,1,0:T(8,128)(2,1)S(1)} %get-tuple-element.93), channel_id=1, source_target_pairs={{0,60},{4,0},{8,4},{12,8},{16,12},{20,16},{24,20},{28,24},{32,28},... | collective-permute-start | bytes 1179656 | tf_op jit(solution)/shard_map/ppermute | solution.py:301
  73.2 0.1 add_add_fusion.idx
  73.3 0.0 collective-permute-done.10.r_hb.hb0
  73.3 0.0 collective-permute-done.11.r_ha.ha0
  73.3 0.1 fold.2
  73.4 1.0 mix.1
  74.4 0.4 collective-permute-start.14
  74.7 2.4 %collective-permute-start.17 = (bf16[1,4,64,256]{3,2,1,0:T(8,128)(2,1)S(1)}, bf16[1,4,64,256]{3,2,1,0:T(8,128)(2,1)S(1)}, u32[]{:S(2)}, u32[]{:S(2)}) collective-permute-start(bf16[1,4,64,256]{3,2,1,0:T(8,128)(2,1)S(1)} %get-tuple-element.76), channel_id=1, source_target_pairs={{0,64},{64,128},{128,192},{192,0},{1,65},{65,129},{129,193},{193,1... | collective-permute-start | bytes 393224 | tf_op jit(solution)/shard_map/ppermute | solution.py:298
  77.1 1.7 %collective-permute-start.18 = (bf16[1,4,64,256]{3,2,1,0:T(8,128)(2,1)S(1)}, bf16[1,4,64,256]{3,2,1,0:T(8,128)(2,1)S(1)}, u32[]{:S(2)}, u32[]{:S(2)}) collective-permute-start(bf16[1,4,64,256]{3,2,1,0:T(8,128)(2,1)S(1)} %get-tuple-element.89), channel_id=1, source_target_pairs={{0,192},{64,0},{128,64},{192,128},{1,193},{65,1},{129,65},{193,129... | collective-permute-start | bytes 393224 | tf_op jit(solution)/shard_map/ppermute | solution.py:298
  78.8 6.9 %collective-permute-done.19.r_hb.hb1 = bf16[4,3,64,256]{3,2,1,0:T(8,128)(2,1)S(1)} collective-permute-done((bf16[4,3,64,256]{3,2,1,0:T(8,128)(2,1)S(1)}, bf16[4,3,64,256]{3,2,1,0:T(8,128)(2,1)S(1)}, u32[]{:S(2)}, u32[]{:S(2)}) %collective-permute-start.19) | collective-permute-done | bytes 393248 | tf_op jit(solution)/shard_map/ppermute | solution.py:301
  85.7 0.0 collective-permute-done.20.r_ha.ha1
  85.7 0.1 fold.3
  85.8 1.4 %collective-permute-start.21 = (bf16[1,4,64,256]{3,2,1,0:T(8,128)(2,1)S(1)}, bf16[1,4,64,256]{3,2,1,0:T(8,128)(2,1)S(1)}, u32[]{:S(2)}, u32[]{:S(2)}) collective-permute-start(bf16[1,4,64,256]{3,2,1,0:T(8,128)(2,1)S(1)} %get-tuple-element.96), channel_id=1, source_target_pairs={{0,64},{64,128},{128,192},{192,0},{1,65},{65,129},{129,193},{193,1... | collective-permute-start | bytes 393224 | tf_op jit(solution)/shard_map/ppermute | solution.py:298
  87.2 2.8 %collective-permute-start.22 = (bf16[1,4,64,256]{3,2,1,0:T(8,128)(2,1)S(1)}, bf16[1,4,64,256]{3,2,1,0:T(8,128)(2,1)S(1)}, u32[]{:S(2)}, u32[]{:S(2)}) collective-permute-start(bf16[1,4,64,256]{3,2,1,0:T(8,128)(2,1)S(1)} %get-tuple-element.97), channel_id=1, source_target_pairs={{0,192},{64,0},{128,64},{192,128},{1,193},{65,1},{129,65},{193,129... | collective-permute-start | bytes 393224 | tf_op jit(solution)/shard_map/ppermute | solution.py:298
  90.0 1.7 %collective-permute-start.16 = (bf16[512,256]{1,0:T(8,128)(2,1)S(1)}, bf16[512,256]{1,0:T(8,128)(2,1)S(1)}, u32[]{:S(2)}, u32[]{:S(2)}) collective-permute-start(bf16[512,256]{1,0:T(8,128)(2,1)S(1)} %get-tuple-element.86), channel_id=1, source_target_pairs={{0,2},{1,3},{2,0},{3,1},{4,6},{5,7},{6,4},{7,5},{8,10},{9,11},{10,... | collective-permute-start | bytes 786440 | tf_op jit(solution)/shard_map/ppermute | solution.py:295
  91.7 2.9 %collective-permute-done.21.tb1 = bf16[1,4,64,256]{3,2,1,0:T(8,128)(2,1)S(1)} collective-permute-done((bf16[1,4,64,256]{3,2,1,0:T(8,128)(2,1)S(1)}, bf16[1,4,64,256]{3,2,1,0:T(8,128)(2,1)S(1)}, u32[]{:S(2)}, u32[]{:S(2)}) %collective-permute-start.21) | collective-permute-done | bytes 131104 | tf_op jit(solution)/shard_map/ppermute | solution.py:298
  94.7 0.0 collective-permute-done.22.ta1
  94.7 1.6 %in_grad.1 = (f32[512,256]{1,0:T(8,128)S(1)}, bf16[512,256]{1,0:T(8,128)(2,1)S(1)}, bf16[512,256]{1,0:T(8,128)(2,1)S(1)}, bf16[512,256]{1,0:T(8,128)(2,1)S(1)}) custom-call(s32[4]{0:T(128)S(1)} %add_add_fusion.idx, bf16[512,128]{1,0:T(8,128)(2,1)S(1)} %get-tuple-element.87.dq0, f32[2,4,64,256]{3,2,1,0:T(8,128)S(1)} %get-tuple-element.88.own0, ...), custom_call_target="tpu_custom_call" | custom-call | tf_op jit(solution)/shard_map/in_grad/pallas_call | solution.py:270
  96.3 0.2 collective-permute-start.23
  96.5 1.9 %collective-permute-start.24 = (bf16[512,256]{1,0:T(8,128)(2,1)S(1)}, bf16[512,256]{1,0:T(8,128)(2,1)S(1)}, u32[]{:S(2)}, u32[]{:S(2)}) collective-permute-start(bf16[512,256]{1,0:T(8,128)(2,1)S(1)} %get-tuple-element.100), channel_id=1, source_target_pairs={{0,3},{1,0},{2,1},{3,2},{4,7},{5,4},{6,5},{7,6},{8,11},{9,8},{10,9... | collective-permute-start | bytes 786440 | tf_op jit(solution)/shard_map/ppermute | solution.py:295
  98.4 0.0 collective-permute-done.14.b
  98.4 0.5 collective-permute-start.25
  98.9 6.2 %collective-permute-done.15.c = bf16[512,256]{1,0:T(8,128)(2,1)S(1)} collective-permute-done((bf16[512,256]{1,0:T(8,128)(2,1)S(1)}, bf16[512,256]{1,0:T(8,128)(2,1)S(1)}, u32[]{:S(2)}, u32[]{:S(2)}) %collective-permute-start.15) | collective-permute-done | bytes 262176 | tf_op jit(solution)/shard_map/ppermute | solution.py:295
  105.1 0.8 mixed_sum.1
  106.0 8.1 %collective-permute-done.24.c = bf16[512,256]{1,0:T(8,128)(2,1)S(1)} collective-permute-done((bf16[512,256]{1,0:T(8,128)(2,1)S(1)}, bf16[512,256]{1,0:T(8,128)(2,1)S(1)}, u32[]{:S(2)}, u32[]{:S(2)}) %collective-permute-start.24) | collective-permute-done | bytes 262176 | tf_op jit(solution)/shard_map/ppermute | solution.py:295
  114.1 0.8 in_grad_sum.1
  (16 shorter events, 0.0 us)
Async XLA Ops:
  0.6 9.5 %collective-permute-start = (bf16[512,256]{1,0:T(8,128)(2,1)}, bf16[512,256]{1,0:T(8,128)(2,1)S(1)}, u32[]{:S(2)}, u32[]{:S(2)}) collective-permute-start(bf16[512,256]{1,0:T(8,128)(2,1)} %bitcast.9), channel_id=1, source_target_pairs={{0,1},{1,2},{2,3},{3,0},{4,5},{5,6},{6,7},{7,4},{8,9},{9,10},{10,1... | collective-permute-start | bytes 786440 | tf_op jit(solution)/shard_map/ppermute | solution.py:295
  1.2 14.8 %collective-permute-start.1 = (bf16[512,256]{1,0:T(8,128)(2,1)}, bf16[512,256]{1,0:T(8,128)(2,1)S(1)}, u32[]{:S(2)}, u32[]{:S(2)}) collective-permute-start(bf16[512,256]{1,0:T(8,128)(2,1)} %bitcast.10), channel_id=1, source_target_pairs={{0,3},{1,0},{2,1},{3,2},{4,7},{5,4},{6,5},{7,6},{8,11},{9,8},{10,9... | collective-permute-start | bytes 786440 | tf_op jit(solution)/shard_map/ppermute | solution.py:295
  2.7 13.3 %collective-permute-start.2 = (bf16[512,256]{1,0:T(8,128)(2,1)}, bf16[512,256]{1,0:T(8,128)(2,1)S(1)}, u32[]{:S(2)}, u32[]{:S(2)}) collective-permute-start(bf16[512,256]{1,0:T(8,128)(2,1)} %bitcast.11), channel_id=1, source_target_pairs={{0,2},{1,3},{2,0},{3,1},{4,6},{5,7},{6,4},{7,5},{8,10},{9,11},{10,... | collective-permute-start | bytes 786440 | tf_op jit(solution)/shard_map/ppermute | solution.py:295
  4.1 1.4 %copy-start = (bf16[1024,3,256]{2,0,1:T(8,128)(2,1)S(1)}, bf16[1024,3,256]{2,0,1:T(8,128)(2,1)}, u32[]{:S(2)}) copy-start(bf16[1024,3,256]{2,0,1:T(8,128)(2,1)} %param.6) | copy-start | bytes 4718596
  5.5 0.9 copy-start.3
  6.6 17.1 %copy-start.4 = (bf16[2,4,64,256]{3,2,1,0:T(8,128)(2,1)S(1)}, bf16[2,4,64,256]{3,2,1,0:T(8,128)(2,1)}, u32[]{:S(2)}) copy-start(bf16[2,4,64,256]{3,2,1,0:T(8,128)(2,1)} %param.5) | copy-start | bytes 786436
  17.3 13.4 %collective-permute-start.3 = (bf16[1,4,64,512]{3,2,1,0:T(8,128)(2,1)S(1)}, bf16[1,4,64,512]{3,2,1,0:T(8,128)(2,1)}, u32[]{:S(2)}, u32[]{:S(2)}) collective-permute-start(bf16[1,4,64,512]{3,2,1,0:T(8,128)(2,1)S(1)} %get-tuple-element.57.f1), channel_id=1, source_target_pairs={{0,64},{64,128},{128,192},{192,0},{1,65},{65,129},{129,193},{193,1... | collective-permute-start | bytes 786440 | tf_op jit(solution)/shard_map/ppermute | solution.py:298
  20.6 14.8 %collective-permute-start.4 = (bf16[1,4,64,512]{3,2,1,0:T(8,128)(2,1)S(1)}, bf16[1,4,64,512]{3,2,1,0:T(8,128)(2,1)}, u32[]{:S(2)}, u32[]{:S(2)}) collective-permute-start(bf16[1,4,64,512]{3,2,1,0:T(8,128)(2,1)S(1)} %get-tuple-element.54.f0), channel_id=1, source_target_pairs={{0,192},{64,0},{128,64},{192,128},{1,193},{65,1},{129,65},{193,129... | collective-permute-start | bytes 786440 | tf_op jit(solution)/shard_map/ppermute | solution.py:298
  23.7 11.7 %collective-permute-start.5 = (bf16[512,256]{1,0:T(8,128)(2,1)S(1)}, bf16[512,256]{1,0:T(8,128)(2,1)}, u32[]{:S(2)}, u32[]{:S(2)}) collective-permute-start(bf16[512,256]{1,0:T(8,128)(2,1)S(1)} %bitcast.13), channel_id=1, source_target_pairs={{0,1},{1,2},{2,3},{3,0},{4,5},{5,6},{6,7},{7,4},{8,9},{9,10},{10,1... | collective-permute-start | bytes 786440 | tf_op jit(solution)/shard_map/ppermute | solution.py:295
  25.0 13.5 %collective-permute-start.6 = (bf16[512,256]{1,0:T(8,128)(2,1)S(1)}, bf16[512,256]{1,0:T(8,128)(2,1)}, u32[]{:S(2)}, u32[]{:S(2)}) collective-permute-start(bf16[512,256]{1,0:T(8,128)(2,1)S(1)} %bitcast.14), channel_id=1, source_target_pairs={{0,3},{1,0},{2,1},{3,2},{4,7},{5,4},{6,5},{7,6},{8,11},{9,8},{10,9... | collective-permute-start | bytes 786440 | tf_op jit(solution)/shard_map/ppermute | solution.py:295
  25.7 12.8 %collective-permute-start.7 = (bf16[512,256]{1,0:T(8,128)(2,1)S(1)}, bf16[512,256]{1,0:T(8,128)(2,1)}, u32[]{:S(2)}, u32[]{:S(2)}) collective-permute-start(bf16[512,256]{1,0:T(8,128)(2,1)S(1)} %bitcast.15), channel_id=1, source_target_pairs={{0,2},{1,3},{2,0},{3,1},{4,6},{5,7},{6,4},{7,5},{8,10},{9,11},{10,... | collective-permute-start | bytes 786440 | tf_op jit(solution)/shard_map/ppermute | solution.py:295
  39.7 3.8 %copy-start.2 = (bf16[256,1024]{1,0:T(8,128)(2,1)S(1)}, bf16[256,1024]{1,0:T(8,128)(2,1)}, u32[]{:S(2)}) copy-start(bf16[256,1024]{1,0:T(8,128)(2,1)} %w.3) | copy-start | bytes 1572868
  39.7 12.1 %collective-permute-start.8 = (bf16[4,3,64,256]{3,2,1,0:T(8,128)(2,1)S(1)}, bf16[4,3,64,256]{3,2,1,0:T(8,128)(2,1)S(1)}, u32[]{:S(2)}, u32[]{:S(2)}) collective-permute-start(bf16[4,3,64,256]{3,2,1,0:T(8,128)(2,1)S(1)} %get-tuple-element.67), channel_id=1, source_target_pairs={{0,4},{4,8},{8,12},{12,16},{16,20},{20,24},{24,28},{28,32},{32,36}... | collective-permute-start | bytes 1179656 | tf_op jit(solution)/shard_map/ppermute | solution.py:301
  39.8 12.0 %collective-permute-start.9 = (bf16[4,3,64,256]{3,2,1,0:T(8,128)(2,1)S(1)}, bf16[4,3,64,256]{3,2,1,0:T(8,128)(2,1)S(1)}, u32[]{:S(2)}, u32[]{:S(2)}) collective-permute-start(bf16[4,3,64,256]{3,2,1,0:T(8,128)(2,1)S(1)} %get-tuple-element.68), channel_id=1, source_target_pairs={{0,60},{4,0},{8,4},{12,8},{16,12},{20,16},{24,20},{28,24},{32,28},... | collective-permute-start | bytes 1179656 | tf_op jit(solution)/shard_map/ppermute | solution.py:301
  51.8 12.0 %collective-permute-start.12 = (bf16[4,3,64,256]{3,2,1,0:T(8,128)(2,1)S(1)}, bf16[4,3,64,256]{3,2,1,0:T(8,128)(2,1)S(1)}, u32[]{:S(2)}, u32[]{:S(2)}) collective-permute-start(bf16[4,3,64,256]{3,2,1,0:T(8,128)(2,1)S(1)} %get-tuple-element.80), channel_id=1, source_target_pairs={{0,4},{4,8},{8,12},{12,16},{16,20},{20,24},{24,28},{28,32},{32,36}... | collective-permute-start | bytes 1179656 | tf_op jit(solution)/shard_map/ppermute | solution.py:301
  51.9 11.9 %collective-permute-start.13 = (bf16[4,3,64,256]{3,2,1,0:T(8,128)(2,1)S(1)}, bf16[4,3,64,256]{3,2,1,0:T(8,128)(2,1)S(1)}, u32[]{:S(2)}, u32[]{:S(2)}) collective-permute-start(bf16[4,3,64,256]{3,2,1,0:T(8,128)(2,1)S(1)} %get-tuple-element.81), channel_id=1, source_target_pairs={{0,60},{4,0},{8,4},{12,8},{16,12},{20,16},{24,20},{28,24},{32,28},... | collective-permute-start | bytes 1179656 | tf_op jit(solution)/shard_map/ppermute | solution.py:301
  61.1 12.2 %collective-permute-start.10 = (bf16[4,3,64,256]{3,2,1,0:T(8,128)(2,1)S(1)}, bf16[4,3,64,256]{3,2,1,0:T(8,128)(2,1)S(1)}, u32[]{:S(2)}, u32[]{:S(2)}) collective-permute-start(bf16[4,3,64,256]{3,2,1,0:T(8,128)(2,1)S(1)} %get-tuple-element.74), channel_id=1, source_target_pairs={{0,4},{4,8},{8,12},{12,16},{16,20},{20,24},{24,28},{28,32},{32,36}... | collective-permute-start | bytes 1179656 | tf_op jit(solution)/shard_map/ppermute | solution.py:301
  61.2 12.1 %collective-permute-start.11 = (bf16[4,3,64,256]{3,2,1,0:T(8,128)(2,1)S(1)}, bf16[4,3,64,256]{3,2,1,0:T(8,128)(2,1)S(1)}, u32[]{:S(2)}, u32[]{:S(2)}) collective-permute-start(bf16[4,3,64,256]{3,2,1,0:T(8,128)(2,1)S(1)} %get-tuple-element.75), channel_id=1, source_target_pairs={{0,60},{4,0},{8,4},{12,8},{16,12},{20,16},{24,20},{28,24},{32,28},... | collective-permute-start | bytes 1179656 | tf_op jit(solution)/shard_map/ppermute | solution.py:301
  70.5 15.2 %collective-permute-start.19 = (bf16[4,3,64,256]{3,2,1,0:T(8,128)(2,1)S(1)}, bf16[4,3,64,256]{3,2,1,0:T(8,128)(2,1)S(1)}, u32[]{:S(2)}, u32[]{:S(2)}) collective-permute-start(bf16[4,3,64,256]{3,2,1,0:T(8,128)(2,1)S(1)} %get-tuple-element.92), channel_id=1, source_target_pairs={{0,4},{4,8},{8,12},{12,16},{16,20},{20,24},{24,28},{28,32},{32,36}... | collective-permute-start | bytes 1179656 | tf_op jit(solution)/shard_map/ppermute | solution.py:301
  70.6 15.2 %collective-permute-start.20 = (bf16[4,3,64,256]{3,2,1,0:T(8,128)(2,1)S(1)}, bf16[4,3,64,256]{3,2,1,0:T(8,128)(2,1)S(1)}, u32[]{:S(2)}, u32[]{:S(2)}) collective-permute-start(bf16[4,3,64,256]{3,2,1,0:T(8,128)(2,1)S(1)} %get-tuple-element.93), channel_id=1, source_target_pairs={{0,60},{4,0},{8,4},{12,8},{16,12},{20,16},{24,20},{28,24},{32,28},... | collective-permute-start | bytes 1179656 | tf_op jit(solution)/shard_map/ppermute | solution.py:301
  73.3 21.4 %copy-start.1 = (bf16[1024,3,256]{2,0,1:T(8,128)(2,1)S(1)}, bf16[1024,3,256]{2,0,1:T(8,128)(2,1)}, u32[]{:S(2)}) copy-start(bf16[1024,3,256]{2,0,1:T(8,128)(2,1)} %param.6) | copy-start | bytes 4718596
  74.4 24.0 %collective-permute-start.14 = (bf16[512,256]{1,0:T(8,128)(2,1)S(1)}, bf16[512,256]{1,0:T(8,128)(2,1)S(1)}, u32[]{:S(2)}, u32[]{:S(2)}) collective-permute-start(bf16[512,256]{1,0:T(8,128)(2,1)S(1)} %get-tuple-element.84), channel_id=1, source_target_pairs={{0,1},{1,2},{2,3},{3,0},{4,5},{5,6},{6,7},{7,4},{8,9},{9,10},{10,1... | collective-permute-start | bytes 786440 | tf_op jit(solution)/shard_map/ppermute | solution.py:295
  74.7 15.3 %collective-permute-start.17 = (bf16[1,4,64,256]{3,2,1,0:T(8,128)(2,1)S(1)}, bf16[1,4,64,256]{3,2,1,0:T(8,128)(2,1)S(1)}, u32[]{:S(2)}, u32[]{:S(2)}) collective-permute-start(bf16[1,4,64,256]{3,2,1,0:T(8,128)(2,1)S(1)} %get-tuple-element.76), channel_id=1, source_target_pairs={{0,64},{64,128},{128,192},{192,0},{1,65},{65,129},{129,193},{193,1... | collective-permute-start | bytes 393224 | tf_op jit(solution)/shard_map/ppermute | solution.py:298
  77.1 12.9 %collective-permute-start.18 = (bf16[1,4,64,256]{3,2,1,0:T(8,128)(2,1)S(1)}, bf16[1,4,64,256]{3,2,1,0:T(8,128)(2,1)S(1)}, u32[]{:S(2)}, u32[]{:S(2)}) collective-permute-start(bf16[1,4,64,256]{3,2,1,0:T(8,128)(2,1)S(1)} %get-tuple-element.89), channel_id=1, source_target_pairs={{0,192},{64,0},{128,64},{192,128},{1,193},{65,1},{129,65},{193,129... | collective-permute-start | bytes 393224 | tf_op jit(solution)/shard_map/ppermute | solution.py:298
  85.8 8.9 %collective-permute-start.21 = (bf16[1,4,64,256]{3,2,1,0:T(8,128)(2,1)S(1)}, bf16[1,4,64,256]{3,2,1,0:T(8,128)(2,1)S(1)}, u32[]{:S(2)}, u32[]{:S(2)}) collective-permute-start(bf16[1,4,64,256]{3,2,1,0:T(8,128)(2,1)S(1)} %get-tuple-element.96), channel_id=1, source_target_pairs={{0,64},{64,128},{128,192},{192,0},{1,65},{65,129},{129,193},{193,1... | collective-permute-start | bytes 393224 | tf_op jit(solution)/shard_map/ppermute | solution.py:298
  87.2 7.5 %collective-permute-start.22 = (bf16[1,4,64,256]{3,2,1,0:T(8,128)(2,1)S(1)}, bf16[1,4,64,256]{3,2,1,0:T(8,128)(2,1)S(1)}, u32[]{:S(2)}, u32[]{:S(2)}) collective-permute-start(bf16[1,4,64,256]{3,2,1,0:T(8,128)(2,1)S(1)} %get-tuple-element.97), channel_id=1, source_target_pairs={{0,192},{64,0},{128,64},{192,128},{1,193},{65,1},{129,65},{193,129... | collective-permute-start | bytes 393224 | tf_op jit(solution)/shard_map/ppermute | solution.py:298
  90.0 15.1 %collective-permute-start.15 = (bf16[512,256]{1,0:T(8,128)(2,1)S(1)}, bf16[512,256]{1,0:T(8,128)(2,1)S(1)}, u32[]{:S(2)}, u32[]{:S(2)}) collective-permute-start(bf16[512,256]{1,0:T(8,128)(2,1)S(1)} %get-tuple-element.85), channel_id=1, source_target_pairs={{0,3},{1,0},{2,1},{3,2},{4,7},{5,4},{6,5},{7,6},{8,11},{9,8},{10,9... | collective-permute-start | bytes 786440 | tf_op jit(solution)/shard_map/ppermute | solution.py:295
  90.0 15.1 %collective-permute-start.16 = (bf16[512,256]{1,0:T(8,128)(2,1)S(1)}, bf16[512,256]{1,0:T(8,128)(2,1)S(1)}, u32[]{:S(2)}, u32[]{:S(2)}) collective-permute-start(bf16[512,256]{1,0:T(8,128)(2,1)S(1)} %get-tuple-element.86), channel_id=1, source_target_pairs={{0,2},{1,3},{2,0},{3,1},{4,6},{5,7},{6,4},{7,5},{8,10},{9,11},{10,... | collective-permute-start | bytes 786440 | tf_op jit(solution)/shard_map/ppermute | solution.py:295
  96.3 9.7 %collective-permute-start.23 = (bf16[512,256]{1,0:T(8,128)(2,1)S(1)}, bf16[512,256]{1,0:T(8,128)(2,1)S(1)}, u32[]{:S(2)}, u32[]{:S(2)}) collective-permute-start(bf16[512,256]{1,0:T(8,128)(2,1)S(1)} %get-tuple-element.99), channel_id=1, source_target_pairs={{0,1},{1,2},{2,3},{3,0},{4,5},{5,6},{6,7},{7,4},{8,9},{9,10},{10,1... | collective-permute-start | bytes 786440 | tf_op jit(solution)/shard_map/ppermute | solution.py:295
  96.5 17.6 %collective-permute-start.24 = (bf16[512,256]{1,0:T(8,128)(2,1)S(1)}, bf16[512,256]{1,0:T(8,128)(2,1)S(1)}, u32[]{:S(2)}, u32[]{:S(2)}) collective-permute-start(bf16[512,256]{1,0:T(8,128)(2,1)S(1)} %get-tuple-element.100), channel_id=1, source_target_pairs={{0,3},{1,0},{2,1},{3,2},{4,7},{5,4},{6,5},{7,6},{8,11},{9,8},{10,9... | collective-permute-start | bytes 786440 | tf_op jit(solution)/shard_map/ppermute | solution.py:295
  98.4 15.7 %collective-permute-start.25 = (bf16[512,256]{1,0:T(8,128)(2,1)S(1)}, bf16[512,256]{1,0:T(8,128)(2,1)S(1)}, u32[]{:S(2)}, u32[]{:S(2)}) collective-permute-start(bf16[512,256]{1,0:T(8,128)(2,1)S(1)} %get-tuple-element.101), channel_id=1, source_target_pairs={{0,2},{1,3},{2,0},{3,1},{4,6},{5,7},{6,4},{7,5},{8,10},{9,11},{10,... | collective-permute-start | bytes 786440 | tf_op jit(solution)/shard_map/ppermute | solution.py:295

commit v5 on v4

--- a/solution.py
+++ b/solution.py
@@ -171,25 +171,23 @@
     g_tma[0] = take(3, 3, 4, g_tma)
 
 
-def stage_body(w, x, w_out, x_out):
+def stage_body(w, w_out):
     w_out[...] = w[...]
-    x_out[...] = x[...]
-
-
-def project_body(idx, x0, x1, x2, x3, w, f0, f1):
-    acc = None
-    for i, x in enumerate((x0, x1, x2, x3)):
-        at = pl.ds(pl.multiple_of(idx[i] * 256, 256), 256)
-        part = [dot(x[...], w[n, at, :]) for n in (1, 2)]
-        acc = part if acc is None else [a + b for a, b in zip(acc, part)]
-    keys, values = (a.astype(BF16) for a in acc)
-    halves = []
-    for half in range(2):
-        at = slice(half * 128, half * 128 + 128)
-        halves += [keys[:, at], values[:, at]]
-    kv = jnp.concatenate(halves, axis=1).reshape(2, 4, 64, 512)
-    f0[...] = kv[0:1]
-    f1[...] = kv[1:2]
+
+
+def project_body(idx, a0, a1, a2, a3, b0, b1, b2, b3, w, f0, f1):
+    for parts, out in (((a0, a1, a2, a3), f0), ((b0, b1, b2, b3), f1)):
+        acc = None
+        for i, x in enumerate(parts):
+            at = pl.ds(pl.multiple_of(idx[i] * 256, 256), 256)
+            part = [dot(x[...], w[n, at, :]) for n in (1, 2)]
+            acc = part if acc is None else [a + b for a, b in zip(acc, part)]
+        keys, values = (a.astype(BF16) for a in acc)
+        halves = []
+        for half in range(2):
+            at = slice(half * 128, half * 128 + 128)
+            halves += [keys[:, at], values[:, at]]
+        out[...] = jnp.concatenate(halves, axis=1).reshape(1, 4, 64, 512)
 
 
 def edges_body(tmb, f0, f1, tma, lo0, hi0, lo1, hi1):
@@ -208,14 +206,16 @@
         s[...] = acc[...].astype(BF16)
 
 
-def query_body(idx, x0, x1, x2, x3, w, out0, out1):
-    acc = None
-    for i, x in enumerate((x0, x1, x2, x3)):
-        part = dot(x[...], w[0, pl.ds(pl.multiple_of(idx[i] * 256, 256), 256), :])
-        acc = part if acc is None else acc + part
-    query = acc.astype(BF16) * jnp.asarray(0.125, BF16)
-    out0[...] = query[:, :128]
-    out1[...] = query[:, 128:]
+def query_body(idx, a0, a1, a2, a3, b0, b1, b2, b3, w, out0, out1):
+    for f, parts in enumerate(((a0, a1, a2, a3), (b0, b1, b2, b3))):
+        acc = None
+        for i, x in enumerate(parts):
+            part = dot(x[...], w[0, pl.ds(pl.multiple_of(idx[i] * 256, 256), 256), :])
+            acc = part if acc is None else acc + part
+        query = acc.astype(BF16) * jnp.asarray(0.125, BF16)
+        at = pl.ds(f * 256, 256)
+        out0[at, :] = query[:, :128]
+        out1[at, :] = query[:, 128:]
 
 
 def back_body(idx, x0, x1, x2, x3, w, out0, out1):
@@ -303,20 +303,21 @@
     pair, frame, edge = (2, 4, 64, 256), (1, 4, 64, 256), (4, 3, 64, 256)
     half = S((512, 128), BF16)
     piece = S((512, 256), BF16)
-    tok = tokens.reshape(512, 256)
     cot = cotangent.reshape(512, 256)
-    t_parts = (ring(tok, 1), ring(tok, -1), ring(tok, 2))
+    own_a, own_b = tokens[0:1].reshape(256, 256), tokens[1:2].reshape(256, 256)
+    right_a, left_b = ring(own_a, 1), ring(own_b, -1)
     flat = jnp.transpose(w_qkv, (1, 0, 2))
-    w_near, tok_near = local_call(stage_body, (S(flat.shape, BF16), piece), None, (flat, tok), name="stage")
+    (w_near,) = local_call(stage_body, (S(flat.shape, BF16),), None, (flat,), name="stage")
+    parts_a = (own_a, right_a, ring(own_a, -1), ring(right_a, 1))
+    parts_b = (own_b, ring(own_b, 1), left_b, ring(left_b, -1))
     wide = S((1, 4, 64, 512), BF16)
     f0, f1 = local_call(
         project_body, (wide, wide),
-        idx, (tok_near, *t_parts, w_near), name="project",
+        idx, (*parts_a, *parts_b, w_near), name="project",
     )
     tmb, tma = frames(f1, 1), frames(f0, -1)
-    tok_late, _ = lax.optimization_barrier((tok_near, f0))
     q0, q1 = local_call(
-        query_body, (half, half), idx, (tok_late, *t_parts, w_near), name="query",
+        query_body, (half, half), idx, (*parts_a, *parts_b, w_near), name="query",
     )
     cot_late, _ = lax.optimization_barrier((cot, f0))
     c_parts = (ring(cot_late, 1), ring(cot_late, -1), ring(cot_late, 2))
@@ -349,28 +350,27 @@
             flops=4 * 6 * 2 * 1536 * 256 * 256 * 2, name="attend", limit=20,
         )
 
-    def settle(g_tmb, g_tma, g_hb, g_ha):
-        r_ha, r_hb = rows(g_hb, -1), rows(g_ha, 1)
-        s_tmb, s_tma = local_call(
+    def fold(g_tmb, g_tma, r_hb, r_ha):
+        return local_call(
             fold_body, (S(frame, BF16),) * 2, None, (g_tmb, g_tma, r_hb, r_ha),
             scratch=[pltpu.VMEM(frame, F32)], name="fold",
         )
-        return r_hb, r_ha, frames(s_tma, 1), frames(s_tmb, -1), s_tma
 
     att0, dq0, g_own0, *g0 = attend(0, q0, b0, f0, f1, tmb, tma, hb0, ha0)
     att1, dq1, g_own1, *g1 = attend(1, q1, b1, f0, f1, tmb, tma, hb1, ha1)
-    back0 = settle(*g0)
-    att0, _ = lax.optimization_barrier((att0, back0[4]))
-    back0 = back0[:4]
-    back1 = settle(*g1)[:4]
+    r_hb0, r_ha0 = rows(g0[3], 1), rows(g0[2], -1)
+    r_hb1, r_ha1 = rows(g1[3], 1), rows(g1[2], -1)
+    s_tmb, s_tma = fold(g0[0], g0[1], r_hb0, r_ha0)
+    back0 = (r_hb0, r_ha0, frames(s_tma, 1), frames(s_tmb, -1))
+    att0, _ = lax.optimization_barrier((att0, s_tma))
     parts = (S((512, 256), F32), piece, piece, piece)
-    m0, m1, m2, m3 = local_call(
-        mixed_body, parts, idx_out, (att0, att1, w_out), name="mix",
-    )
+    m0, m1, m2, m3 = local_call(mixed_body, parts, idx_out, (att0, att1, w_out), name="mix")
+    r_hb1, r_ha1, m1, m2 = lax.optimization_barrier((r_hb1, r_ha1, ring(m1, 1), ring(m2, -1)))
+    m3 = ring(m3, 2)
+    s_tmb, s_tma = fold(g1[0], g1[1], r_hb1, r_ha1)
+    back1 = (r_hb1, r_ha1, frames(s_tma, 1), frames(s_tmb, -1))
     out = (S((2, 4, 64, 256), BF16),)
-    (mixed,) = local_call(
-        sum_body, out, None, (m0, ring(m1, 1), ring(m2, -1), ring(m3, 2)), name="mixed_sum"
-    )
+    (mixed,) = local_call(sum_body, out, None, (m0, m1, m2, m3), name="mixed_sum")
     e0, e1, e2, e3 = local_call(
         grad_body, parts, idx_out, (dq0, g_own0, *back0, dq1, g_own1, *back1, flat),
         scratch=[pltpu.VMEM(pair, F32)], name="in_grad", limit=14,

time: 115 us -> 112 us (0.974)
  waiting for transfers between devices: 51 us -> 42.4 us
  starting transfers between devices: 37.7 us -> 42.3 us
    ppermute x8, waiting for transfers between devices: 13.5 us -> 6.72 us  [rows(): lax.ppermute(array, 'height', [(i, (i + by) % n_h) for i in range(n_h)])]
    ppermute x12 -> x15, starting transfers between devices: 12.1 us -> 16.9 us  [ring(): lax.ppermute(array, 'tensor', [(i, (i + by) % n_x) for i in range(n_x)])]
    ppermute x12 -> x15, waiting for transfers between devices: 26.7 us -> 23.4 us  [ring(): lax.ppermute(array, 'tensor', [(i, (i + by) % n_x) for i in range(n_x)])]
    ppermute x6, waiting for transfers between devices: 10.7 us -> 12.3 us  [frames(): return lax.ppermute(array, 'tm', [(i, (i + by) % n_t) for i in range(n_t)])]
    unnamed x10 -> x8, local copies, waits for them, and re-layouts: 2.37 us -> 1.42 us
  transfers between devices with their start and end apart: 26 -> 29, of which waited for: 10 -> 14; matrix products, arithmetic and copies ran while one was open for 0% -> 0% of each run, Pallas kernels for 17% -> 18%
where the time goes in v5:
time: 112 us; the launch traced here: 111 us
  waiting for transfers between devices  42.4 us (38%)
  starting transfers between devices  42.3 us (38%)
  Pallas kernels  22.7 us (20%)
  local copies, waits for them, and re-layouts  2.41 us (2%)
    ppermute x15, waiting for transfers between devices, ring(): lax.ppermute(array, 'tensor', [(i, (i + by) % n_x) for i in range(n_x)])  23.4 us
    pallas_call x13, Pallas kernels, local_call(): pl.pallas_call(body, out_shape=tuple(outs), in_specs=specs, out_specs=(vm...  22.7 us
    ppermute x15, starting transfers between devices, ring(): lax.ppermute(array, 'tensor', [(i, (i + by) % n_x) for i in range(n_x)])  16.9 us
    ppermute x6, starting transfers between devices, frames(): return lax.ppermute(array, 'tm', [(i, (i + by) % n_t) for i in range(n_t)])  14.6 us
    ppermute x6, waiting for transfers between devices, frames(): return lax.ppermute(array, 'tm', [(i, (i + by) % n_t) for i in range(n_t)])  12.3 us
    ppermute x8, starting transfers between devices, rows(): lax.ppermute(array, 'height', [(i, (i + by) % n_h) for i in range(n_h)])  10.8 us
    ppermute x8, waiting for transfers between devices, rows(): lax.ppermute(array, 'height', [(i, (i + by) % n_h) for i in range(n_h)])  6.72 us
  transfers between devices with their start and end apart: 29, of which 14 were waited for; matrix products, arithmetic and copies ran while one was open for 0% of the time, Pallas kernels for 18%

profile of v5, /device:TPU:22, one launch (start us, length us, event | category | flops | bytes accessed | tf_op | source)
XLA Modules:
  0.0 110.9 jit_solution(6207022610916755227)
XLA Ops:
  0.6 1.0 fusion
  1.6 0.6 collective-permute-start
  2.2 1.5 %collective-permute-start.4 = (bf16[256,256]{1,0:T(8,128)(2,1)S(1)}, bf16[256,256]{1,0:T(8,128)(2,1)S(1)}, u32[]{:S(2)}, u32[]{:S(2)}) collective-permute-start(bf16[256,256]{1,0:T(8,128)(2,1)S(1)} %bitcast.10), channel_id=1, source_target_pairs={{0,3},{1,0},{2,1},{3,2},{4,7},{5,4},{6,5},{7,6},{8,11},{9,8},{10,9... | collective-permute-start | bytes 393224 | tf_op jit(solution)/shard_map/ppermute | solution.py:295
  3.7 0.8 collective-permute-start.1
  4.6 2.4 %collective-permute-start.3 = (bf16[256,256]{1,0:T(8,128)(2,1)S(1)}, bf16[256,256]{1,0:T(8,128)(2,1)S(1)}, u32[]{:S(2)}, u32[]{:S(2)}) collective-permute-start(bf16[256,256]{1,0:T(8,128)(2,1)S(1)} %bitcast.11), channel_id=1, source_target_pairs={{0,1},{1,2},{2,3},{3,0},{4,5},{5,6},{6,7},{7,4},{8,9},{9,10},{10,1... | collective-permute-start | bytes 393224 | tf_op jit(solution)/shard_map/ppermute | solution.py:295
  7.0 0.8 collective-permute-done.a1
  7.7 0.9 collective-permute-start.2
  8.6 1.1 %collective-permute-done.4.b2 = bf16[256,256]{1,0:T(8,128)(2,1)S(1)} collective-permute-done((bf16[256,256]{1,0:T(8,128)(2,1)S(1)}, bf16[256,256]{1,0:T(8,128)(2,1)S(1)}, u32[]{:S(2)}, u32[]{:S(2)}) %collective-permute-start.4) | collective-permute-done | bytes 131104 | tf_op jit(solution)/shard_map/ppermute | solution.py:295
  9.7 0.3 collective-permute-start.5
  10.1 1.4 %copy-done = bf16[1024,3,256]{2,0,1:T(8,128)(2,1)S(1)} copy-done((bf16[1024,3,256]{2,0,1:T(8,128)(2,1)S(1)}, bf16[1024,3,256]{2,0,1:T(8,128)(2,1)}, u32[]{:S(2)}) %copy-start) | copy-done | bytes 1572888
  11.5 0.1 stage.1.w
  11.6 0.0 copy-start.3
  11.6 0.1 add_add_fusion.1.idx
  11.7 0.0 collective-permute-done.1.a2
  11.7 0.0 collective-permute-done.3.b1
  11.7 1.0 collective-permute-done.2.a3
  12.7 3.2 %collective-permute-done.5.b3 = bf16[256,256]{1,0:T(8,128)(2,1)S(1)} collective-permute-done((bf16[256,256]{1,0:T(8,128)(2,1)S(1)}, bf16[256,256]{1,0:T(8,128)(2,1)S(1)}, u32[]{:S(2)}, u32[]{:S(2)}) %collective-permute-start.5) | collective-permute-done | bytes 131104 | tf_op jit(solution)/shard_map/ppermute | solution.py:295
  15.9 1.2 %project.1 = (bf16[1,4,64,512]{3,2,1,0:T(8,128)(2,1)S(1)}, bf16[1,4,64,512]{3,2,1,0:T(8,128)(2,1)S(1)}) custom-call(s32[4]{0:T(128)S(1)} %add_add_fusion.1.idx, bf16[256,256]{1,0:T(8,128)(2,1)S(1)} %bitcast.16, bf16[256,256]{1,0:T(8,128)(2,1)S(1)} %collective-permute-done.a1, bf16[256,256]{1,0:T(8,128)(2,1)S(1)} %collective-permute-done.1.a2, ...), custom_call_target="tpu_custom_call" | custom-call | tf_op jit(solution)/shard_map/project/pallas_call | solution.py:270
  17.2 3.3 %collective-permute-start.6 = (bf16[1,4,64,512]{3,2,1,0:T(8,128)(2,1)S(1)}, bf16[1,4,64,512]{3,2,1,0:T(8,128)(2,1)}, u32[]{:S(2)}, u32[]{:S(2)}) collective-permute-start(bf16[1,4,64,512]{3,2,1,0:T(8,128)(2,1)S(1)} %get-tuple-element.54.f1), channel_id=1, source_target_pairs={{0,64},{64,128},{128,192},{192,0},{1,65},{65,129},{129,193},{193,1... | collective-permute-start | bytes 786440 | tf_op jit(solution)/shard_map/ppermute | solution.py:298
  20.5 3.1 %collective-permute-start.7 = (bf16[1,4,64,512]{3,2,1,0:T(8,128)(2,1)S(1)}, bf16[1,4,64,512]{3,2,1,0:T(8,128)(2,1)}, u32[]{:S(2)}, u32[]{:S(2)}) collective-permute-start(bf16[1,4,64,512]{3,2,1,0:T(8,128)(2,1)S(1)} %get-tuple-element.55.f0), channel_id=1, source_target_pairs={{0,192},{64,0},{128,64},{192,128},{1,193},{65,1},{129,65},{193,129... | collective-permute-start | bytes 786440 | tf_op jit(solution)/shard_map/ppermute | solution.py:298
  23.7 0.0 collective-permute-start.8
  23.7 2.0 %collective-permute-start.9 = (bf16[512,256]{1,0:T(8,128)(2,1)S(1)}, bf16[512,256]{1,0:T(8,128)(2,1)}, u32[]{:S(2)}, u32[]{:S(2)}) collective-permute-start(bf16[512,256]{1,0:T(8,128)(2,1)S(1)} %bitcast.19), channel_id=1, source_target_pairs={{0,3},{1,0},{2,1},{3,2},{4,7},{5,4},{6,5},{7,6},{8,11},{9,8},{10,9... | collective-permute-start | bytes 786440 | tf_op jit(solution)/shard_map/ppermute | solution.py:295
  25.7 7.0 %collective-permute-done.6.tmb = bf16[1,4,64,512]{3,2,1,0:T(8,128)(2,1)} collective-permute-done((bf16[1,4,64,512]{3,2,1,0:T(8,128)(2,1)S(1)}, bf16[1,4,64,512]{3,2,1,0:T(8,128)(2,1)}, u32[]{:S(2)}, u32[]{:S(2)}) %collective-permute-start.6) | collective-permute-done | bytes 262176 | tf_op jit(solution)/shard_map/ppermute | solution.py:298
  32.7 0.6 collective-permute-done.7.tma
  33.4 2.9 %collective-permute-done.9.x2 = bf16[512,256]{1,0:T(8,128)(2,1)} collective-permute-done((bf16[512,256]{1,0:T(8,128)(2,1)S(1)}, bf16[512,256]{1,0:T(8,128)(2,1)}, u32[]{:S(2)}, u32[]{:S(2)}) %collective-permute-start.9) | collective-permute-done | bytes 262176 | tf_op jit(solution)/shard_map/ppermute | solution.py:295
  36.3 1.1 %edges.1 = (bf16[4,3,64,256]{3,2,1,0:T(8,128)(2,1)S(1)}, bf16[4,3,64,256]{3,2,1,0:T(8,128)(2,1)S(1)}, bf16[4,3,64,256]{3,2,1,0:T(8,128)(2,1)S(1)}, bf16[4,3,64,256]{3,2,1,0:T(8,128)(2,1)S(1)}) custom-call(bf16[1,4,64,512]{3,2,1,0:T(8,128)(2,1)} %collective-permute-done.6.tmb, bf16[1,4,64,512]{3,2,1,0:T(8,128)(2,1)S(1)} %get-tuple-element.55.f0, ...), custom_call_target="tpu_custom_call" | custom-call | tf_op jit(solution)/shard_map/edges/pallas_call | solution.py:270
  37.4 0.0 copy-start.2
  37.4 0.1 collective-permute-start.11
  37.5 2.6 %collective-permute-start.12 = (bf16[4,3,64,256]{3,2,1,0:T(8,128)(2,1)S(1)}, bf16[4,3,64,256]{3,2,1,0:T(8,128)(2,1)S(1)}, u32[]{:S(2)}, u32[]{:S(2)}) collective-permute-start(bf16[4,3,64,256]{3,2,1,0:T(8,128)(2,1)S(1)} %get-tuple-element.66), channel_id=1, source_target_pairs={{0,60},{4,0},{8,4},{12,8},{16,12},{20,16},{24,20},{28,24},{32,28},... | collective-permute-start | bytes 1179656 | tf_op jit(solution)/shard_map/ppermute | solution.py:301
  40.2 0.1 and_convert_fusion.valid
  40.3 1.0 query.1
  41.3 1.6 %back.1 = (bf16[512,128]{1,0:T(8,128)(2,1)S(1)}, bf16[512,128]{1,0:T(8,128)(2,1)S(1)}) custom-call(s32[4]{0:T(128)S(1)} %add_add_fusion.1.idx, bf16[512,256]{1,0:T(8,128)(2,1)S(1)} %bitcast.21, bf16[512,256]{1,0:T(8,128)(2,1)} %collective-permute-done.8.x1, bf16[512,256]{1,0:T(8,128)(2,1)} %collective-permute-done.9.x2, ...), custom_call_target="tpu_custom_call" | custom-call | tf_op jit(solution)/shard_map/back/pallas_call | solution.py:270
  42.9 6.7 %collective-permute-done.11.hb = bf16[4,3,64,256]{3,2,1,0:T(8,128)(2,1)S(1)} collective-permute-done((bf16[4,3,64,256]{3,2,1,0:T(8,128)(2,1)S(1)}, bf16[4,3,64,256]{3,2,1,0:T(8,128)(2,1)S(1)}, u32[]{:S(2)}, u32[]{:S(2)}) %collective-permute-start.11) | collective-permute-done | bytes 393248 | tf_op jit(solution)/shard_map/ppermute | solution.py:301
  49.5 0.1 collective-permute-start.15
  49.6 2.5 %collective-permute-start.16 = (bf16[4,3,64,256]{3,2,1,0:T(8,128)(2,1)S(1)}, bf16[4,3,64,256]{3,2,1,0:T(8,128)(2,1)S(1)}, u32[]{:S(2)}, u32[]{:S(2)}) collective-permute-start(bf16[4,3,64,256]{3,2,1,0:T(8,128)(2,1)S(1)} %get-tuple-element.79), channel_id=1, source_target_pairs={{0,60},{4,0},{8,4},{12,8},{16,12},{20,16},{24,20},{28,24},{32,28},... | collective-permute-start | bytes 1179656 | tf_op jit(solution)/shard_map/ppermute | solution.py:301
  52.2 6.7 %attend.2 = (bf16[512,128]{1,0:T(8,128)(2,1)S(1)}, bf16[512,128]{1,0:T(8,128)(2,1)S(1)}, f32[2,4,64,256]{3,2,1,0:T(8,128)S(1)}, f32[1,4,64,256]{3,2,1,0:T(8,128)...) custom-call(s32[4,10]{1,0:T(4,128)S(1)} %and_convert_fusion.valid, ...), custom_call_target="tpu_custom_call" | custom-call | flops 9663676416 | tf_op jit(solution)/shard_map/attend/pallas_call | solution.py:270
  58.8 0.1 collective-permute-start.13
  58.9 2.6 %collective-permute-start.14 = (bf16[4,3,64,256]{3,2,1,0:T(8,128)(2,1)S(1)}, bf16[4,3,64,256]{3,2,1,0:T(8,128)(2,1)S(1)}, u32[]{:S(2)}, u32[]{:S(2)}) collective-permute-start(bf16[4,3,64,256]{3,2,1,0:T(8,128)(2,1)S(1)} %get-tuple-element.73), channel_id=1, source_target_pairs={{0,60},{4,0},{8,4},{12,8},{16,12},{20,16},{24,20},{28,24},{32,28},... | collective-permute-start | bytes 1179656 | tf_op jit(solution)/shard_map/ppermute | solution.py:301
  61.6 6.7 %attend.3 = (bf16[512,128]{1,0:T(8,128)(2,1)S(1)}, bf16[512,128]{1,0:T(8,128)(2,1)S(1)}, f32[2,4,64,256]{3,2,1,0:T(8,128)S(1)}, f32[1,4,64,256]{3,2,1,0:T(8,128)...) custom-call(s32[4,10]{1,0:T(4,128)S(1)} %and_convert_fusion.valid, ...), custom_call_target="tpu_custom_call" | custom-call | flops 9663676416 | tf_op jit(solution)/shard_map/attend/pallas_call | solution.py:270
  68.2 0.1 collective-permute-start.17
  68.3 2.6 %collective-permute-start.18 = (bf16[4,3,64,256]{3,2,1,0:T(8,128)(2,1)S(1)}, bf16[4,3,64,256]{3,2,1,0:T(8,128)(2,1)S(1)}, u32[]{:S(2)}, u32[]{:S(2)}) collective-permute-start(bf16[4,3,64,256]{3,2,1,0:T(8,128)(2,1)S(1)} %get-tuple-element.83), channel_id=1, source_target_pairs={{0,60},{4,0},{8,4},{12,8},{16,12},{20,16},{24,20},{28,24},{32,28},... | collective-permute-start | bytes 1179656 | tf_op jit(solution)/shard_map/ppermute | solution.py:301
  70.9 0.1 add_add_fusion.idx
  71.0 0.1 fold.2
  71.1 1.0 mix.1
  72.1 0.5 collective-permute-start.19
  72.6 1.6 %collective-permute-start.20 = (bf16[512,256]{1,0:T(8,128)(2,1)S(1)}, bf16[512,256]{1,0:T(8,128)(2,1)S(1)}, u32[]{:S(2)}, u32[]{:S(2)}) collective-permute-start(bf16[512,256]{1,0:T(8,128)(2,1)S(1)} %get-tuple-element.85), channel_id=1, source_target_pairs={{0,3},{1,0},{2,1},{3,2},{4,7},{5,4},{6,5},{7,6},{8,11},{9,8},{10,9... | collective-permute-start | bytes 786440 | tf_op jit(solution)/shard_map/ppermute | solution.py:295
  74.2 1.4 %collective-permute-start.22 = (bf16[1,4,64,256]{3,2,1,0:T(8,128)(2,1)S(1)}, bf16[1,4,64,256]{3,2,1,0:T(8,128)(2,1)S(1)}, u32[]{:S(2)}, u32[]{:S(2)}) collective-permute-start(bf16[1,4,64,256]{3,2,1,0:T(8,128)(2,1)S(1)} %get-tuple-element.74), channel_id=1, source_target_pairs={{0,64},{64,128},{128,192},{192,0},{1,65},{65,129},{129,193},{193,1... | collective-permute-start | bytes 393224 | tf_op jit(solution)/shard_map/ppermute | solution.py:298
  75.6 3.0 %collective-permute-done.19.b = bf16[512,256]{1,0:T(8,128)(2,1)S(1)} collective-permute-done((bf16[512,256]{1,0:T(8,128)(2,1)S(1)}, bf16[512,256]{1,0:T(8,128)(2,1)S(1)}, u32[]{:S(2)}, u32[]{:S(2)}) %collective-permute-start.19) | collective-permute-done | bytes 262176 | tf_op jit(solution)/shard_map/ppermute | solution.py:295
  78.6 2.5 %collective-permute-start.23 = (bf16[1,4,64,256]{3,2,1,0:T(8,128)(2,1)S(1)}, bf16[1,4,64,256]{3,2,1,0:T(8,128)(2,1)S(1)}, u32[]{:S(2)}, u32[]{:S(2)}) collective-permute-start(bf16[1,4,64,256]{3,2,1,0:T(8,128)(2,1)S(1)} %get-tuple-element.91), channel_id=1, source_target_pairs={{0,192},{64,0},{128,64},{192,128},{1,193},{65,1},{129,65},{193,129... | collective-permute-start | bytes 393224 | tf_op jit(solution)/shard_map/ppermute | solution.py:298
  81.1 0.0 collective-permute-done.18.r_ha.ha1
  81.1 0.1 fold.3
  81.2 1.4 %collective-permute-start.24 = (bf16[1,4,64,256]{3,2,1,0:T(8,128)(2,1)S(1)}, bf16[1,4,64,256]{3,2,1,0:T(8,128)(2,1)S(1)}, u32[]{:S(2)}, u32[]{:S(2)}) collective-permute-start(bf16[1,4,64,256]{3,2,1,0:T(8,128)(2,1)S(1)} %get-tuple-element.98), channel_id=1, source_target_pairs={{0,64},{64,128},{128,192},{192,0},{1,65},{65,129},{129,193},{193,1... | collective-permute-start | bytes 393224 | tf_op jit(solution)/shard_map/ppermute | solution.py:298
  82.6 2.8 %collective-permute-start.25 = (bf16[1,4,64,256]{3,2,1,0:T(8,128)(2,1)S(1)}, bf16[1,4,64,256]{3,2,1,0:T(8,128)(2,1)S(1)}, u32[]{:S(2)}, u32[]{:S(2)}) collective-permute-start(bf16[1,4,64,256]{3,2,1,0:T(8,128)(2,1)S(1)} %get-tuple-element.99), channel_id=1, source_target_pairs={{0,192},{64,0},{128,64},{192,128},{1,193},{65,1},{129,65},{193,129... | collective-permute-start | bytes 393224 | tf_op jit(solution)/shard_map/ppermute | solution.py:298
  85.4 0.7 collective-permute-start.21
  86.1 0.6 collective-permute-done.22.tb0
  86.8 2.4 %collective-permute-done.23.ta0 = bf16[1,4,64,256]{3,2,1,0:T(8,128)(2,1)S(1)} collective-permute-done((bf16[1,4,64,256]{3,2,1,0:T(8,128)(2,1)S(1)}, bf16[1,4,64,256]{3,2,1,0:T(8,128)(2,1)S(1)}, u32[]{:S(2)}, u32[]{:S(2)}) %collective-permute-start.23) | collective-permute-done | bytes 131104 | tf_op jit(solution)/shard_map/ppermute | solution.py:298
  89.1 1.6 %collective-permute-done.25.ta1 = bf16[1,4,64,256]{3,2,1,0:T(8,128)(2,1)S(1)} collective-permute-done((bf16[1,4,64,256]{3,2,1,0:T(8,128)(2,1)S(1)}, bf16[1,4,64,256]{3,2,1,0:T(8,128)(2,1)S(1)}, u32[]{:S(2)}, u32[]{:S(2)}) %collective-permute-start.25) | collective-permute-done | bytes 131104 | tf_op jit(solution)/shard_map/ppermute | solution.py:298
  90.7 1.6 %in_grad.1 = (f32[512,256]{1,0:T(8,128)S(1)}, bf16[512,256]{1,0:T(8,128)(2,1)S(1)}, bf16[512,256]{1,0:T(8,128)(2,1)S(1)}, bf16[512,256]{1,0:T(8,128)(2,1)S(1)}) custom-call(s32[4]{0:T(128)S(1)} %add_add_fusion.idx, bf16[512,128]{1,0:T(8,128)(2,1)S(1)} %get-tuple-element.89.dq0, f32[2,4,64,256]{3,2,1,0:T(8,128)S(1)} %get-tuple-element.90.own0, ...), custom_call_target="tpu_custom_call" | custom-call | tf_op jit(solution)/shard_map/in_grad/pallas_call | solution.py:270
  92.3 3.9 %collective-permute-start.26 = (bf16[512,256]{1,0:T(8,128)(2,1)S(1)}, bf16[512,256]{1,0:T(8,128)(2,1)S(1)}, u32[]{:S(2)}, u32[]{:S(2)}) collective-permute-start(bf16[512,256]{1,0:T(8,128)(2,1)S(1)} %get-tuple-element.101), channel_id=1, source_target_pairs={{0,1},{1,2},{2,3},{3,0},{4,5},{5,6},{6,7},{7,4},{8,9},{9,10},{10,1... | collective-permute-start | bytes 786440 | tf_op jit(solution)/shard_map/ppermute | solution.py:295
  96.2 1.6 %collective-permute-start.28 = (bf16[512,256]{1,0:T(8,128)(2,1)S(1)}, bf16[512,256]{1,0:T(8,128)(2,1)S(1)}, u32[]{:S(2)}, u32[]{:S(2)}) collective-permute-start(bf16[512,256]{1,0:T(8,128)(2,1)S(1)} %get-tuple-element.103), channel_id=1, source_target_pairs={{0,2},{1,3},{2,0},{3,1},{4,6},{5,7},{6,4},{7,5},{8,10},{9,11},{10,... | collective-permute-start | bytes 786440 | tf_op jit(solution)/shard_map/ppermute | solution.py:295
  97.8 0.8 mixed_sum.1
  98.6 8.0 %collective-permute-done.26.b = bf16[512,256]{1,0:T(8,128)(2,1)S(1)} collective-permute-done((bf16[512,256]{1,0:T(8,128)(2,1)S(1)}, bf16[512,256]{1,0:T(8,128)(2,1)S(1)}, u32[]{:S(2)}, u32[]{:S(2)}) %collective-permute-start.26) | collective-permute-done | bytes 262176 | tf_op jit(solution)/shard_map/ppermute | solution.py:295
  106.6 3.4 %collective-permute-done.27.c = bf16[512,256]{1,0:T(8,128)(2,1)S(1)} collective-permute-done((bf16[512,256]{1,0:T(8,128)(2,1)S(1)}, bf16[512,256]{1,0:T(8,128)(2,1)S(1)}, u32[]{:S(2)}, u32[]{:S(2)}) %collective-permute-start.27) | collective-permute-done | bytes 262176 | tf_op jit(solution)/shard_map/ppermute | solution.py:295
  110.1 0.8 in_grad_sum.1
  (21 shorter events, 0.1 us)
Async XLA Ops:
  1.6 6.1 %collective-permute-start = (bf16[256,256]{1,0:T(8,128)(2,1)S(1)}, bf16[256,256]{1,0:T(8,128)(2,1)S(1)}, u32[]{:S(2)}, u32[]{:S(2)}) collective-permute-start(bf16[256,256]{1,0:T(8,128)(2,1)S(1)} %bitcast.14), channel_id=1, source_target_pairs={{0,1},{1,2},{2,3},{3,0},{4,5},{5,6},{6,7},{7,4},{8,9},{9,10},{10,1... | collective-permute-start | bytes 393224 | tf_op jit(solution)/shard_map/ppermute | solution.py:295
  2.2 7.6 %collective-permute-start.4 = (bf16[256,256]{1,0:T(8,128)(2,1)S(1)}, bf16[256,256]{1,0:T(8,128)(2,1)S(1)}, u32[]{:S(2)}, u32[]{:S(2)}) collective-permute-start(bf16[256,256]{1,0:T(8,128)(2,1)S(1)} %bitcast.10), channel_id=1, source_target_pairs={{0,3},{1,0},{2,1},{3,2},{4,7},{5,4},{6,5},{7,6},{8,11},{9,8},{10,9... | collective-permute-start | bytes 393224 | tf_op jit(solution)/shard_map/ppermute | solution.py:295
  3.7 8.0 %collective-permute-start.1 = (bf16[256,256]{1,0:T(8,128)(2,1)S(1)}, bf16[256,256]{1,0:T(8,128)(2,1)S(1)}, u32[]{:S(2)}, u32[]{:S(2)}) collective-permute-start(bf16[256,256]{1,0:T(8,128)(2,1)S(1)} %bitcast.15), channel_id=1, source_target_pairs={{0,3},{1,0},{2,1},{3,2},{4,7},{5,4},{6,5},{7,6},{8,11},{9,8},{10,9... | collective-permute-start | bytes 393224 | tf_op jit(solution)/shard_map/ppermute | solution.py:295
  4.6 7.2 %collective-permute-start.3 = (bf16[256,256]{1,0:T(8,128)(2,1)S(1)}, bf16[256,256]{1,0:T(8,128)(2,1)S(1)}, u32[]{:S(2)}, u32[]{:S(2)}) collective-permute-start(bf16[256,256]{1,0:T(8,128)(2,1)S(1)} %bitcast.11), channel_id=1, source_target_pairs={{0,1},{1,2},{2,3},{3,0},{4,5},{5,6},{6,7},{7,4},{8,9},{9,10},{10,1... | collective-permute-start | bytes 393224 | tf_op jit(solution)/shard_map/ppermute | solution.py:295
  7.7 5.0 %collective-permute-start.2 = (bf16[256,256]{1,0:T(8,128)(2,1)S(1)}, bf16[256,256]{1,0:T(8,128)(2,1)S(1)}, u32[]{:S(2)}, u32[]{:S(2)}) collective-permute-start(bf16[256,256]{1,0:T(8,128)(2,1)S(1)} %collective-permute-done.a1), channel_id=1, source_target_pairs={{0,1},{1,2},{2,3},{3,0},{4,5},{5,6},{6,7},{7,4},{8,9},{9,10},{10,1... | collective-permute-start | bytes 393224 | tf_op jit(solution)/shard_map/ppermute | solution.py:295
  9.7 6.2 %collective-permute-start.5 = (bf16[256,256]{1,0:T(8,128)(2,1)S(1)}, bf16[256,256]{1,0:T(8,128)(2,1)S(1)}, u32[]{:S(2)}, u32[]{:S(2)}) collective-permute-start(bf16[256,256]{1,0:T(8,128)(2,1)S(1)} %collective-permute-done.4.b2), channel_id=1, source_target_pairs={{0,3},{1,0},{2,1},{3,2},{4,7},{5,4},{6,5},{7,6},{8,11},{9,8},{10,9... | collective-permute-start | bytes 393224 | tf_op jit(solution)/shard_map/ppermute | solution.py:295
  10.1 1.4 %copy-start = (bf16[1024,3,256]{2,0,1:T(8,128)(2,1)S(1)}, bf16[1024,3,256]{2,0,1:T(8,128)(2,1)}, u32[]{:S(2)}) copy-start(bf16[1024,3,256]{2,0,1:T(8,128)(2,1)} %param.6) | copy-start | bytes 4718596
  11.6 12.1 %copy-start.3 = (bf16[2,4,64,256]{3,2,1,0:T(8,128)(2,1)S(1)}, bf16[2,4,64,256]{3,2,1,0:T(8,128)(2,1)}, u32[]{:S(2)}) copy-start(bf16[2,4,64,256]{3,2,1,0:T(8,128)(2,1)} %param.5) | copy-start | bytes 786436
  17.2 15.5 %collective-permute-start.6 = (bf16[1,4,64,512]{3,2,1,0:T(8,128)(2,1)S(1)}, bf16[1,4,64,512]{3,2,1,0:T(8,128)(2,1)}, u32[]{:S(2)}, u32[]{:S(2)}) collective-permute-start(bf16[1,4,64,512]{3,2,1,0:T(8,128)(2,1)S(1)} %get-tuple-element.54.f1), channel_id=1, source_target_pairs={{0,64},{64,128},{128,192},{192,0},{1,65},{65,129},{129,193},{193,1... | collective-permute-start | bytes 786440 | tf_op jit(solution)/shard_map/ppermute | solution.py:298
  20.5 12.8 %collective-permute-start.7 = (bf16[1,4,64,512]{3,2,1,0:T(8,128)(2,1)S(1)}, bf16[1,4,64,512]{3,2,1,0:T(8,128)(2,1)}, u32[]{:S(2)}, u32[]{:S(2)}) collective-permute-start(bf16[1,4,64,512]{3,2,1,0:T(8,128)(2,1)S(1)} %get-tuple-element.55.f0), channel_id=1, source_target_pairs={{0,192},{64,0},{128,64},{192,128},{1,193},{65,1},{129,65},{193,129... | collective-permute-start | bytes 786440 | tf_op jit(solution)/shard_map/ppermute | solution.py:298
  23.7 9.7 %collective-permute-start.8 = (bf16[512,256]{1,0:T(8,128)(2,1)S(1)}, bf16[512,256]{1,0:T(8,128)(2,1)}, u32[]{:S(2)}, u32[]{:S(2)}) collective-permute-start(bf16[512,256]{1,0:T(8,128)(2,1)S(1)} %bitcast.18), channel_id=1, source_target_pairs={{0,1},{1,2},{2,3},{3,0},{4,5},{5,6},{6,7},{7,4},{8,9},{9,10},{10,1... | collective-permute-start | bytes 786440 | tf_op jit(solution)/shard_map/ppermute | solution.py:295
  23.7 12.6 %collective-permute-start.9 = (bf16[512,256]{1,0:T(8,128)(2,1)S(1)}, bf16[512,256]{1,0:T(8,128)(2,1)}, u32[]{:S(2)}, u32[]{:S(2)}) collective-permute-start(bf16[512,256]{1,0:T(8,128)(2,1)S(1)} %bitcast.19), channel_id=1, source_target_pairs={{0,3},{1,0},{2,1},{3,2},{4,7},{5,4},{6,5},{7,6},{8,11},{9,8},{10,9... | collective-permute-start | bytes 786440 | tf_op jit(solution)/shard_map/ppermute | solution.py:295
  25.7 10.6 %collective-permute-start.10 = (bf16[512,256]{1,0:T(8,128)(2,1)S(1)}, bf16[512,256]{1,0:T(8,128)(2,1)}, u32[]{:S(2)}, u32[]{:S(2)}) collective-permute-start(bf16[512,256]{1,0:T(8,128)(2,1)S(1)} %bitcast.20), channel_id=1, source_target_pairs={{0,2},{1,3},{2,0},{3,1},{4,6},{5,7},{6,4},{7,5},{8,10},{9,11},{10,... | collective-permute-start | bytes 786440 | tf_op jit(solution)/shard_map/ppermute | solution.py:295
  37.4 3.8 %copy-start.2 = (bf16[256,1024]{1,0:T(8,128)(2,1)S(1)}, bf16[256,1024]{1,0:T(8,128)(2,1)}, u32[]{:S(2)}) copy-start(bf16[256,1024]{1,0:T(8,128)(2,1)} %w.3) | copy-start | bytes 1572868
  37.4 12.1 %collective-permute-start.11 = (bf16[4,3,64,256]{3,2,1,0:T(8,128)(2,1)S(1)}, bf16[4,3,64,256]{3,2,1,0:T(8,128)(2,1)S(1)}, u32[]{:S(2)}, u32[]{:S(2)}) collective-permute-start(bf16[4,3,64,256]{3,2,1,0:T(8,128)(2,1)S(1)} %get-tuple-element.65), channel_id=1, source_target_pairs={{0,4},{4,8},{8,12},{12,16},{16,20},{20,24},{24,28},{28,32},{32,36}... | collective-permute-start | bytes 1179656 | tf_op jit(solution)/shard_map/ppermute | solution.py:301
  37.5 12.0 %collective-permute-start.12 = (bf16[4,3,64,256]{3,2,1,0:T(8,128)(2,1)S(1)}, bf16[4,3,64,256]{3,2,1,0:T(8,128)(2,1)S(1)}, u32[]{:S(2)}, u32[]{:S(2)}) collective-permute-start(bf16[4,3,64,256]{3,2,1,0:T(8,128)(2,1)S(1)} %get-tuple-element.66), channel_id=1, source_target_pairs={{0,60},{4,0},{8,4},{12,8},{16,12},{20,16},{24,20},{28,24},{32,28},... | collective-permute-start | bytes 1179656 | tf_op jit(solution)/shard_map/ppermute | solution.py:301
  49.5 12.0 %collective-permute-start.15 = (bf16[4,3,64,256]{3,2,1,0:T(8,128)(2,1)S(1)}, bf16[4,3,64,256]{3,2,1,0:T(8,128)(2,1)S(1)}, u32[]{:S(2)}, u32[]{:S(2)}) collective-permute-start(bf16[4,3,64,256]{3,2,1,0:T(8,128)(2,1)S(1)} %get-tuple-element.78), channel_id=1, source_target_pairs={{0,4},{4,8},{8,12},{12,16},{16,20},{20,24},{24,28},{28,32},{32,36}... | collective-permute-start | bytes 1179656 | tf_op jit(solution)/shard_map/ppermute | solution.py:301
  49.6 11.9 %collective-permute-start.16 = (bf16[4,3,64,256]{3,2,1,0:T(8,128)(2,1)S(1)}, bf16[4,3,64,256]{3,2,1,0:T(8,128)(2,1)S(1)}, u32[]{:S(2)}, u32[]{:S(2)}) collective-permute-start(bf16[4,3,64,256]{3,2,1,0:T(8,128)(2,1)S(1)} %get-tuple-element.79), channel_id=1, source_target_pairs={{0,60},{4,0},{8,4},{12,8},{16,12},{20,16},{24,20},{28,24},{32,28},... | collective-permute-start | bytes 1179656 | tf_op jit(solution)/shard_map/ppermute | solution.py:301
  58.8 12.2 %collective-permute-start.13 = (bf16[4,3,64,256]{3,2,1,0:T(8,128)(2,1)S(1)}, bf16[4,3,64,256]{3,2,1,0:T(8,128)(2,1)S(1)}, u32[]{:S(2)}, u32[]{:S(2)}) collective-permute-start(bf16[4,3,64,256]{3,2,1,0:T(8,128)(2,1)S(1)} %get-tuple-element.72), channel_id=1, source_target_pairs={{0,4},{4,8},{8,12},{12,16},{16,20},{20,24},{24,28},{28,32},{32,36}... | collective-permute-start | bytes 1179656 | tf_op jit(solution)/shard_map/ppermute | solution.py:301
  58.9 12.1 %collective-permute-start.14 = (bf16[4,3,64,256]{3,2,1,0:T(8,128)(2,1)S(1)}, bf16[4,3,64,256]{3,2,1,0:T(8,128)(2,1)S(1)}, u32[]{:S(2)}, u32[]{:S(2)}) collective-permute-start(bf16[4,3,64,256]{3,2,1,0:T(8,128)(2,1)S(1)} %get-tuple-element.73), channel_id=1, source_target_pairs={{0,60},{4,0},{8,4},{12,8},{16,12},{20,16},{24,20},{28,24},{32,28},... | collective-permute-start | bytes 1179656 | tf_op jit(solution)/shard_map/ppermute | solution.py:301
  68.2 12.9 %collective-permute-start.17 = (bf16[4,3,64,256]{3,2,1,0:T(8,128)(2,1)S(1)}, bf16[4,3,64,256]{3,2,1,0:T(8,128)(2,1)S(1)}, u32[]{:S(2)}, u32[]{:S(2)}) collective-permute-start(bf16[4,3,64,256]{3,2,1,0:T(8,128)(2,1)S(1)} %get-tuple-element.82), channel_id=1, source_target_pairs={{0,4},{4,8},{8,12},{12,16},{16,20},{20,24},{24,28},{28,32},{32,36}... | collective-permute-start | bytes 1179656 | tf_op jit(solution)/shard_map/ppermute | solution.py:301
  68.3 12.8 %collective-permute-start.18 = (bf16[4,3,64,256]{3,2,1,0:T(8,128)(2,1)S(1)}, bf16[4,3,64,256]{3,2,1,0:T(8,128)(2,1)S(1)}, u32[]{:S(2)}, u32[]{:S(2)}) collective-permute-start(bf16[4,3,64,256]{3,2,1,0:T(8,128)(2,1)S(1)} %get-tuple-element.83), channel_id=1, source_target_pairs={{0,60},{4,0},{8,4},{12,8},{16,12},{20,16},{24,20},{28,24},{32,28},... | collective-permute-start | bytes 1179656 | tf_op jit(solution)/shard_map/ppermute | solution.py:301
  71.0 19.7 %copy-start.1 = (bf16[1024,3,256]{2,0,1:T(8,128)(2,1)S(1)}, bf16[1024,3,256]{2,0,1:T(8,128)(2,1)}, u32[]{:S(2)}) copy-start(bf16[1024,3,256]{2,0,1:T(8,128)(2,1)} %param.6) | copy-start | bytes 4718596
  72.1 6.4 %collective-permute-start.19 = (bf16[512,256]{1,0:T(8,128)(2,1)S(1)}, bf16[512,256]{1,0:T(8,128)(2,1)S(1)}, u32[]{:S(2)}, u32[]{:S(2)}) collective-permute-start(bf16[512,256]{1,0:T(8,128)(2,1)S(1)} %get-tuple-element.84), channel_id=1, source_target_pairs={{0,1},{1,2},{2,3},{3,0},{4,5},{5,6},{6,7},{7,4},{8,9},{9,10},{10,1... | collective-permute-start | bytes 786440 | tf_op jit(solution)/shard_map/ppermute | solution.py:295
  72.6 8.5 %collective-permute-start.20 = (bf16[512,256]{1,0:T(8,128)(2,1)S(1)}, bf16[512,256]{1,0:T(8,128)(2,1)S(1)}, u32[]{:S(2)}, u32[]{:S(2)}) collective-permute-start(bf16[512,256]{1,0:T(8,128)(2,1)S(1)} %get-tuple-element.85), channel_id=1, source_target_pairs={{0,3},{1,0},{2,1},{3,2},{4,7},{5,4},{6,5},{7,6},{8,11},{9,8},{10,9... | collective-permute-start | bytes 786440 | tf_op jit(solution)/shard_map/ppermute | solution.py:295
  74.2 12.6 %collective-permute-start.22 = (bf16[1,4,64,256]{3,2,1,0:T(8,128)(2,1)S(1)}, bf16[1,4,64,256]{3,2,1,0:T(8,128)(2,1)S(1)}, u32[]{:S(2)}, u32[]{:S(2)}) collective-permute-start(bf16[1,4,64,256]{3,2,1,0:T(8,128)(2,1)S(1)} %get-tuple-element.74), channel_id=1, source_target_pairs={{0,64},{64,128},{128,192},{192,0},{1,65},{65,129},{129,193},{193,1... | collective-permute-start | bytes 393224 | tf_op jit(solution)/shard_map/ppermute | solution.py:298
  78.6 10.6 %collective-permute-start.23 = (bf16[1,4,64,256]{3,2,1,0:T(8,128)(2,1)S(1)}, bf16[1,4,64,256]{3,2,1,0:T(8,128)(2,1)S(1)}, u32[]{:S(2)}, u32[]{:S(2)}) collective-permute-start(bf16[1,4,64,256]{3,2,1,0:T(8,128)(2,1)S(1)} %get-tuple-element.91), channel_id=1, source_target_pairs={{0,192},{64,0},{128,64},{192,128},{1,193},{65,1},{129,65},{193,129... | collective-permute-start | bytes 393224 | tf_op jit(solution)/shard_map/ppermute | solution.py:298
  81.2 7.9 %collective-permute-start.24 = (bf16[1,4,64,256]{3,2,1,0:T(8,128)(2,1)S(1)}, bf16[1,4,64,256]{3,2,1,0:T(8,128)(2,1)S(1)}, u32[]{:S(2)}, u32[]{:S(2)}) collective-permute-start(bf16[1,4,64,256]{3,2,1,0:T(8,128)(2,1)S(1)} %get-tuple-element.98), channel_id=1, source_target_pairs={{0,64},{64,128},{128,192},{192,0},{1,65},{65,129},{129,193},{193,1... | collective-permute-start | bytes 393224 | tf_op jit(solution)/shard_map/ppermute | solution.py:298
  82.6 8.1 %collective-permute-start.25 = (bf16[1,4,64,256]{3,2,1,0:T(8,128)(2,1)S(1)}, bf16[1,4,64,256]{3,2,1,0:T(8,128)(2,1)S(1)}, u32[]{:S(2)}, u32[]{:S(2)}) collective-permute-start(bf16[1,4,64,256]{3,2,1,0:T(8,128)(2,1)S(1)} %get-tuple-element.99), channel_id=1, source_target_pairs={{0,192},{64,0},{128,64},{192,128},{1,193},{65,1},{129,65},{193,129... | collective-permute-start | bytes 393224 | tf_op jit(solution)/shard_map/ppermute | solution.py:298
  85.4 12.4 %collective-permute-start.21 = (bf16[512,256]{1,0:T(8,128)(2,1)S(1)}, bf16[512,256]{1,0:T(8,128)(2,1)S(1)}, u32[]{:S(2)}, u32[]{:S(2)}) collective-permute-start(bf16[512,256]{1,0:T(8,128)(2,1)S(1)} %get-tuple-element.88), channel_id=1, source_target_pairs={{0,2},{1,3},{2,0},{3,1},{4,6},{5,7},{6,4},{7,5},{8,10},{9,11},{10,... | collective-permute-start | bytes 786440 | tf_op jit(solution)/shard_map/ppermute | solution.py:295
  92.3 14.3 %collective-permute-start.26 = (bf16[512,256]{1,0:T(8,128)(2,1)S(1)}, bf16[512,256]{1,0:T(8,128)(2,1)S(1)}, u32[]{:S(2)}, u32[]{:S(2)}) collective-permute-start(bf16[512,256]{1,0:T(8,128)(2,1)S(1)} %get-tuple-element.101), channel_id=1, source_target_pairs={{0,1},{1,2},{2,3},{3,0},{4,5},{5,6},{6,7},{7,4},{8,9},{9,10},{10,1... | collective-permute-start | bytes 786440 | tf_op jit(solution)/shard_map/ppermute | solution.py:295
  96.2 13.8 %collective-permute-start.27 = (bf16[512,256]{1,0:T(8,128)(2,1)S(1)}, bf16[512,256]{1,0:T(8,128)(2,1)S(1)}, u32[]{:S(2)}, u32[]{:S(2)}) collective-permute-start(bf16[512,256]{1,0:T(8,128)(2,1)S(1)} %get-tuple-element.102), channel_id=1, source_target_pairs={{0,3},{1,0},{2,1},{3,2},{4,7},{5,4},{6,5},{7,6},{8,11},{9,8},{10,9... | collective-permute-start | bytes 786440 | tf_op jit(solution)/shard_map/ppermute | solution.py:295
  96.2 13.8 %collective-permute-start.28 = (bf16[512,256]{1,0:T(8,128)(2,1)S(1)}, bf16[512,256]{1,0:T(8,128)(2,1)S(1)}, u32[]{:S(2)}, u32[]{:S(2)}) collective-permute-start(bf16[512,256]{1,0:T(8,128)(2,1)S(1)} %get-tuple-element.103), channel_id=1, source_target_pairs={{0,2},{1,3},{2,0},{3,1},{4,6},{5,7},{6,4},{7,5},{8,10},{9,11},{10,... | collective-permute-start | bytes 786440 | tf_op jit(solution)/shard_map/ppermute | solution.py:295

commit v6 on v5

--- a/solution.py
+++ b/solution.py
@@ -190,12 +190,11 @@
         out[...] = jnp.concatenate(halves, axis=1).reshape(1, 4, 64, 512)
 
 
-def edges_body(tmb, f0, f1, tma, lo0, hi0, lo1, hi1):
-    for half, (lo, hi) in enumerate(((lo0, hi0), (lo1, hi1))):
-        lanes = pl.ds(half * 256, 256)
-        for i, ref in enumerate((tmb, f0, f1, tma)):
-            lo[i] = ref[0, 0:3, :, lanes]
-            hi[i] = ref[0, 1:4, :, lanes]
+def edges_body(half, tmb, f0, f1, tma, lo, hi):
+    lanes = pl.ds(half * 256, 256)
+    for i, ref in enumerate((tmb, f0, f1, tma)):
+        lo[i] = ref[0, 0:3, :, lanes]
+        hi[i] = ref[0, 1:4, :, lanes]
 
 
 def fold_body(g_tmb, g_tma, r_hb, r_ha, s_tmb, s_tma, acc):
@@ -326,9 +325,14 @@
         back_body, (half, half), idx, (cot, *c_parts, w_out),
         name="back",
     )
-    lo0, hi0, lo1, hi1 = local_call(
-        edges_body, (S(edge, BF16),) * 4, None, (tmb, f0, f1, tma), name="edges"
-    )
+    def edges(n, *around):
+        return local_call(
+            functools.partial(edges_body, n), (S(edge, BF16),) * 2, None, around, name="edges"
+        )
+
+    lo0, hi0 = edges(0, tmb, f0, f1, tma)
+    f0_late, _ = lax.optimization_barrier((f0, lo0))
+    lo1, hi1 = edges(1, tmb, f0_late, f1, tma)
     hb0, ha0 = rows(hi0, 1), rows(lo0, -1)
     hi1, lo1, hb0, ha0 = lax.optimization_barrier((hi1, lo1, hb0, ha0))
     hb1, ha1 = rows(hi1, 1), rows(lo1, -1)

time: 112 us -> 110 us (0.982)
  starting transfers between devices: 42.3 us -> 40.1 us
  Pallas kernels: 22.7 us -> 20.8 us
  waiting for transfers between devices: 42.4 us -> 44.3 us
    ppermute x15, starting transfers between devices: 16.9 us -> 14.7 us  [ring(): lax.ppermute(array, 'tensor', [(i, (i + by) % n_x) for i in range(n_x)])]
    ppermute x6, waiting for transfers between devices: 12.3 us -> 14.4 us  [frames(): return lax.ppermute(array, 'tm', [(i, (i + by) % n_t) for i in range(n_t)])]
    pallas_call x13 -> x14, Pallas kernels: 22.7 us -> 20.8 us  [local_call(): pl.pallas_call(body, out_shape=tuple(outs), in_specs=specs, out_specs=(vm...]
    unnamed x8 -> x12, local copies, waits for them, and re-layouts: 1.42 us -> 2.37 us
  transfers between devices with their start and end apart: 29 -> 29, of which waited for: 14 -> 15; matrix products, arithmetic and copies ran while one was open for 0% -> 0% of each run, Pallas kernels for 18% -> 17%
where the time goes in v6:
time: 110 us
  waiting for transfers between devices  44.3 us (40%)
  starting transfers between devices  40.1 us (36%)
  Pallas kernels  20.8 us (19%)
  local copies, waits for them, and re-layouts  3.35 us (3%)
    ppermute x15, waiting for transfers between devices, ring(): lax.ppermute(array, 'tensor', [(i, (i + by) % n_x) for i in range(n_x)])  23.7 us
    pallas_call x14, Pallas kernels, local_call(): pl.pallas_call(body, out_shape=tuple(outs), in_specs=specs, out_specs=(vm...  20.8 us
    ppermute x15, starting transfers between devices, ring(): lax.ppermute(array, 'tensor', [(i, (i + by) % n_x) for i in range(n_x)])  14.7 us
    ppermute x6, starting transfers between devices, frames(): return lax.ppermute(array, 'tm', [(i, (i + by) % n_t) for i in range(n_t)])  14.6 us
    ppermute x6, waiting for transfers between devices, frames(): return lax.ppermute(array, 'tm', [(i, (i + by) % n_t) for i in range(n_t)])  14.4 us
    ppermute x8, starting transfers between devices, rows(): lax.ppermute(array, 'height', [(i, (i + by) % n_h) for i in range(n_h)])  10.8 us
    ppermute x8, waiting for transfers between devices, rows(): lax.ppermute(array, 'height', [(i, (i + by) % n_h) for i in range(n_h)])  6.2 us
    unnamed x12, local copies, waits for them, and re-layouts  2.37 us
  transfers between devices with their start and end apart: 29, of which 15 were waited for; matrix products, arithmetic and copies ran while one was open for 0% of the time, Pallas kernels for 17%

profile of v6, /device:TPU:22, one launch (start us, length us, event | category | flops | bytes accessed | tf_op | source)
XLA Modules:
  0.0 109.6 jit_solution(13325656096574023353)
XLA Ops:
  0.6 1.0 fusion
  1.6 0.6 collective-permute-start
  2.2 1.5 %collective-permute-start.4 = (bf16[256,256]{1,0:T(8,128)(2,1)S(1)}, bf16[256,256]{1,0:T(8,128)(2,1)S(1)}, u32[]{:S(2)}, u32[]{:S(2)}) collective-permute-start(bf16[256,256]{1,0:T(8,128)(2,1)S(1)} %bitcast.10), channel_id=1, source_target_pairs={{0,3},{1,0},{2,1},{3,2},{4,7},{5,4},{6,5},{7,6},{8,11},{9,8},{10,9... | collective-permute-start | bytes 393224 | tf_op jit(solution)/shard_map/ppermute | solution.py:294
  3.7 0.8 collective-permute-start.1
  4.6 2.4 %collective-permute-start.3 = (bf16[256,256]{1,0:T(8,128)(2,1)S(1)}, bf16[256,256]{1,0:T(8,128)(2,1)S(1)}, u32[]{:S(2)}, u32[]{:S(2)}) collective-permute-start(bf16[256,256]{1,0:T(8,128)(2,1)S(1)} %bitcast.11), channel_id=1, source_target_pairs={{0,1},{1,2},{2,3},{3,0},{4,5},{5,6},{6,7},{7,4},{8,9},{9,10},{10,1... | collective-permute-start | bytes 393224 | tf_op jit(solution)/shard_map/ppermute | solution.py:294
  7.0 0.8 collective-permute-done.a1
  7.7 0.9 collective-permute-start.2
  8.6 1.1 %collective-permute-done.4.b2 = bf16[256,256]{1,0:T(8,128)(2,1)S(1)} collective-permute-done((bf16[256,256]{1,0:T(8,128)(2,1)S(1)}, bf16[256,256]{1,0:T(8,128)(2,1)S(1)}, u32[]{:S(2)}, u32[]{:S(2)}) %collective-permute-start.4) | collective-permute-done | bytes 131104 | tf_op jit(solution)/shard_map/ppermute | solution.py:294
  9.7 0.3 collective-permute-start.5
  10.1 1.4 %copy-done = bf16[1024,3,256]{2,0,1:T(8,128)(2,1)S(1)} copy-done((bf16[1024,3,256]{2,0,1:T(8,128)(2,1)S(1)}, bf16[1024,3,256]{2,0,1:T(8,128)(2,1)}, u32[]{:S(2)}) %copy-start) | copy-done | bytes 1572888
  11.5 0.1 stage.1.w
  11.6 0.1 add_add_fusion.1.idx
  11.7 0.0 collective-permute-done.1.a2
  11.7 1.0 collective-permute-done.2.a3
  12.7 3.2 %collective-permute-done.5.b3 = bf16[256,256]{1,0:T(8,128)(2,1)S(1)} collective-permute-done((bf16[256,256]{1,0:T(8,128)(2,1)S(1)}, bf16[256,256]{1,0:T(8,128)(2,1)S(1)}, u32[]{:S(2)}, u32[]{:S(2)}) %collective-permute-start.5) | collective-permute-done | bytes 131104 | tf_op jit(solution)/shard_map/ppermute | solution.py:294
  15.9 1.3 %project.1 = (bf16[1,4,64,512]{3,2,1,0:T(8,128)(2,1)S(1)}, bf16[1,4,64,512]{3,2,1,0:T(8,128)(2,1)S(1)}) custom-call(s32[4]{0:T(128)S(1)} %add_add_fusion.1.idx, bf16[256,256]{1,0:T(8,128)(2,1)S(1)} %bitcast.16, bf16[256,256]{1,0:T(8,128)(2,1)S(1)} %collective-permute-done.a1, bf16[256,256]{1,0:T(8,128)(2,1)S(1)} %collective-permute-done.1.a2, ...), custom_call_target="tpu_custom_call" | custom-call | tf_op jit(solution)/shard_map/project/pallas_call | solution.py:269
  17.2 3.3 %collective-permute-start.6 = (bf16[1,4,64,512]{3,2,1,0:T(8,128)(2,1)S(1)}, bf16[1,4,64,512]{3,2,1,0:T(8,128)(2,1)S(1)}, u32[]{:S(2)}, u32[]{:S(2)}) collective-permute-start(bf16[1,4,64,512]{3,2,1,0:T(8,128)(2,1)S(1)} %get-tuple-element.55.f1), channel_id=1, source_target_pairs={{0,64},{64,128},{128,192},{192,0},{1,65},{65,129},{129,193},{193,1... | collective-permute-start | bytes 786440 | tf_op jit(solution)/shard_map/ppermute | solution.py:297
  20.5 3.1 %collective-permute-start.7 = (bf16[1,4,64,512]{3,2,1,0:T(8,128)(2,1)S(1)}, bf16[1,4,64,512]{3,2,1,0:T(8,128)(2,1)S(1)}, u32[]{:S(2)}, u32[]{:S(2)}) collective-permute-start(bf16[1,4,64,512]{3,2,1,0:T(8,128)(2,1)S(1)} %get-tuple-element.65.f0), channel_id=1, source_target_pairs={{0,192},{64,0},{128,64},{192,128},{1,193},{65,1},{129,65},{193,129... | collective-permute-start | bytes 786440 | tf_op jit(solution)/shard_map/ppermute | solution.py:297
  23.7 2.0 %collective-permute-start.9 = (bf16[512,256]{1,0:T(8,128)(2,1)}, bf16[512,256]{1,0:T(8,128)(2,1)}, u32[]{:S(2)}, u32[]{:S(2)}) collective-permute-start(bf16[512,256]{1,0:T(8,128)(2,1)} %bitcast.19), channel_id=1, source_target_pairs={{0,3},{1,0},{2,1},{3,2},{4,7},{5,4},{6,5},{7,6},{8,11},{9,8},{10,9... | collective-permute-start | bytes 786440 | tf_op jit(solution)/shard_map/ppermute | solution.py:294
  25.7 6.9 %collective-permute-done.6.tmb = bf16[1,4,64,512]{3,2,1,0:T(8,128)(2,1)S(1)} collective-permute-done((bf16[1,4,64,512]{3,2,1,0:T(8,128)(2,1)S(1)}, bf16[1,4,64,512]{3,2,1,0:T(8,128)(2,1)S(1)}, u32[]{:S(2)}, u32[]{:S(2)}) %collective-permute-start.6) | collective-permute-done | bytes 262176 | tf_op jit(solution)/shard_map/ppermute | solution.py:297
  32.6 0.6 collective-permute-done.7.tma
  33.3 3.2 %collective-permute-done.9.x2 = bf16[512,256]{1,0:T(8,128)(2,1)} collective-permute-done((bf16[512,256]{1,0:T(8,128)(2,1)}, bf16[512,256]{1,0:T(8,128)(2,1)}, u32[]{:S(2)}, u32[]{:S(2)}) %collective-permute-start.9) | collective-permute-done | bytes 262176 | tf_op jit(solution)/shard_map/ppermute | solution.py:294
  36.5 0.1 edges.2
  36.6 0.1 collective-permute-start.11
  36.7 2.6 %collective-permute-start.12 = (bf16[4,3,64,256]{3,2,1,0:T(8,128)(2,1)S(1)}, bf16[4,3,64,256]{3,2,1,0:T(8,128)(2,1)S(1)}, u32[]{:S(2)}, u32[]{:S(2)}) collective-permute-start(bf16[4,3,64,256]{3,2,1,0:T(8,128)(2,1)S(1)} %get-tuple-element.64), channel_id=1, source_target_pairs={{0,60},{4,0},{8,4},{12,8},{16,12},{20,16},{24,20},{28,24},{32,28},... | collective-permute-start | bytes 1179656 | tf_op jit(solution)/shard_map/ppermute | solution.py:300
  39.3 0.1 and_convert_fusion.valid
  39.4 0.9 copy-done.4
  40.3 1.0 query.1
  41.3 0.1 edges.3
  41.4 0.0 copy-done.5
  41.4 1.6 %back.1 = (bf16[512,128]{1,0:T(8,128)(2,1)S(1)}, bf16[512,128]{1,0:T(8,128)(2,1)S(1)}) custom-call(s32[4]{0:T(128)S(1)} %add_add_fusion.1.idx, bf16[512,256]{1,0:T(8,128)(2,1)S(1)} %bitcast.21, bf16[512,256]{1,0:T(8,128)(2,1)} %collective-permute-done.8.x1, bf16[512,256]{1,0:T(8,128)(2,1)} %collective-permute-done.9.x2, ...), custom_call_target="tpu_custom_call" | custom-call | tf_op jit(solution)/shard_map/back/pallas_call | solution.py:269
  43.0 5.7 %collective-permute-done.11.hb = bf16[4,3,64,256]{3,2,1,0:T(8,128)(2,1)S(1)} collective-permute-done((bf16[4,3,64,256]{3,2,1,0:T(8,128)(2,1)S(1)}, bf16[4,3,64,256]{3,2,1,0:T(8,128)(2,1)S(1)}, u32[]{:S(2)}, u32[]{:S(2)}) %collective-permute-start.11) | collective-permute-done | bytes 393248 | tf_op jit(solution)/shard_map/ppermute | solution.py:300
  48.7 0.1 collective-permute-start.15
  48.8 2.5 %collective-permute-start.16 = (bf16[4,3,64,256]{3,2,1,0:T(8,128)(2,1)S(1)}, bf16[4,3,64,256]{3,2,1,0:T(8,128)(2,1)S(1)}, u32[]{:S(2)}, u32[]{:S(2)}) collective-permute-start(bf16[4,3,64,256]{3,2,1,0:T(8,128)(2,1)S(1)} %get-tuple-element.81), channel_id=1, source_target_pairs={{0,60},{4,0},{8,4},{12,8},{16,12},{20,16},{24,20},{28,24},{32,28},... | collective-permute-start | bytes 1179656 | tf_op jit(solution)/shard_map/ppermute | solution.py:300
  51.3 6.2 %attend.2 = (bf16[512,128]{1,0:T(8,128)(2,1)S(1)}, bf16[512,128]{1,0:T(8,128)(2,1)S(1)}, f32[2,4,64,256]{3,2,1,0:T(8,128)S(1)}, f32[1,4,64,256]{3,2,1,0:T(8,128)...) custom-call(s32[4,10]{1,0:T(4,128)S(1)} %and_convert_fusion.valid, ...), custom_call_target="tpu_custom_call" | custom-call | flops 9663676416 | tf_op jit(solution)/shard_map/attend/pallas_call | solution.py:269
  57.5 0.1 collective-permute-start.13
  57.6 2.6 %collective-permute-start.14 = (bf16[4,3,64,256]{3,2,1,0:T(8,128)(2,1)S(1)}, bf16[4,3,64,256]{3,2,1,0:T(8,128)(2,1)S(1)}, u32[]{:S(2)}, u32[]{:S(2)}) collective-permute-start(bf16[4,3,64,256]{3,2,1,0:T(8,128)(2,1)S(1)} %get-tuple-element.75), channel_id=1, source_target_pairs={{0,60},{4,0},{8,4},{12,8},{16,12},{20,16},{24,20},{28,24},{32,28},... | collective-permute-start | bytes 1179656 | tf_op jit(solution)/shard_map/ppermute | solution.py:300
  60.2 0.5 collective-permute-done.15.hb
  60.7 6.2 %attend.3 = (bf16[512,128]{1,0:T(8,128)(2,1)S(1)}, bf16[512,128]{1,0:T(8,128)(2,1)S(1)}, f32[2,4,64,256]{3,2,1,0:T(8,128)S(1)}, f32[1,4,64,256]{3,2,1,0:T(8,128)...) custom-call(s32[4,10]{1,0:T(4,128)S(1)} %and_convert_fusion.valid, ...), custom_call_target="tpu_custom_call" | custom-call | flops 9663676416 | tf_op jit(solution)/shard_map/attend/pallas_call | solution.py:269
  66.9 0.1 collective-permute-start.17
  67.0 2.6 %collective-permute-start.18 = (bf16[4,3,64,256]{3,2,1,0:T(8,128)(2,1)S(1)}, bf16[4,3,64,256]{3,2,1,0:T(8,128)(2,1)S(1)}, u32[]{:S(2)}, u32[]{:S(2)}) collective-permute-start(bf16[4,3,64,256]{3,2,1,0:T(8,128)(2,1)S(1)} %get-tuple-element.85), channel_id=1, source_target_pairs={{0,60},{4,0},{8,4},{12,8},{16,12},{20,16},{24,20},{28,24},{32,28},... | collective-permute-start | bytes 1179656 | tf_op jit(solution)/shard_map/ppermute | solution.py:300
  69.6 0.1 add_add_fusion.idx
  69.7 0.1 fold.2
  69.8 1.0 mix.1
  70.8 0.5 collective-permute-start.19
  71.3 1.6 %collective-permute-start.20 = (bf16[512,256]{1,0:T(8,128)(2,1)S(1)}, bf16[512,256]{1,0:T(8,128)(2,1)S(1)}, u32[]{:S(2)}, u32[]{:S(2)}) collective-permute-start(bf16[512,256]{1,0:T(8,128)(2,1)S(1)} %get-tuple-element.87), channel_id=1, source_target_pairs={{0,3},{1,0},{2,1},{3,2},{4,7},{5,4},{6,5},{7,6},{8,11},{9,8},{10,9... | collective-permute-start | bytes 786440 | tf_op jit(solution)/shard_map/ppermute | solution.py:294
  72.9 1.4 %collective-permute-start.22 = (bf16[1,4,64,256]{3,2,1,0:T(8,128)(2,1)S(1)}, bf16[1,4,64,256]{3,2,1,0:T(8,128)(2,1)S(1)}, u32[]{:S(2)}, u32[]{:S(2)}) collective-permute-start(bf16[1,4,64,256]{3,2,1,0:T(8,128)(2,1)S(1)} %get-tuple-element.76), channel_id=1, source_target_pairs={{0,64},{64,128},{128,192},{192,0},{1,65},{65,129},{129,193},{193,1... | collective-permute-start | bytes 393224 | tf_op jit(solution)/shard_map/ppermute | solution.py:297
  74.3 3.3 %collective-permute-done.19.b = bf16[512,256]{1,0:T(8,128)(2,1)S(1)} collective-permute-done((bf16[512,256]{1,0:T(8,128)(2,1)S(1)}, bf16[512,256]{1,0:T(8,128)(2,1)S(1)}, u32[]{:S(2)}, u32[]{:S(2)}) %collective-permute-start.19) | collective-permute-done | bytes 262176 | tf_op jit(solution)/shard_map/ppermute | solution.py:294
  77.5 2.6 %collective-permute-start.23 = (bf16[1,4,64,256]{3,2,1,0:T(8,128)(2,1)S(1)}, bf16[1,4,64,256]{3,2,1,0:T(8,128)(2,1)S(1)}, u32[]{:S(2)}, u32[]{:S(2)}) collective-permute-start(bf16[1,4,64,256]{3,2,1,0:T(8,128)(2,1)S(1)} %get-tuple-element.93), channel_id=1, source_target_pairs={{0,192},{64,0},{128,64},{192,128},{1,193},{65,1},{129,65},{193,129... | collective-permute-start | bytes 393224 | tf_op jit(solution)/shard_map/ppermute | solution.py:297
  80.1 0.1 fold.3
  80.2 0.7 collective-permute-start.24
  80.9 3.5 %collective-permute-start.25 = (bf16[1,4,64,256]{3,2,1,0:T(8,128)(2,1)S(1)}, bf16[1,4,64,256]{3,2,1,0:T(8,128)(2,1)S(1)}, u32[]{:S(2)}, u32[]{:S(2)}) collective-permute-start(bf16[1,4,64,256]{3,2,1,0:T(8,128)(2,1)S(1)} %get-tuple-element.101), channel_id=1, source_target_pairs={{0,192},{64,0},{128,64},{192,128},{1,193},{65,1},{129,65},{193,129... | collective-permute-start | bytes 393224 | tf_op jit(solution)/shard_map/ppermute | solution.py:297
  84.4 0.7 collective-permute-start.21
  85.1 0.3 collective-permute-done.22.tb0
  85.4 3.4 %collective-permute-done.23.ta0 = bf16[1,4,64,256]{3,2,1,0:T(8,128)(2,1)S(1)} collective-permute-done((bf16[1,4,64,256]{3,2,1,0:T(8,128)(2,1)S(1)}, bf16[1,4,64,256]{3,2,1,0:T(8,128)(2,1)S(1)}, u32[]{:S(2)}, u32[]{:S(2)}) %collective-permute-start.23) | collective-permute-done | bytes 131104 | tf_op jit(solution)/shard_map/ppermute | solution.py:297
  88.8 3.1 %collective-permute-done.25.ta1 = bf16[1,4,64,256]{3,2,1,0:T(8,128)(2,1)S(1)} collective-permute-done((bf16[1,4,64,256]{3,2,1,0:T(8,128)(2,1)S(1)}, bf16[1,4,64,256]{3,2,1,0:T(8,128)(2,1)S(1)}, u32[]{:S(2)}, u32[]{:S(2)}) %collective-permute-start.25) | collective-permute-done | bytes 131104 | tf_op jit(solution)/shard_map/ppermute | solution.py:297
  91.9 1.6 %in_grad.1 = (f32[512,256]{1,0:T(8,128)S(1)}, bf16[512,256]{1,0:T(8,128)(2,1)S(1)}, bf16[512,256]{1,0:T(8,128)(2,1)S(1)}, bf16[512,256]{1,0:T(8,128)(2,1)S(1)}) custom-call(s32[4]{0:T(128)S(1)} %add_add_fusion.idx, bf16[512,128]{1,0:T(8,128)(2,1)S(1)} %get-tuple-element.91.dq0, f32[2,4,64,256]{3,2,1,0:T(8,128)S(1)} %get-tuple-element.92.own0, ...), custom_call_target="tpu_custom_call" | custom-call | tf_op jit(solution)/shard_map/in_grad/pallas_call | solution.py:269
  93.6 1.7 %collective-permute-start.26 = (bf16[512,256]{1,0:T(8,128)(2,1)S(1)}, bf16[512,256]{1,0:T(8,128)(2,1)S(1)}, u32[]{:S(2)}, u32[]{:S(2)}) collective-permute-start(bf16[512,256]{1,0:T(8,128)(2,1)S(1)} %get-tuple-element.103), channel_id=1, source_target_pairs={{0,1},{1,2},{2,3},{3,0},{4,5},{5,6},{6,7},{7,4},{8,9},{9,10},{10,1... | collective-permute-start | bytes 786440 | tf_op jit(solution)/shard_map/ppermute | solution.py:294
  95.3 0.4 collective-permute-start.27
  95.7 1.2 %collective-permute-start.28 = (bf16[512,256]{1,0:T(8,128)(2,1)S(1)}, bf16[512,256]{1,0:T(8,128)(2,1)S(1)}, u32[]{:S(2)}, u32[]{:S(2)}) collective-permute-start(bf16[512,256]{1,0:T(8,128)(2,1)S(1)} %get-tuple-element.105), channel_id=1, source_target_pairs={{0,2},{1,3},{2,0},{3,1},{4,6},{5,7},{6,4},{7,5},{8,10},{9,11},{10,... | collective-permute-start | bytes 786440 | tf_op jit(solution)/shard_map/ppermute | solution.py:294
  96.8 0.8 mixed_sum.1
  97.7 7.8 %collective-permute-done.26.b = bf16[512,256]{1,0:T(8,128)(2,1)S(1)} collective-permute-done((bf16[512,256]{1,0:T(8,128)(2,1)S(1)}, bf16[512,256]{1,0:T(8,128)(2,1)S(1)}, u32[]{:S(2)}, u32[]{:S(2)}) %collective-permute-start.26) | collective-permute-done | bytes 262176 | tf_op jit(solution)/shard_map/ppermute | solution.py:294
  105.4 3.4 %collective-permute-done.27.c = bf16[512,256]{1,0:T(8,128)(2,1)S(1)} collective-permute-done((bf16[512,256]{1,0:T(8,128)(2,1)S(1)}, bf16[512,256]{1,0:T(8,128)(2,1)S(1)}, u32[]{:S(2)}, u32[]{:S(2)}) %collective-permute-start.27) | collective-permute-done | bytes 262176 | tf_op jit(solution)/shard_map/ppermute | solution.py:294
  108.8 0.8 in_grad_sum.1
  (26 shorter events, 0.1 us)
Async XLA Ops:
  1.6 6.1 %collective-permute-start = (bf16[256,256]{1,0:T(8,128)(2,1)S(1)}, bf16[256,256]{1,0:T(8,128)(2,1)S(1)}, u32[]{:S(2)}, u32[]{:S(2)}) collective-permute-start(bf16[256,256]{1,0:T(8,128)(2,1)S(1)} %bitcast.14), channel_id=1, source_target_pairs={{0,1},{1,2},{2,3},{3,0},{4,5},{5,6},{6,7},{7,4},{8,9},{9,10},{10,1... | collective-permute-start | bytes 393224 | tf_op jit(solution)/shard_map/ppermute | solution.py:294
  2.2 7.6 %collective-permute-start.4 = (bf16[256,256]{1,0:T(8,128)(2,1)S(1)}, bf16[256,256]{1,0:T(8,128)(2,1)S(1)}, u32[]{:S(2)}, u32[]{:S(2)}) collective-permute-start(bf16[256,256]{1,0:T(8,128)(2,1)S(1)} %bitcast.10), channel_id=1, source_target_pairs={{0,3},{1,0},{2,1},{3,2},{4,7},{5,4},{6,5},{7,6},{8,11},{9,8},{10,9... | collective-permute-start | bytes 393224 | tf_op jit(solution)/shard_map/ppermute | solution.py:294
  3.7 8.0 %collective-permute-start.1 = (bf16[256,256]{1,0:T(8,128)(2,1)S(1)}, bf16[256,256]{1,0:T(8,128)(2,1)S(1)}, u32[]{:S(2)}, u32[]{:S(2)}) collective-permute-start(bf16[256,256]{1,0:T(8,128)(2,1)S(1)} %bitcast.15), channel_id=1, source_target_pairs={{0,3},{1,0},{2,1},{3,2},{4,7},{5,4},{6,5},{7,6},{8,11},{9,8},{10,9... | collective-permute-start | bytes 393224 | tf_op jit(solution)/shard_map/ppermute | solution.py:294
  4.6 7.2 %collective-permute-start.3 = (bf16[256,256]{1,0:T(8,128)(2,1)S(1)}, bf16[256,256]{1,0:T(8,128)(2,1)S(1)}, u32[]{:S(2)}, u32[]{:S(2)}) collective-permute-start(bf16[256,256]{1,0:T(8,128)(2,1)S(1)} %bitcast.11), channel_id=1, source_target_pairs={{0,1},{1,2},{2,3},{3,0},{4,5},{5,6},{6,7},{7,4},{8,9},{9,10},{10,1... | collective-permute-start | bytes 393224 | tf_op jit(solution)/shard_map/ppermute | solution.py:294
  7.7 5.0 %collective-permute-start.2 = (bf16[256,256]{1,0:T(8,128)(2,1)S(1)}, bf16[256,256]{1,0:T(8,128)(2,1)S(1)}, u32[]{:S(2)}, u32[]{:S(2)}) collective-permute-start(bf16[256,256]{1,0:T(8,128)(2,1)S(1)} %collective-permute-done.a1), channel_id=1, source_target_pairs={{0,1},{1,2},{2,3},{3,0},{4,5},{5,6},{6,7},{7,4},{8,9},{9,10},{10,1... | collective-permute-start | bytes 393224 | tf_op jit(solution)/shard_map/ppermute | solution.py:294
  9.7 6.2 %collective-permute-start.5 = (bf16[256,256]{1,0:T(8,128)(2,1)S(1)}, bf16[256,256]{1,0:T(8,128)(2,1)S(1)}, u32[]{:S(2)}, u32[]{:S(2)}) collective-permute-start(bf16[256,256]{1,0:T(8,128)(2,1)S(1)} %collective-permute-done.4.b2), channel_id=1, source_target_pairs={{0,3},{1,0},{2,1},{3,2},{4,7},{5,4},{6,5},{7,6},{8,11},{9,8},{10,9... | collective-permute-start | bytes 393224 | tf_op jit(solution)/shard_map/ppermute | solution.py:294
  10.1 1.4 %copy-start = (bf16[1024,3,256]{2,0,1:T(8,128)(2,1)S(1)}, bf16[1024,3,256]{2,0,1:T(8,128)(2,1)}, u32[]{:S(2)}) copy-start(bf16[1024,3,256]{2,0,1:T(8,128)(2,1)} %param.6) | copy-start | bytes 4718596
  15.9 1.3 %copy-start.3 = (bf16[256,256]{1,0:T(8,128)(2,1)}, bf16[256,256]{1,0:T(8,128)(2,1)S(1)}, u32[]{:S(2)}) copy-start(bf16[256,256]{1,0:T(8,128)(2,1)S(1)} %collective-permute-done.5.b3) | copy-start | bytes 393220
  17.2 15.4 %collective-permute-start.6 = (bf16[1,4,64,512]{3,2,1,0:T(8,128)(2,1)S(1)}, bf16[1,4,64,512]{3,2,1,0:T(8,128)(2,1)S(1)}, u32[]{:S(2)}, u32[]{:S(2)}) collective-permute-start(bf16[1,4,64,512]{3,2,1,0:T(8,128)(2,1)S(1)} %get-tuple-element.55.f1), channel_id=1, source_target_pairs={{0,64},{64,128},{128,192},{192,0},{1,65},{65,129},{129,193},{193,1... | collective-permute-start | bytes 786440 | tf_op jit(solution)/shard_map/ppermute | solution.py:297
  20.5 12.7 %collective-permute-start.7 = (bf16[1,4,64,512]{3,2,1,0:T(8,128)(2,1)S(1)}, bf16[1,4,64,512]{3,2,1,0:T(8,128)(2,1)S(1)}, u32[]{:S(2)}, u32[]{:S(2)}) collective-permute-start(bf16[1,4,64,512]{3,2,1,0:T(8,128)(2,1)S(1)} %get-tuple-element.65.f0), channel_id=1, source_target_pairs={{0,192},{64,0},{128,64},{192,128},{1,193},{65,1},{129,65},{193,129... | collective-permute-start | bytes 786440 | tf_op jit(solution)/shard_map/ppermute | solution.py:297
  23.7 9.6 %collective-permute-start.8 = (bf16[512,256]{1,0:T(8,128)(2,1)}, bf16[512,256]{1,0:T(8,128)(2,1)}, u32[]{:S(2)}, u32[]{:S(2)}) collective-permute-start(bf16[512,256]{1,0:T(8,128)(2,1)} %bitcast.18), channel_id=1, source_target_pairs={{0,1},{1,2},{2,3},{3,0},{4,5},{5,6},{6,7},{7,4},{8,9},{9,10},{10,1... | collective-permute-start | bytes 786440 | tf_op jit(solution)/shard_map/ppermute | solution.py:294
  23.7 12.8 %collective-permute-start.9 = (bf16[512,256]{1,0:T(8,128)(2,1)}, bf16[512,256]{1,0:T(8,128)(2,1)}, u32[]{:S(2)}, u32[]{:S(2)}) collective-permute-start(bf16[512,256]{1,0:T(8,128)(2,1)} %bitcast.19), channel_id=1, source_target_pairs={{0,3},{1,0},{2,1},{3,2},{4,7},{5,4},{6,5},{7,6},{8,11},{9,8},{10,9... | collective-permute-start | bytes 786440 | tf_op jit(solution)/shard_map/ppermute | solution.py:294
  25.7 10.8 %collective-permute-start.10 = (bf16[512,256]{1,0:T(8,128)(2,1)}, bf16[512,256]{1,0:T(8,128)(2,1)}, u32[]{:S(2)}, u32[]{:S(2)}) collective-permute-start(bf16[512,256]{1,0:T(8,128)(2,1)} %bitcast.20), channel_id=1, source_target_pairs={{0,2},{1,3},{2,0},{3,1},{4,6},{5,7},{6,4},{7,5},{8,10},{9,11},{10,... | collective-permute-start | bytes 786440 | tf_op jit(solution)/shard_map/ppermute | solution.py:294
  36.6 12.1 %collective-permute-start.11 = (bf16[4,3,64,256]{3,2,1,0:T(8,128)(2,1)S(1)}, bf16[4,3,64,256]{3,2,1,0:T(8,128)(2,1)S(1)}, u32[]{:S(2)}, u32[]{:S(2)}) collective-permute-start(bf16[4,3,64,256]{3,2,1,0:T(8,128)(2,1)S(1)} %get-tuple-element.68), channel_id=1, source_target_pairs={{0,4},{4,8},{8,12},{12,16},{16,20},{20,24},{24,28},{28,32},{32,36}... | collective-permute-start | bytes 1179656 | tf_op jit(solution)/shard_map/ppermute | solution.py:300
  36.7 12.0 %collective-permute-start.12 = (bf16[4,3,64,256]{3,2,1,0:T(8,128)(2,1)S(1)}, bf16[4,3,64,256]{3,2,1,0:T(8,128)(2,1)S(1)}, u32[]{:S(2)}, u32[]{:S(2)}) collective-permute-start(bf16[4,3,64,256]{3,2,1,0:T(8,128)(2,1)S(1)} %get-tuple-element.64), channel_id=1, source_target_pairs={{0,60},{4,0},{8,4},{12,8},{16,12},{20,16},{24,20},{28,24},{32,28},... | collective-permute-start | bytes 1179656 | tf_op jit(solution)/shard_map/ppermute | solution.py:300
  39.4 0.9 copy-start.4
  40.3 1.1 copy-start.2
  40.3 1.1 %copy-start.5 = (bf16[2,4,64,256]{3,2,1,0:T(8,128)(2,1)S(1)}, bf16[2,4,64,256]{3,2,1,0:T(8,128)(2,1)}, u32[]{:S(2)}) copy-start(bf16[2,4,64,256]{3,2,1,0:T(8,128)(2,1)} %param.5) | copy-start | bytes 786436
  48.7 12.1 %collective-permute-start.15 = (bf16[4,3,64,256]{3,2,1,0:T(8,128)(2,1)S(1)}, bf16[4,3,64,256]{3,2,1,0:T(8,128)(2,1)S(1)}, u32[]{:S(2)}, u32[]{:S(2)}) collective-permute-start(bf16[4,3,64,256]{3,2,1,0:T(8,128)(2,1)S(1)} %get-tuple-element.80), channel_id=1, source_target_pairs={{0,4},{4,8},{8,12},{12,16},{16,20},{20,24},{24,28},{28,32},{32,36}... | collective-permute-start | bytes 1179656 | tf_op jit(solution)/shard_map/ppermute | solution.py:300
  48.8 12.0 %collective-permute-start.16 = (bf16[4,3,64,256]{3,2,1,0:T(8,128)(2,1)S(1)}, bf16[4,3,64,256]{3,2,1,0:T(8,128)(2,1)S(1)}, u32[]{:S(2)}, u32[]{:S(2)}) collective-permute-start(bf16[4,3,64,256]{3,2,1,0:T(8,128)(2,1)S(1)} %get-tuple-element.81), channel_id=1, source_target_pairs={{0,60},{4,0},{8,4},{12,8},{16,12},{20,16},{24,20},{28,24},{32,28},... | collective-permute-start | bytes 1179656 | tf_op jit(solution)/shard_map/ppermute | solution.py:300
  57.5 12.2 %collective-permute-start.13 = (bf16[4,3,64,256]{3,2,1,0:T(8,128)(2,1)S(1)}, bf16[4,3,64,256]{3,2,1,0:T(8,128)(2,1)S(1)}, u32[]{:S(2)}, u32[]{:S(2)}) collective-permute-start(bf16[4,3,64,256]{3,2,1,0:T(8,128)(2,1)S(1)} %get-tuple-element.74), channel_id=1, source_target_pairs={{0,4},{4,8},{8,12},{12,16},{16,20},{20,24},{24,28},{28,32},{32,36}... | collective-permute-start | bytes 1179656 | tf_op jit(solution)/shard_map/ppermute | solution.py:300
  57.6 12.1 %collective-permute-start.14 = (bf16[4,3,64,256]{3,2,1,0:T(8,128)(2,1)S(1)}, bf16[4,3,64,256]{3,2,1,0:T(8,128)(2,1)S(1)}, u32[]{:S(2)}, u32[]{:S(2)}) collective-permute-start(bf16[4,3,64,256]{3,2,1,0:T(8,128)(2,1)S(1)} %get-tuple-element.75), channel_id=1, source_target_pairs={{0,60},{4,0},{8,4},{12,8},{16,12},{20,16},{24,20},{28,24},{32,28},... | collective-permute-start | bytes 1179656 | tf_op jit(solution)/shard_map/ppermute | solution.py:300
  66.9 13.2 %collective-permute-start.17 = (bf16[4,3,64,256]{3,2,1,0:T(8,128)(2,1)S(1)}, bf16[4,3,64,256]{3,2,1,0:T(8,128)(2,1)S(1)}, u32[]{:S(2)}, u32[]{:S(2)}) collective-permute-start(bf16[4,3,64,256]{3,2,1,0:T(8,128)(2,1)S(1)} %get-tuple-element.84), channel_id=1, source_target_pairs={{0,4},{4,8},{8,12},{12,16},{16,20},{20,24},{24,28},{28,32},{32,36}... | collective-permute-start | bytes 1179656 | tf_op jit(solution)/shard_map/ppermute | solution.py:300
  67.0 13.1 %collective-permute-start.18 = (bf16[4,3,64,256]{3,2,1,0:T(8,128)(2,1)S(1)}, bf16[4,3,64,256]{3,2,1,0:T(8,128)(2,1)S(1)}, u32[]{:S(2)}, u32[]{:S(2)}) collective-permute-start(bf16[4,3,64,256]{3,2,1,0:T(8,128)(2,1)S(1)} %get-tuple-element.85), channel_id=1, source_target_pairs={{0,60},{4,0},{8,4},{12,8},{16,12},{20,16},{24,20},{28,24},{32,28},... | collective-permute-start | bytes 1179656 | tf_op jit(solution)/shard_map/ppermute | solution.py:300
  69.7 22.2 %copy-start.1 = (bf16[1024,3,256]{2,0,1:T(8,128)(2,1)S(1)}, bf16[1024,3,256]{2,0,1:T(8,128)(2,1)}, u32[]{:S(2)}) copy-start(bf16[1024,3,256]{2,0,1:T(8,128)(2,1)} %param.6) | copy-start | bytes 4718596
  70.8 6.7 %collective-permute-start.19 = (bf16[512,256]{1,0:T(8,128)(2,1)S(1)}, bf16[512,256]{1,0:T(8,128)(2,1)S(1)}, u32[]{:S(2)}, u32[]{:S(2)}) collective-permute-start(bf16[512,256]{1,0:T(8,128)(2,1)S(1)} %get-tuple-element.86), channel_id=1, source_target_pairs={{0,1},{1,2},{2,3},{3,0},{4,5},{5,6},{6,7},{7,4},{8,9},{9,10},{10,1... | collective-permute-start | bytes 786440 | tf_op jit(solution)/shard_map/ppermute | solution.py:294
  71.3 8.8 %collective-permute-start.20 = (bf16[512,256]{1,0:T(8,128)(2,1)S(1)}, bf16[512,256]{1,0:T(8,128)(2,1)S(1)}, u32[]{:S(2)}, u32[]{:S(2)}) collective-permute-start(bf16[512,256]{1,0:T(8,128)(2,1)S(1)} %get-tuple-element.87), channel_id=1, source_target_pairs={{0,3},{1,0},{2,1},{3,2},{4,7},{5,4},{6,5},{7,6},{8,11},{9,8},{10,9... | collective-permute-start | bytes 786440 | tf_op jit(solution)/shard_map/ppermute | solution.py:294
  72.9 12.5 %collective-permute-start.22 = (bf16[1,4,64,256]{3,2,1,0:T(8,128)(2,1)S(1)}, bf16[1,4,64,256]{3,2,1,0:T(8,128)(2,1)S(1)}, u32[]{:S(2)}, u32[]{:S(2)}) collective-permute-start(bf16[1,4,64,256]{3,2,1,0:T(8,128)(2,1)S(1)} %get-tuple-element.76), channel_id=1, source_target_pairs={{0,64},{64,128},{128,192},{192,0},{1,65},{65,129},{129,193},{193,1... | collective-permute-start | bytes 393224 | tf_op jit(solution)/shard_map/ppermute | solution.py:297
  77.5 11.3 %collective-permute-start.23 = (bf16[1,4,64,256]{3,2,1,0:T(8,128)(2,1)S(1)}, bf16[1,4,64,256]{3,2,1,0:T(8,128)(2,1)S(1)}, u32[]{:S(2)}, u32[]{:S(2)}) collective-permute-start(bf16[1,4,64,256]{3,2,1,0:T(8,128)(2,1)S(1)} %get-tuple-element.93), channel_id=1, source_target_pairs={{0,192},{64,0},{128,64},{192,128},{1,193},{65,1},{129,65},{193,129... | collective-permute-start | bytes 393224 | tf_op jit(solution)/shard_map/ppermute | solution.py:297
  80.2 8.7 %collective-permute-start.24 = (bf16[1,4,64,256]{3,2,1,0:T(8,128)(2,1)S(1)}, bf16[1,4,64,256]{3,2,1,0:T(8,128)(2,1)S(1)}, u32[]{:S(2)}, u32[]{:S(2)}) collective-permute-start(bf16[1,4,64,256]{3,2,1,0:T(8,128)(2,1)S(1)} %get-tuple-element.100), channel_id=1, source_target_pairs={{0,64},{64,128},{128,192},{192,0},{1,65},{65,129},{129,193},{193,1... | collective-permute-start | bytes 393224 | tf_op jit(solution)/shard_map/ppermute | solution.py:297
  80.9 11.0 %collective-permute-start.25 = (bf16[1,4,64,256]{3,2,1,0:T(8,128)(2,1)S(1)}, bf16[1,4,64,256]{3,2,1,0:T(8,128)(2,1)S(1)}, u32[]{:S(2)}, u32[]{:S(2)}) collective-permute-start(bf16[1,4,64,256]{3,2,1,0:T(8,128)(2,1)S(1)} %get-tuple-element.101), channel_id=1, source_target_pairs={{0,192},{64,0},{128,64},{192,128},{1,193},{65,1},{129,65},{193,129... | collective-permute-start | bytes 393224 | tf_op jit(solution)/shard_map/ppermute | solution.py:297
  84.4 12.4 %collective-permute-start.21 = (bf16[512,256]{1,0:T(8,128)(2,1)S(1)}, bf16[512,256]{1,0:T(8,128)(2,1)S(1)}, u32[]{:S(2)}, u32[]{:S(2)}) collective-permute-start(bf16[512,256]{1,0:T(8,128)(2,1)S(1)} %get-tuple-element.90), channel_id=1, source_target_pairs={{0,2},{1,3},{2,0},{3,1},{4,6},{5,7},{6,4},{7,5},{8,10},{9,11},{10,... | collective-permute-start | bytes 786440 | tf_op jit(solution)/shard_map/ppermute | solution.py:294
  93.6 11.9 %collective-permute-start.26 = (bf16[512,256]{1,0:T(8,128)(2,1)S(1)}, bf16[512,256]{1,0:T(8,128)(2,1)S(1)}, u32[]{:S(2)}, u32[]{:S(2)}) collective-permute-start(bf16[512,256]{1,0:T(8,128)(2,1)S(1)} %get-tuple-element.103), channel_id=1, source_target_pairs={{0,1},{1,2},{2,3},{3,0},{4,5},{5,6},{6,7},{7,4},{8,9},{9,10},{10,1... | collective-permute-start | bytes 786440 | tf_op jit(solution)/shard_map/ppermute | solution.py:294
  95.3 13.5 %collective-permute-start.27 = (bf16[512,256]{1,0:T(8,128)(2,1)S(1)}, bf16[512,256]{1,0:T(8,128)(2,1)S(1)}, u32[]{:S(2)}, u32[]{:S(2)}) collective-permute-start(bf16[512,256]{1,0:T(8,128)(2,1)S(1)} %get-tuple-element.104), channel_id=1, source_target_pairs={{0,3},{1,0},{2,1},{3,2},{4,7},{5,4},{6,5},{7,6},{8,11},{9,8},{10,9... | collective-permute-start | bytes 786440 | tf_op jit(solution)/shard_map/ppermute | solution.py:294
  95.7 13.1 %collective-permute-start.28 = (bf16[512,256]{1,0:T(8,128)(2,1)S(1)}, bf16[512,256]{1,0:T(8,128)(2,1)S(1)}, u32[]{:S(2)}, u32[]{:S(2)}) collective-permute-start(bf16[512,256]{1,0:T(8,128)(2,1)S(1)} %get-tuple-element.105), channel_id=1, source_target_pairs={{0,2},{1,3},{2,0},{3,1},{4,6},{5,7},{6,4},{7,5},{8,10},{9,11},{10,... | collective-permute-start | bytes 786440 | tf_op jit(solution)/shard_map/ppermute | solution.py:294
